TPU v7x, 32 devices: a whole 2x2x4 slice. The times are simulated.
32 devices in a mesh: blk: 2 (over x), head: 4 (over z), bend: 4 (over y, core).
Axes of the slice: x: 2, y: 2, z: 4, core: 2. Of those that a mesh axis runs over, the one named last changes fastest.
Arguments:
- queries: bfloat16 [8192, 768], P(('bend', 'blk', 'head')), parts along dimension 0, may hold values from -9 to 9
- keys_values: bfloat16 [2, 8192, 768], P(None, ('bend', 'blk', 'head')), parts along dimension 1, may hold values from -6 to 6
- surface: bfloat16 [8192, 768], P(('bend', 'blk', 'head')), parts along dimension 0, may hold values from -6 to 6
- out_weight: bfloat16 [768, 768], P('head'), may hold values from -0.21875 to 0.21875
- up_weight: bfloat16 [768, 3072], P('head'), may hold values from -0.21875 to 0.21875
- down_weight: bfloat16 [3072, 768], P('head'), may hold values from -0.109375 to 0.109375
- norm_gain: float32 [768], replicated, may hold values from 0.25 to 1.75
- block_lists: int32 [32, 4], P(('bend', 'blk', 'head')), parts along dimension 0, may hold values from 0 to 7, as said below
- list_lengths: int32 [32], P(('bend', 'blk', 'head')), parts along dimension 0, may hold values from 1 to 4
Outputs:
- mixed_out: bfloat16 [8192, 768], P(('bend', 'blk', 'head')), parts along dimension 0
There are 4 independent parts, one for each index of `bend`. A program takes and returns all parts, laid end to end along the dimension named above; an argument that names none is the same for every part. Nothing has to cross between parts.
Inputs may be any that keep to these rules, and one draw needn't show every extreme that they name: `block_lists`: the list of query block b holds distinct anchor blocks, all within cycle distance 3 (modulo 8) of anchor block b, and its first entry is that block itself.
All inputs are finite; a program needn't handle non-finite values.
Results may differ from a plain program's by a relative error of at most 0.0065.
Values may be sent and summed in bfloat16 or wider, within the bound.
No kernel may reach another device: no remote copies, remote signals or barrier semaphores. Data moves between devices by JAX's collectives and lax.ppermute only.
A program may use at most 128 MiB of HBM per device.

v0:
```python
import jax
import jax.numpy as jnp
from jax import lax
from jax.sharding import PartitionSpec as P

HEADS = 12
HD = 64
LIST = 4


def passed_along(block, axis, distance):
    devices = range(lax.axis_size(axis))
    route = [((i - distance) % len(devices), i) for i in devices]
    return lax.ppermute(block, axis, route)


def fold_rows(running, left_side, portion):
    return running + jnp.dot(left_side, portion, preferred_element_type=jnp.float32)


def shards(
    queries,
    keys_values,
    surface,
    out_weight,
    up_weight,
    down_weight,
    norm_gain,
    block_lists,
    list_lengths,
):
    row_count, feature_width = queries.shape
    query_blocks = block_lists.shape[0]
    block_rows = row_count // query_blocks
    loop_size = lax.axis_size(("blk", "head"))
    cycle_reach = min(3, (loop_size - 1) // 2)
    own_index = lax.axis_index(("blk", "head"))
    query_heads = queries.reshape(query_blocks, block_rows, HEADS, HD)
    score_scale = 1.0 / HD**0.5
    entry_live = jnp.arange(LIST, dtype=jnp.int32)[None, :] < list_lengths[:, None]
    start_state = (
        jnp.full((query_blocks, HEADS, block_rows), -1e30, jnp.float32),
        jnp.zeros((query_blocks, HEADS, block_rows), jnp.float32),
        jnp.zeros((query_blocks, HEADS, block_rows, HD), jnp.float32),
    )

    def absorb(softmax_state, anchor_pair, source):
        listed = jnp.any((block_lists == source) & entry_live, axis=1)
        running_max, running_sum, running_acc = softmax_state
        block_keys = anchor_pair[0].reshape(block_rows, HEADS, HD)
        block_values = anchor_pair[1].reshape(block_rows, HEADS, HD)
        scores = (
            jnp.einsum(
                "bqhd,khd->bhqk", query_heads, block_keys, preferred_element_type=jnp.float32
            )
            * score_scale
        )
        block_max = jnp.max(scores, axis=3)
        new_max = jnp.where(listed[:, None, None], jnp.maximum(running_max, block_max), running_max)
        ratio = jnp.exp(running_max - new_max)
        weights_exp = jnp.where(
            listed[:, None, None, None], jnp.exp(scores - new_max[..., None]), 0.0
        )
        new_sum = running_sum * ratio + jnp.sum(weights_exp, axis=3)
        probs = weights_exp.astype(jnp.bfloat16)
        new_acc = running_acc * ratio[..., None] + jnp.einsum(
            "bhqk,khd->bhqd", probs, block_values, preferred_element_type=jnp.float32
        )
        return (new_max, new_sum, new_acc)

    moving = passed_along(keys_values, ("blk", "head"), -cycle_reach)
    source = (own_index + cycle_reach) % loop_size
    softmax_state = absorb(start_state, moving, source)
    for cycle_turn in range(2 * cycle_reach):
        moving = passed_along(moving, ("blk", "head"), 1)
        source = (source - 1) % loop_size
        softmax_state = absorb(softmax_state, moving, source)
    final_max, final_sum, final_acc = softmax_state
    context = final_acc / final_sum[..., None]
    context = (
        jnp.transpose(context, (0, 2, 1, 3)).reshape(row_count, feature_width).astype(jnp.bfloat16)
    )
    residual = surface.astype(jnp.float32)
    hidden = fold_rows(residual, context, lax.all_gather(out_weight, "head", axis=0, tiled=True))
    mean_square = jnp.mean(hidden * hidden, axis=1, keepdims=True)
    normed = (hidden * lax.rsqrt(mean_square + 1e-05) * norm_gain[None, :]).astype(jnp.bfloat16)
    up_start = jnp.zeros((row_count, up_weight.shape[1]), jnp.float32)
    pre_gelu = fold_rows(up_start, normed, lax.all_gather(up_weight, "head", axis=0, tiled=True))
    activated = jax.nn.gelu(pre_gelu, approximate=True).astype(jnp.bfloat16)
    mixed_out = fold_rows(
        hidden, activated, lax.all_gather(down_weight, "head", axis=0, tiled=True)
    )
    return mixed_out.astype(jnp.bfloat16)


def solution(mesh):
    return jax.shard_map(
        shards,
        mesh=mesh,
        in_specs=(
            P(("bend", "blk", "head"), None),
            P(None, ("bend", "blk", "head"), None),
            P(("bend", "blk", "head"), None),
            P("head", None),
            P("head", None),
            P("head", None),
            P(),
            P(("bend", "blk", "head"), None),
            P(("bend", "blk", "head")),
        ),
        out_specs=P(("bend", "blk", "head"), None),
        check_vma=False,
    )
```

profile of v0, /device:TPU:0, one launch (start us, length us, event | category | flops | bytes accessed | tf_op | source)
XLA Modules:
  0.0 330.7 jit_solution(3232886668099132254)
XLA Ops:
  8.1 4.0 %collective-permute-start = (bf16[2,256,768]{2,1,0:T(8,128)(2,1)}, bf16[2,256,768]{2,1,0:T(8,128)(2,1)S(1)}, u32[]{:S(2)}, u32[]{:S(2)}) collective-permute-start(bf16[2,256,768]{2,1,0:T(8,128)(2,1)} %param.10), channel_id=1, source_target_pairs={{12,0},{16,4},{20,8},{24,12},{28,16},{0,20},{4,24},{8,28},{13,1},{... | collective-permute-start | bytes 2359304 | tf_op jit(solution)/shard_map/ppermute | solution.py:14
  12.1 27.5 %collective-permute-done = bf16[2,256,768]{2,1,0:T(8,128)(2,1)S(1)} collective-permute-done((bf16[2,256,768]{2,1,0:T(8,128)(2,1)}, bf16[2,256,768]{2,1,0:T(8,128)(2,1)S(1)}, u32[]{:S(2)}, u32[]{:S(2)}) %collective-permute-start) | collective-permute-done | bytes 786464 | tf_op jit(solution)/shard_map/ppermute | solution.py:14
  39.5 9.9 %collective-permute-start.1 = (bf16[2,256,768]{2,1,0:T(8,128)(2,1)S(1)}, bf16[2,256,768]{2,1,0:T(8,128)(2,1)S(1)}, u32[]{:S(2)}, u32[]{:S(2)}) collective-permute-start(bf16[2,256,768]{2,1,0:T(8,128)(2,1)S(1)} %collective-permute-done), channel_id=1, source_target_pairs={{28,0},{0,4},{4,8},{8,12},{12,16},{16,20},{20,24},{24,28},{29,1},{... | collective-permute-start | bytes 2359304 | tf_op jit(solution)/shard_map/ppermute | solution.py:14
  49.4 22.2 %collective-permute-done.1 = bf16[2,256,768]{2,1,0:T(8,128)(2,1)S(1)} collective-permute-done((bf16[2,256,768]{2,1,0:T(8,128)(2,1)S(1)}, bf16[2,256,768]{2,1,0:T(8,128)(2,1)S(1)}, u32[]{:S(2)}, u32[]{:S(2)}) %collective-permute-start.1) | collective-permute-done | bytes 786464 | tf_op jit(solution)/shard_map/ppermute | solution.py:14
  71.6 6.3 %collective-permute-start.2 = (bf16[2,256,768]{2,1,0:T(8,128)(2,1)S(1)}, bf16[2,256,768]{2,1,0:T(8,128)(2,1)S(1)}, u32[]{:S(2)}, u32[]{:S(2)}) collective-permute-start(bf16[2,256,768]{2,1,0:T(8,128)(2,1)S(1)} %collective-permute-done.1), channel_id=1, source_target_pairs={{28,0},{0,4},{4,8},{8,12},{12,16},{16,20},{20,24},{24,28},{29,1},{... | collective-permute-start | bytes 2359304 | tf_op jit(solution)/shard_map/ppermute | solution.py:14
  80.6 31.0 %collective-permute-done.2 = bf16[2,256,768]{2,1,0:T(8,128)(2,1)S(1)} collective-permute-done((bf16[2,256,768]{2,1,0:T(8,128)(2,1)S(1)}, bf16[2,256,768]{2,1,0:T(8,128)(2,1)S(1)}, u32[]{:S(2)}, u32[]{:S(2)}) %collective-permute-start.2) | collective-permute-done | bytes 786464 | tf_op jit(solution)/shard_map/ppermute | solution.py:14
  111.6 19.8 %collective-permute-start.3 = (bf16[2,256,768]{2,1,0:T(8,128)(2,1)S(1)}, bf16[2,256,768]{2,1,0:T(8,128)(2,1)}, u32[]{:S(2)}, u32[]{:S(2)}) collective-permute-start(bf16[2,256,768]{2,1,0:T(8,128)(2,1)S(1)} %collective-permute-done.2), channel_id=1, source_target_pairs={{28,0},{0,4},{4,8},{8,12},{12,16},{16,20},{20,24},{24,28},{29,1},{... | collective-permute-start | bytes 2359304 | tf_op jit(solution)/shard_map/ppermute | solution.py:14
  133.7 2.9 bitcast_reduce_fusion.6
  138.5 26.6 %collective-permute-done.3 = bf16[2,256,768]{2,1,0:T(8,128)(2,1)} collective-permute-done((bf16[2,256,768]{2,1,0:T(8,128)(2,1)S(1)}, bf16[2,256,768]{2,1,0:T(8,128)(2,1)}, u32[]{:S(2)}, u32[]{:S(2)}) %collective-permute-start.3) | collective-permute-done | bytes 786464 | tf_op jit(solution)/shard_map/ppermute | solution.py:14
  165.0 13.2 %collective-permute-start.4 = (bf16[2,256,768]{2,1,0:T(8,128)(2,1)}, bf16[2,256,768]{2,1,0:T(8,128)(2,1)}, u32[]{:S(2)}, u32[]{:S(2)}) collective-permute-start(bf16[2,256,768]{2,1,0:T(8,128)(2,1)} %collective-permute-done.3), channel_id=1, source_target_pairs={{28,0},{0,4},{4,8},{8,12},{12,16},{16,20},{20,24},{24,28},{29,1},{... | collective-permute-start | bytes 2359304 | tf_op jit(solution)/shard_map/ppermute | solution.py:14
  178.3 2.2 bitcast_reduce_fusion.5
  185.3 3.3 bitcast_reduce_fusion.4
  188.6 6.6 %collective-permute-done.4 = bf16[2,256,768]{2,1,0:T(8,128)(2,1)} collective-permute-done((bf16[2,256,768]{2,1,0:T(8,128)(2,1)}, bf16[2,256,768]{2,1,0:T(8,128)(2,1)}, u32[]{:S(2)}, u32[]{:S(2)}) %collective-permute-start.4) | collective-permute-done | bytes 786464 | tf_op jit(solution)/shard_map/ppermute | solution.py:14
  196.1 2.0 fusion.200
  198.2 1.9 copy.48
  202.0 3.9 %bitcast_reduce_fusion.3 = (f32[12,256]{1,0:T(8,128)}, f32[12,256,256]{2,1,0:T(8,128)}) fusion(bf16[256,12,64]{0,2,1:T(8,128)(2,1)} %bitcast.450, bf16[256,12,64]{0,2,1:T(8,128)(2,1)S(1)} %bitcast.436), kind=kOutput, calls=%fused_computation.22 | convolution fusion | flops 102233088 | bytes 3944448 | tf_op jit(solution)/shard_map/bqhd,khd->bhqk/dot_general | solution.py:53
  205.9 2.1 fusion.199
  212.2 2.1 collective-permute-start.6
  214.3 3.9 %bitcast_reduce_fusion.2 = (f32[12,256]{1,0:T(8,128)}, f32[12,256,256]{2,1,0:T(8,128)}) fusion(bf16[256,12,64]{0,2,1:T(8,128)(2,1)} %bitcast.445, bf16[256,12,64]{0,2,1:T(8,128)(2,1)S(1)} %bitcast.437), kind=kOutput, calls=%fused_computation.18 | convolution fusion | flops 102233088 | bytes 3944448 | tf_op jit(solution)/shard_map/bqhd,khd->bhqk/dot_general | solution.py:53
  218.2 2.1 fusion.198
  220.3 2.0 copy.54
  224.2 3.9 %bitcast_reduce_fusion.1 = (f32[12,256]{1,0:T(8,128)}, f32[12,256,256]{2,1,0:T(8,128)}) fusion(bf16[256,12,64]{0,2,1:T(8,128)(2,1)} %bitcast.451, bf16[256,12,64]{0,2,1:T(8,128)(2,1)S(1)} %bitcast.438), kind=kOutput, calls=%fused_computation.14 | convolution fusion | flops 102233088 | bytes 3944448 | tf_op jit(solution)/shard_map/bqhd,khd->bhqk/dot_general | solution.py:53
  228.1 2.0 fusion.197
  230.1 1.9 copy.57
  235.9 4.2 %maximum_select_fusion = (f32[12,256]{1,0:T(8,128)S(1)}, f32[12,256]{1,0:T(8,128)S(1)}, f32[12,256]{1,0:T(8,128)S(1)}, f32[12,256]{1,0:T(8,128)S(1)}, f32[12,256...) fusion(f32[12,256]{1,0:T(8,128)S(1)} %get-tuple-element.42, pred[]{:T(512)} %get-tuple-element.5, ...), kind=kLoop, calls=%fused_computation.128 | loop fusion | flops 43008 | bytes 172039 | tf_op jit(solution)/shard_map/jit(_where)/select_n | solution.py:59
  243.2 3.0 fusion.22
  246.2 3.0 fusion.26
  249.3 2.5 fusion.30
  251.8 2.4 bitcast_add_fusion
  263.7 2.1 multiply_reduce_fusion
  265.8 50.8 %all-gather.8.cloned.1.call-done = bf16[3072,768]{1,0:T(8,128)(2,1)} async-done(((bf16[768,768]{1,0:T(8,128)(2,1)}), bf16[3072,768]{1,0:T(8,128)(2,1)}) %all-gather.8.cloned.1.call-update) | async-done | bytes 4718608 | tf_op jit(solution)/shard_map/all_gather | solution.py:91
  316.7 7.5 %fusion.154 = bf16[256,768]{1,0:T(8,128)(2,1)} fusion(f32[256,768]{1,0:T(8,128)S(1)} %get-tuple-element.57, bf16[3072,768]{1,0:T(8,128)(2,1)} %all-gather.8.cloned.1.call-done, bf16[768,3072]{1,0:T(8,128)(2,1)} %all-gather.6.cloned.1.call-done, f32[768]{0:T(1024)S(1)} %copy-done.22, f32[256]{0:T(256)S(1)} %add_rsqrt_fusion), kind=kOutput, calls=%fused_computation.120 | convolution fusion | flops 2423980032 | bytes 10620928 | tf_op jit(solution)/shard_map/dot_general | solution.py:18
  (85 shorter events, 37.5 us)
Async XLA Ops:
  6.5 73.3 %copy-start.21 = (s32[1,4]{1,0:T(1,128)S(1)}, s32[1,4]{1,0:T(1,128)}, u32[]{:S(2)}) copy-start(s32[1,4]{1,0:T(1,128)} %param.16) | copy-start | bytes 52
  6.5 257.2 %all-gather.4.cloned.1.call-start = ((), (), s32[]{:S(2)}) async-start(), calls=%async_computation | async-start | bytes 1474560 | tf_op jit(solution)/shard_map/all_gather | solution.py:84
  7.3 258.6 %all-gather.6.cloned.1.call-start = ((), (), s32[]{:S(2)}) async-start(), calls=%async_computation.1 | async-start | bytes 5898240 | tf_op jit(solution)/shard_map/all_gather | solution.py:88
  8.0 308.6 %all-gather.8.cloned.1.call-start = ((), (), s32[]{:S(2)}) async-start(), calls=%async_computation.2 | async-start | bytes 5898240 | tf_op jit(solution)/shard_map/all_gather | solution.py:91
  8.1 31.5 %collective-permute-start = (bf16[2,256,768]{2,1,0:T(8,128)(2,1)}, bf16[2,256,768]{2,1,0:T(8,128)(2,1)S(1)}, u32[]{:S(2)}, u32[]{:S(2)}) collective-permute-start(bf16[2,256,768]{2,1,0:T(8,128)(2,1)} %param.10), channel_id=1, source_target_pairs={{12,0},{16,4},{20,8},{24,12},{28,16},{0,20},{4,24},{8,28},{13,1},{... | collective-permute-start | bytes 2359304 | tf_op jit(solution)/shard_map/ppermute | solution.py:14
  39.5 32.1 %copy-start.12 = (bf16[2,256,768]{2,1,0:T(8,128)(2,1)}, bf16[2,256,768]{2,1,0:T(8,128)(2,1)S(1)}, u32[]{:S(2)}) copy-start(bf16[2,256,768]{2,1,0:T(8,128)(2,1)S(1)} %collective-permute-done) | copy-start | bytes 2359300
  39.5 32.1 %collective-permute-start.1 = (bf16[2,256,768]{2,1,0:T(8,128)(2,1)S(1)}, bf16[2,256,768]{2,1,0:T(8,128)(2,1)S(1)}, u32[]{:S(2)}, u32[]{:S(2)}) collective-permute-start(bf16[2,256,768]{2,1,0:T(8,128)(2,1)S(1)} %collective-permute-done), channel_id=1, source_target_pairs={{28,0},{0,4},{4,8},{8,12},{12,16},{16,20},{20,24},{24,28},{29,1},{... | collective-permute-start | bytes 2359304 | tf_op jit(solution)/shard_map/ppermute | solution.py:14
  71.6 40.0 %collective-permute-start.2 = (bf16[2,256,768]{2,1,0:T(8,128)(2,1)S(1)}, bf16[2,256,768]{2,1,0:T(8,128)(2,1)S(1)}, u32[]{:S(2)}, u32[]{:S(2)}) collective-permute-start(bf16[2,256,768]{2,1,0:T(8,128)(2,1)S(1)} %collective-permute-done.1), channel_id=1, source_target_pairs={{28,0},{0,4},{4,8},{8,12},{12,16},{16,20},{20,24},{24,28},{29,1},{... | collective-permute-start | bytes 2359304 | tf_op jit(solution)/shard_map/ppermute | solution.py:14
  111.6 24.9 %copy-start.10 = (bf16[2,256,768]{2,1,0:T(8,128)(2,1)}, bf16[2,256,768]{2,1,0:T(8,128)(2,1)S(1)}, u32[]{:S(2)}) copy-start(bf16[2,256,768]{2,1,0:T(8,128)(2,1)S(1)} %collective-permute-done.2) | copy-start | bytes 2359300
  111.6 53.4 %collective-permute-start.3 = (bf16[2,256,768]{2,1,0:T(8,128)(2,1)S(1)}, bf16[2,256,768]{2,1,0:T(8,128)(2,1)}, u32[]{:S(2)}, u32[]{:S(2)}) collective-permute-start(bf16[2,256,768]{2,1,0:T(8,128)(2,1)S(1)} %collective-permute-done.2), channel_id=1, source_target_pairs={{28,0},{0,4},{4,8},{8,12},{12,16},{16,20},{20,24},{24,28},{29,1},{... | collective-permute-start | bytes 2359304 | tf_op jit(solution)/shard_map/ppermute | solution.py:14
  138.5 42.1 %copy-start.11 = (bf16[2,256,768]{2,1,0:T(8,128)(2,1)S(1)}, bf16[2,256,768]{2,1,0:T(8,128)(2,1)}, u32[]{:S(2)}) copy-start(bf16[2,256,768]{2,1,0:T(8,128)(2,1)} %copy-done.10) | copy-start | bytes 2359300
  165.0 30.2 %collective-permute-start.4 = (bf16[2,256,768]{2,1,0:T(8,128)(2,1)}, bf16[2,256,768]{2,1,0:T(8,128)(2,1)}, u32[]{:S(2)}, u32[]{:S(2)}) collective-permute-start(bf16[2,256,768]{2,1,0:T(8,128)(2,1)} %collective-permute-done.3), channel_id=1, source_target_pairs={{28,0},{0,4},{4,8},{8,12},{12,16},{16,20},{20,24},{24,28},{29,1},{... | collective-permute-start | bytes 2359304 | tf_op jit(solution)/shard_map/ppermute | solution.py:14
  195.2 17.0 %collective-permute-start.5 = (bf16[2,256,768]{2,1,0:T(8,128)(2,1)}, bf16[2,256,768]{2,1,0:T(8,128)(2,1)}, u32[]{:S(2)}, u32[]{:S(2)}) collective-permute-start(bf16[2,256,768]{2,1,0:T(8,128)(2,1)} %collective-permute-done.4), channel_id=1, source_target_pairs={{28,0},{0,4},{4,8},{8,12},{12,16},{16,20},{20,24},{24,28},{29,1},{... | collective-permute-start | bytes 2359304 | tf_op jit(solution)/shard_map/ppermute | solution.py:14
  212.2 15.9 %collective-permute-start.6 = (bf16[2,256,768]{2,1,0:T(8,128)(2,1)}, bf16[2,256,768]{2,1,0:T(8,128)(2,1)}, u32[]{:S(2)}, u32[]{:S(2)}) collective-permute-start(bf16[2,256,768]{2,1,0:T(8,128)(2,1)} %collective-permute-done.5), channel_id=1, source_target_pairs={{28,0},{0,4},{4,8},{8,12},{12,16},{16,20},{20,24},{24,28},{29,1},{... | collective-permute-start | bytes 2359304 | tf_op jit(solution)/shard_map/ppermute | solution.py:14
  234.0 1.9 copy-start.16
  234.0 1.9 copy-start.17
  234.0 1.9 copy-start.18
  234.0 1.9 copy-start.19
  234.0 1.9 copy-start.20
  234.0 9.2 %copy-start.4 = (f32[12,256,256]{2,1,0:T(8,128)S(1)}, f32[12,256,256]{2,1,0:T(8,128)}, u32[]{:S(2)}) copy-start(f32[12,256,256]{2,1,0:T(8,128)} %get-tuple-element.55) | copy-start | bytes 9437188
  243.2 3.0 copy-start
  243.2 3.0 copy-start.1
  246.2 3.0 copy-start.2
  246.2 3.0 copy-start.3
  249.3 5.0 %copy-start.14 = (bf16[1,256,768]{1,2,0:T(8,128)(2,1)S(1)}, bf16[1,256,768]{1,2,0:T(8,128)(2,1)}, u32[]{:S(2)}) copy-start(bf16[1,256,768]{1,2,0:T(8,128)(2,1)} %copy.40) | copy-start | bytes 1179652
  251.8 3.7 %copy-start.5 = (bf16[1,256,768]{1,2,0:T(8,128)(2,1)S(1)}, bf16[1,256,768]{1,2,0:T(8,128)(2,1)}, u32[]{:S(2)}) copy-start(bf16[1,256,768]{1,2,0:T(8,128)(2,1)} %copy.43) | copy-start | bytes 1179652
  255.5 1.4 copy-start.6
  256.9 1.3 copy-start.7
  258.2 1.4 copy-start.8
  259.6 1.4 copy-start.9
  262.3 1.4 copy-start.13
  262.4 54.3 %copy-start.22 = (f32[768]{0:T(1024)S(1)}, f32[768]{0:T(1024)}, u32[]{:S(2)}) copy-start(f32[768]{0:T(1024)} %param.15) | copy-start | bytes 9220
  (1 other events, 1.3 us)
Sparse Core Ops, SparseCore 0:
  8.9 42.3 all-gather.3
  52.8 124.7 all-gather.5
  179.2 137.3 all-gather.7
where the time goes:
time: 332 us; the launch traced here: 331 us
  waiting for transfers between devices  167 us (50%)
  starting transfers between devices  56.2 us (17%)
  matrix products  40.7 us (12%)
  local copies, waits for them, and re-layouts  33.9 us (10%)
  other arithmetic  18.9 us (6%)
  between operations  14.3 us (4%)
    ppermute x7, waiting for transfers between devices, passed_along(): return lax.ppermute(block, axis, route)  114 us
    ppermute x7, starting transfers between devices, passed_along(): return lax.ppermute(block, axis, route)  56.2 us
    all_gather x1, waiting for transfers between devices, shards(): lax.all_gather(down_weight, 'head', axis=0, tiled=True)  50.8 us
    dot_general x7, matrix products, absorb(): jnp.einsum('bqhd,khd->bhqk', query_heads, block_keys, preferred_element_t...  21.9 us
    slice x13, local copies, waits for them, and re-layouts, absorb(): block_values = anchor_pair[1].reshape(block_rows, HEADS, HD)  20.7 us
    slice x8, local copies, waits for them, and re-layouts, absorb(): block_keys = anchor_pair[0].reshape(block_rows, HEADS, HD)  11.9 us
    reduce_sum x4, other arithmetic, absorb(): new_sum = running_sum * ratio + jnp.sum(weights_exp, axis=3)  9.72 us
    dot_general x2, matrix products, fold_rows(): jnp.dot(left_side, portion, preferred_element_type=jnp.float32)  9.6 us
  transfers between devices with their start and end apart: 10, of which 7 were waited for; matrix products, arithmetic and copies ran while one was open for 26% of the time, Pallas kernels for 0%

commit v1 on v0

--- a/solution.py
+++ b/solution.py
@@ -1,11 +1,19 @@
+import functools
+import itertools
+
 import jax
 import jax.numpy as jnp
 from jax import lax
+from jax.experimental import pallas as pl
+from jax.experimental.pallas import tpu as pltpu
+from jax.sharding import Mesh
 from jax.sharding import PartitionSpec as P
 
 HEADS = 12
 HD = 64
 LIST = 4
+MIB = 1024 * 1024
+LOG2E = 1.4426950408889634
 
 
 def passed_along(block, axis, distance):
@@ -18,7 +26,7 @@
     return running + jnp.dot(left_side, portion, preferred_element_type=jnp.float32)
 
 
-def shards(
+def ring_shards(
     queries,
     keys_values,
     surface,
@@ -93,21 +101,381 @@
     return mixed_out.astype(jnp.bfloat16)
 
 
+AXES = ("blk", "head", "side", "core")
+SIZES = (2, 4, 2, 2)
+DEVICES = list(itertools.product(*(range(size) for size in SIZES)))
+ZS = 4
+HZ = HEADS // ZS
+ANY = pl.BlockSpec(memory_space=pl.ANY)
+SMEM = pl.BlockSpec(memory_space=pltpu.SMEM)
+VMEM = pl.BlockSpec(memory_space=pltpu.VMEM)
+
+
+def flat(x, z, y, c):
+    return ((x * SIZES[1] + z) * SIZES[2] + y) * SIZES[3] + c
+
+
+def sent(value, route):
+    return lax.ppermute(value, AXES, [(flat(*d), flat(*route(*d))) for d in DEVICES])
+
+
+def along_head(distance):
+    return lambda x, z, y, c: (x, (z + distance) % ZS, y, c)
+
+
+def over_blk(x, z, y, c):
+    return (1 - x, z, y, c)
+
+
+def plane_first(x, z, y, c):
+    return (1 - x, z, y, c) if c == 0 else (x, z, 1 - y, c)
+
+
+def plane_second(x, z, y, c):
+    return (x, z, 1 - y, c) if c == 0 else (1 - x, z, y, c)
+
+
+def other_core(x, z, y, c):
+    return (x, z, y, 1 - c)
+
+
+def pack_kernel(place, q_ref, kv_ref, out_w, up_w, down_w, *refs):
+    kv_slots, q_slots, piece = refs[:ZS], refs[ZS : 2 * ZS], refs[2 * ZS]
+    kv_all, q_all, sems = refs[2 * ZS + 1 :]
+    x, z, y, c = place[0], place[1], place[2], place[3]
+    p = 2 * x + y
+    m = 2 * p + c
+    ro, cols = out_w.shape[0] // 4, out_w.shape[1] // 2
+    ru, rd = up_w.shape[0], down_w.shape[0] // 8
+    rows = [ro, ro + ru, ro + ru + rd]
+    copies = [
+        pltpu.make_async_copy(
+            out_w.at[pl.ds(pl.multiple_of(p * ro, 16), ro), pl.ds(pl.multiple_of(c * cols, 128), cols)],
+            piece.at[pl.ds(0, ro)],
+            sems.at[0],
+        ),
+        pltpu.make_async_copy(
+            up_w.at[:, pl.ds(pl.multiple_of(m * cols, 128), cols)],
+            piece.at[pl.ds(rows[0], ru)],
+            sems.at[1],
+        ),
+    ]
+    for half in range(2):
+        copies.append(
+            pltpu.make_async_copy(
+                down_w.at[pl.ds(pl.multiple_of(m * rd, 16), rd), pl.ds(half * cols, cols)],
+                piece.at[pl.ds(rows[1 + half], rd)],
+                sems.at[2 + half],
+            )
+        )
+    for copy in copies:
+        copy.start()
+    n = q_ref.shape[0] // 2
+    for head in range(HEADS):
+        lanes = slice(head * HD, (head + 1) * HD)
+        kv_all[head // HZ, head % HZ] = jnp.concatenate(
+            [kv_ref[0, :, lanes], kv_ref[1, :, lanes]], axis=1
+        )
+        q_all[head // HZ, head % HZ] = jnp.concatenate([q_ref[:n, lanes], q_ref[n:, lanes]], axis=1)
+    for s in range(ZS):
+        there = lax.rem(z + s, ZS)
+        kv_slots[s][...] = kv_all[there]
+        q_slots[s][...] = q_all[there]
+    for copy in copies:
+        copy.wait()
+
+
+def packed(place, queries, keys_values, out_weight, up_weight, down_weight):
+    rows, width = queries.shape
+    cols = width // 2
+    piece_rows = out_weight.shape[0] // 4 + up_weight.shape[0] + down_weight.shape[0] // 4
+    kv_shape, q_shape = (HZ, rows, 2 * HD), (HZ, rows // 2, 2 * HD)
+    made = lambda shape: jax.ShapeDtypeStruct(shape, jnp.bfloat16)
+    outs = pl.pallas_call(
+        pack_kernel,
+        out_shape=[made(kv_shape)] * ZS + [made(q_shape)] * ZS + [made((piece_rows, cols))],
+        in_specs=[SMEM, VMEM, VMEM, ANY, ANY, ANY],
+        out_specs=[VMEM] * (2 * ZS) + [ANY],
+        scratch_shapes=[
+            pltpu.VMEM((ZS,) + kv_shape, jnp.bfloat16),
+            pltpu.VMEM((ZS,) + q_shape, jnp.bfloat16),
+            pltpu.SemaphoreType.DMA((4,)),
+        ],
+        compiler_params=pltpu.CompilerParams(vmem_limit_bytes=16 * MIB),
+        cost_estimate=pl.CostEstimate(flops=0, bytes_accessed=4 * MIB, transcendentals=0),
+        name="pack_heads",
+    )(place, queries, keys_values, out_weight, up_weight, down_weight)
+    return outs[:ZS], outs[ZS : 2 * ZS], outs[2 * ZS]
+
+
+def attend_kernel(place, lists, *refs):
+    kv_near, kv_far, q_slots = refs[:ZS], refs[ZS : 2 * ZS], refs[2 * ZS : 3 * ZS]
+    out_slots, (blocks, sems) = refs[3 * ZS : 4 * ZS], refs[4 * ZS :]
+    x, z = place[0], place[1]
+    copies = []
+    for s in range(ZS):
+        source = lax.rem(z - s + ZS, ZS)
+        for side, held in ((x, kv_near[s]), (1 - x, kv_far[s])):
+            copies.append(
+                pltpu.make_async_copy(held, blocks.at[side * ZS + source], sems.at[len(copies)])
+            )
+    for copy in copies:
+        copy.start()
+    for copy in copies:
+        copy.wait()
+    n = q_slots[0].shape[1]
+    low = lax.broadcasted_iota(jnp.int32, (n, 2 * HD), 1) < HD
+    scale = LOG2E / HD**0.5
+    for s in range(ZS):
+
+        @pl.loop(0, HZ)
+        def _(h, s=s):
+            pair = q_slots[s][h]
+            results = []
+            for half in range(2):
+                q = pair if half == 0 else pltpu.roll(pair, HD, 1)
+                q = jnp.where(low, q, jnp.zeros_like(q))
+                scores = []
+                for j in range(LIST):
+                    kv = blocks[lists[s, j], h]
+                    raw = lax.dot_general(
+                        q, kv, (((1,), (1,)), ((), ())), preferred_element_type=jnp.float32
+                    )
+                    if j > 0:
+                        raw = jnp.where(j < lists[s, LIST], raw, -1e30)
+                    scores.append(raw)
+                top = scores[0]
+                for raw in scores[1:]:
+                    top = jnp.maximum(top, raw)
+                top = jnp.max(top, axis=1, keepdims=True)
+                total, acc = None, None
+                for j in range(LIST):
+                    weights = jnp.exp2((scores[j] - top) * scale)
+                    total = weights if j == 0 else total + weights
+                    part = jnp.dot(
+                        weights.astype(jnp.bfloat16),
+                        blocks[lists[s, j], h],
+                        preferred_element_type=jnp.float32,
+                    )
+                    acc = part if j == 0 else acc + part
+                results.append(acc / jnp.sum(total, axis=1, keepdims=True))
+            upper, lower = results
+            both = jnp.where(low, pltpu.roll(upper, HD, 1), lower)
+            out_slots[s][h] = both.astype(jnp.bfloat16)
+
+
+def attended(place, lists, kv_near, kv_far, q_slots):
+    kv_shape, q_shape = kv_near[0].shape, q_slots[0].shape
+    return pl.pallas_call(
+        attend_kernel,
+        out_shape=[jax.ShapeDtypeStruct(q_shape, jnp.bfloat16)] * ZS,
+        in_specs=[SMEM, SMEM] + [ANY] * (2 * ZS) + [VMEM] * ZS,
+        out_specs=[VMEM] * ZS,
+        scratch_shapes=[
+            pltpu.VMEM((2 * ZS,) + kv_shape, jnp.bfloat16),
+            pltpu.SemaphoreType.DMA((2 * ZS,)),
+        ],
+        compiler_params=pltpu.CompilerParams(vmem_limit_bytes=16 * MIB),
+        cost_estimate=pl.CostEstimate(
+            flops=2 * 10**9, bytes_accessed=3 * MIB, transcendentals=3 * 10**6
+        ),
+        name="attend",
+    )(place, lists, *kv_near, *kv_far, *q_slots)
+
+
+def feed_kernel(groups, place, gain, surface, *refs):
+    ctx_slots, (out_w, up_w, down_w) = refs[:ZS], refs[ZS : ZS + 3]
+    refs = refs[ZS + 3 :]
+    count = 2 * 2 * len(groups)
+    held, o_ref = refs[:count], refs[count]
+    out_all, up_all, down_all, sems = refs[count + 1 :]
+    x, z, y, c = place[0], place[1], place[2], place[3]
+    rs, width = out_w.shape
+    cols = width // 2
+    ro, ru, rd = rs // 4, up_w.shape[0], down_w.shape[0] // 8
+    rows = [0, ro, ro + ru, ro + ru + rd]
+    first, second, third = [], [], []
+
+    def copied(into, source, target, sem):
+        into.append(pltpu.make_async_copy(source, target, sems.at[sem]))
+
+    copied(first, out_w, out_all.at[pl.ds(0, rs)], 0)
+    copied(second, up_w, up_all.at[pl.ds(pl.multiple_of(z * ru, 16), ru)], 1)
+    copied(third, down_w, down_all.at[pl.ds(pl.multiple_of(z * 8 * rd, 16), 8 * rd)], 2)
+    at = 0
+    for slots in groups:
+        for swapped in range(2):
+            core = c if swapped == 0 else 1 - c
+            fx, fy = jnp.where(core == 0, 1 - x, x), jnp.where(core == 0, y, 1 - y)
+            for later in range(2):
+                ref = held[at]
+                at += 1
+                for i, k in enumerate(slots):
+                    source = lax.rem(z - k + ZS, ZS)
+                    for e in range(2):
+                        px, py = (x, y) if e == 0 else (fx, fy)
+                        if later:
+                            px = jnp.where(core == 0, px, 1 - px)
+                            py = jnp.where(core == 0, 1 - py, py)
+                        p = 2 * px + py
+                        m = 2 * p + core
+                        piece = ref.at[e, i]
+                        slot_row = ((ZS - k) % ZS) * rs
+                        copied(
+                            first,
+                            piece.at[pl.ds(0, ro)],
+                            out_all.at[
+                                pl.ds(pl.multiple_of(slot_row + p * ro, 16), ro),
+                                pl.ds(pl.multiple_of(core * cols, 128), cols),
+                            ],
+                            0,
+                        )
+                        copied(
+                            second,
+                            piece.at[pl.ds(rows[1], ru)],
+                            up_all.at[
+                                pl.ds(pl.multiple_of(source * ru, 16), ru),
+                                pl.ds(pl.multiple_of(m * cols, 128), cols),
+                            ],
+                            1,
+                        )
+                        for half in range(2):
+                            copied(
+                                third,
+                                piece.at[pl.ds(rows[2 + half], rd)],
+                                down_all.at[
+                                    pl.ds(pl.multiple_of((source * 8 + m) * rd, 16), rd),
+                                    pl.ds(half * cols, cols),
+                                ],
+                                2,
+                            )
+    for copy in first + second + third:
+        copy.start()
+
+    def context_of(half):
+        lanes = slice(half * HD, (half + 1) * HD)
+        return jnp.concatenate(
+            [ctx_slots[s][h, :, lanes] for s in range(ZS) for h in range(HZ)], axis=1
+        )
+
+    context = jnp.concatenate([context_of(0), context_of(1)], axis=0)
+    for copy in first:
+        copy.wait()
+    hidden = surface[...].astype(jnp.float32) + jnp.dot(
+        context, out_all[...], preferred_element_type=jnp.float32
+    )
+    mean_square = jnp.mean(hidden * hidden, axis=1, keepdims=True)
+    normed = (hidden * lax.rsqrt(mean_square + 1e-05) * gain[...]).astype(jnp.bfloat16)
+    for copy in second:
+        copy.wait()
+    total = hidden
+    steps = up_w.shape[1] // width
+    for step in range(steps):
+        pre = jnp.dot(
+            normed, up_all[:, step * width : (step + 1) * width], preferred_element_type=jnp.float32
+        )
+        act = jax.nn.gelu(pre, approximate=True).astype(jnp.bfloat16)
+        if step == 0:
+            for copy in third:
+                copy.wait()
+        total = total + jnp.dot(
+            act, down_all[step * width : (step + 1) * width, :], preferred_element_type=jnp.float32
+        )
+    o_ref[...] = total.astype(jnp.bfloat16)
+
+
+def fed(groups, place, gain, surface, ctx_slots, weights, held):
+    out_weight, up_weight, down_weight = weights
+    width, hidden_units = up_weight.shape[0] * ZS, up_weight.shape[1]
+    return pl.pallas_call(
+        functools.partial(feed_kernel, groups),
+        out_shape=jax.ShapeDtypeStruct(surface.shape, jnp.bfloat16),
+        in_specs=[SMEM, VMEM, VMEM] + [VMEM] * ZS + [ANY] * (3 + len(held)),
+        out_specs=VMEM,
+        scratch_shapes=[
+            pltpu.VMEM((width, width), jnp.bfloat16),
+            pltpu.VMEM((width, hidden_units), jnp.bfloat16),
+            pltpu.VMEM((hidden_units, width), jnp.bfloat16),
+            pltpu.SemaphoreType.DMA((3,)),
+        ],
+        compiler_params=pltpu.CompilerParams(vmem_limit_bytes=40 * MIB),
+        cost_estimate=pl.CostEstimate(
+            flops=3 * 10**9, bytes_accessed=12 * MIB, transcendentals=10**6
+        ),
+        name="feed",
+    )(place, gain, surface, *ctx_slots, out_weight, up_weight, down_weight, *held)
+
+
+def split_shards(
+    queries,
+    keys_values,
+    surface,
+    out_weight,
+    up_weight,
+    down_weight,
+    norm_gain,
+    block_lists,
+    list_lengths,
+):
+    place = jnp.stack([lax.axis_index(axis) for axis in AXES]).astype(jnp.int32)
+    entries = jnp.concatenate([block_lists[0], list_lengths, jnp.zeros(3, jnp.int32)])[None, :]
+    kv_slots, q_slots, piece = packed(
+        place, queries, keys_values, out_weight, up_weight, down_weight
+    )
+    shifts = (1, 3, 2)
+    lists, near, q_got = {0: entries}, {0: kv_slots[0]}, {0: q_slots[0]}
+    far = {0: sent(kv_slots[0], over_blk)}
+    for s in shifts:
+        near[s] = sent(kv_slots[s], along_head(s))
+    for s in shifts:
+        q_got[s] = sent(q_slots[s], along_head(s))
+        lists[s] = sent(entries, along_head(s))
+    for s in shifts:
+        far[s] = sent(near[s], over_blk)
+
+    groups = ((1, 3), (2,))
+    held = []
+    for slots in groups:
+        mine = jnp.stack([sent(piece, along_head(k)) for k in slots])
+        pair = jnp.stack([mine, sent(mine, plane_first)])
+        other = sent(pair, plane_second)
+        held += [pair, other, sent(pair, other_core), sent(other, other_core)]
+
+    order = range(ZS)
+    ctx = attended(
+        place,
+        jnp.concatenate([lists[s] for s in order]),
+        [near[s] for s in order],
+        [far[s] for s in order],
+        [q_got[s] for s in order],
+    )
+    ctx_slots = [ctx[0]] + [sent(ctx[s], along_head(-s)) for s in range(1, ZS)]
+    weights = (out_weight, up_weight, down_weight)
+    return fed(groups, place, norm_gain[None, :], surface, ctx_slots, weights, held)
+
+
 def solution(mesh):
+    sizes = (mesh.shape["blk"], mesh.shape["head"], mesh.shape["bend"])
+    if sizes == (2, 4, 4):
+        mesh = Mesh(mesh.devices.reshape(SIZES), AXES)
+        parts, shards = ("side", "core"), split_shards
+    else:
+        parts, shards = ("bend",), ring_shards
+    rows = parts + ("blk", "head")
     return jax.shard_map(
         shards,
         mesh=mesh,
         in_specs=(
-            P(("bend", "blk", "head"), None),
-            P(None, ("bend", "blk", "head"), None),
-            P(("bend", "blk", "head"), None),
+            P(rows, None),
+            P(None, rows, None),
+            P(rows, None),
             P("head", None),
             P("head", None),
             P("head", None),
             P(),
-            P(("bend", "blk", "head"), None),
-            P(("bend", "blk", "head")),
+            P(rows, None),
+            P(rows),
         ),
-        out_specs=P(("bend", "blk", "head"), None),
+        out_specs=P(rows, None),
         check_vma=False,
     )

time: 332 us -> 151 us (0.45)
  waiting for transfers between devices: 167 us -> 98.3 us
  matrix products: 40.7 us -> 0 us
  starting transfers between devices: 56.2 us -> 23.8 us
  local copies, waits for them, and re-layouts: 33.9 us -> 5.66 us
  Pallas kernels: 0 us -> 21.7 us
  other arithmetic: 18.9 us -> 0.51 us
  between operations: 14.3 us -> 0.8 us
    all_gather x3 -> x0, waiting for transfers between devices: 50.9 us -> none  [the longest x1 50.8 us: shards(): lax.all_gather(down_weight, 'head', axis=0, tiled=True)]
    dot_general x16 -> x0, matrix products: 40.7 us -> none  [the longest x7 21.9 us: absorb(): jnp.einsum('bqhd,khd->bhqk', query_heads, block_keys, preferred_element_t...]
    slice x21 -> x0, local copies, waits for them, and re-layouts: 32.6 us -> none  [the longest x13 20.7 us: absorb(): block_values = anchor_pair[1].reshape(block_rows, HEADS, HD)]
    ppermute x7 -> x27, starting transfers between devices: 56.2 us -> 23.8 us  [sent(): lax.ppermute(value, AXES, [(flat(*d), flat(*route(*d))) for d in DEVICES])]
    pallas_call x0 -> x3, Pallas kernels: none -> 21.7 us  [the longest x1 13 us: attended(): pl.pallas_call(attend_kernel, out_shape=[jax.ShapeDtypeStruct(q_shape, jn...]
    ppermute x7 -> x27, waiting for transfers between devices: 114 us -> 98.3 us  [sent(): lax.ppermute(value, AXES, [(flat(*d), flat(*route(*d))) for d in DEVICES])]
    reduce_sum x4 -> x0, other arithmetic: 9.72 us -> none  [absorb(): new_sum = running_sum * ratio + jnp.sum(weights_exp, axis=3)]
    select_n x2 -> x0, other arithmetic: 6.04 us -> none  [absorb(): jnp.where(listed[:, None, None], jnp.maximum(running_max, block_max), run...]
  transfers between devices with their start and end apart: 10 -> 27, of which waited for: 7 -> 17; matrix products, arithmetic and copies ran while one was open for 26% -> 0% of each run, Pallas kernels for 0% -> 9%
where the time goes in v1:
time: 151 us
  waiting for transfers between devices  98.3 us (65%)
  starting transfers between devices  23.8 us (16%)
  Pallas kernels  21.7 us (14%)
  local copies, waits for them, and re-layouts  5.66 us (4%)
    ppermute x27, waiting for transfers between devices, sent(): lax.ppermute(value, AXES, [(flat(*d), flat(*route(*d))) for d in DEVICES])  98.3 us
    ppermute x27, starting transfers between devices, sent(): lax.ppermute(value, AXES, [(flat(*d), flat(*route(*d))) for d in DEVICES])  23.8 us
    pallas_call x1, Pallas kernels, attended(): pl.pallas_call(attend_kernel, out_shape=[jax.ShapeDtypeStruct(q_shape, jn...  13 us
    pallas_call x1, Pallas kernels, fed(): pl.pallas_call(functools.partial(feed_kernel, groups), out_shape=jax.Shap...  7.57 us
    unnamed x22, local copies, waits for them, and re-layouts  5.66 us
  transfers between devices with their start and end apart: 27, of which 17 were waited for; matrix products, arithmetic and copies ran while one was open for 0% of the time, Pallas kernels for 9%

profile of v1, /device:TPU:0, one launch (start us, length us, event | category | flops | bytes accessed | tf_op | source)
XLA Modules:
  0.0 150.7 jit_solution(8898048856063433708)
XLA Ops:
  0.1 1.3 copy-done
  1.4 1.3 copy-done.2
  2.6 1.0 copy-done.4
  3.6 1.1 copy-done.6
  4.7 1.0 copy-done.7
  5.7 1.1 pack_heads.1
  6.8 5.1 %collective-permute-start.17 = (bf16[432,384]{1,0:T(8,128)(2,1)S(1)}, bf16[432,384]{1,0:T(8,128)(2,1)S(1)}, u32[]{:S(2)}, u32[]{:S(2)}) collective-permute-start(bf16[432,384]{1,0:T(8,128)(2,1)S(1)} %get-tuple-element.30), channel_id=1, source_target_pairs={{0,12},{1,13},{2,14},{3,15},{4,0},{5,1},{6,2},{7,3},{8,4},{9,5},{1... | collective-permute-start | bytes 995336 | tf_op jit(solution)/shard_map/ppermute | solution.py:119
  12.0 8.2 %collective-permute-done.17 = bf16[432,384]{1,0:T(8,128)(2,1)S(1)} collective-permute-done((bf16[432,384]{1,0:T(8,128)(2,1)S(1)}, bf16[432,384]{1,0:T(8,128)(2,1)S(1)}, u32[]{:S(2)}, u32[]{:S(2)}) %collective-permute-start.17) | collective-permute-done | bytes 331808 | tf_op jit(solution)/shard_map/ppermute | solution.py:119
  20.2 6.9 %collective-permute-done.16 = bf16[432,384]{1,0:T(8,128)(2,1)S(1)} collective-permute-done((bf16[432,384]{1,0:T(8,128)(2,1)S(1)}, bf16[432,384]{1,0:T(8,128)(2,1)S(1)}, u32[]{:S(2)}, u32[]{:S(2)}) %collective-permute-start.16) | collective-permute-done | bytes 331808 | tf_op jit(solution)/shard_map/ppermute | solution.py:119
  27.1 1.6 %collective-permute-start.18 = (bf16[2,432,384]{2,1,0:T(8,128)(2,1)S(1)}, bf16[2,432,384]{2,1,0:T(8,128)(2,1)S(1)}, u32[]{:S(2)}, u32[]{:S(2)}) collective-permute-start(bf16[2,432,384]{2,1,0:T(8,128)(2,1)S(1)} %get-tuple-element.32), channel_id=1, source_target_pairs={{0,16},{1,3},{2,18},{3,1},{4,20},{5,7},{6,22},{7,5},{8,24},{9,11},... | collective-permute-start | bytes 1990664 | tf_op jit(solution)/shard_map/ppermute | solution.py:119
  28.7 9.2 %collective-permute-done.18 = bf16[2,432,384]{2,1,0:T(8,128)(2,1)S(1)} collective-permute-done((bf16[2,432,384]{2,1,0:T(8,128)(2,1)S(1)}, bf16[2,432,384]{2,1,0:T(8,128)(2,1)S(1)}, u32[]{:S(2)}, u32[]{:S(2)}) %collective-permute-start.18) | collective-permute-done | bytes 663584 | tf_op jit(solution)/shard_map/ppermute | solution.py:119
  38.0 1.6 %collective-permute-start.19 = (bf16[2,2,432,384]{3,2,1,0:T(8,128)(2,1)S(1)}, bf16[2,2,432,384]{3,2,1,0:T(8,128)(2,1)S(1)}, u32[]{:S(2)}, u32[]{:S(2)}) collective-permute-start(bf16[2,2,432,384]{3,2,1,0:T(8,128)(2,1)S(1)} %pad_maximum_fusion.refs_7_), channel_id=1, source_target_pairs={{0,2},{1,17},{2,0},{3,19},{4,6},{5,21},{6,4},{7,23},{8,10},{9,25},... | collective-permute-start | bytes 3981320 | tf_op jit(solution)/shard_map/ppermute | solution.py:119
  40.4 14.8 %collective-permute-done.22 = bf16[432,384]{1,0:T(8,128)(2,1)S(1)} collective-permute-done((bf16[432,384]{1,0:T(8,128)(2,1)S(1)}, bf16[432,384]{1,0:T(8,128)(2,1)S(1)}, u32[]{:S(2)}, u32[]{:S(2)}) %collective-permute-start.22) | collective-permute-done | bytes 331808 | tf_op jit(solution)/shard_map/ppermute | solution.py:119
  56.4 1.3 collective-permute-start.2
  58.5 3.8 %collective-permute-done.23 = bf16[1,432,384]{2,1,0:T(8,128)(2,1)S(1)} collective-permute-done((bf16[1,432,384]{2,1,0:T(8,128)(2,1)S(1)}, bf16[1,432,384]{2,1,0:T(8,128)(2,1)S(1)}, u32[]{:S(2)}, u32[]{:S(2)}) %collective-permute-start.23) | collective-permute-done | bytes 331808 | tf_op jit(solution)/shard_map/ppermute | solution.py:119
  62.3 1.3 collective-permute-start.12
  63.7 6.3 %collective-permute-done.1 = s32[1,8]{1,0:T(1,128)S(1)} collective-permute-done((s32[1,8]{1,0:T(1,128)S(1)}, s32[1,8]{1,0:T(1,128)S(1)}, u32[]{:S(2)}, u32[]{:S(2)}) %collective-permute-start.1) | collective-permute-done | bytes 64 | tf_op jit(solution)/shard_map/ppermute | solution.py:119
  70.1 5.3 %collective-permute-done = s32[1,8]{1,0:T(1,128)S(1)} collective-permute-done((s32[1,8]{1,0:T(1,128)S(1)}, s32[1,8]{1,0:T(1,128)S(1)}, u32[]{:S(2)}, u32[]{:S(2)}) %collective-permute-start) | collective-permute-done | bytes 64 | tf_op jit(solution)/shard_map/ppermute | solution.py:119
  76.8 9.3 %collective-permute-done.3.refs_1_ = bf16[3,256,128]{2,1,0:T(8,128)(2,1)S(1)} collective-permute-done((bf16[3,256,128]{2,1,0:T(8,128)(2,1)S(1)}, bf16[3,256,128]{2,1,0:T(8,128)(2,1)S(1)}, u32[]{:S(2)}, u32[]{:S(2)}) %collective-permute-start.3) | collective-permute-done | bytes 196640 | tf_op jit(solution)/shard_map/ppermute | solution.py:119
  86.1 7.5 %collective-permute-done.4.refs_2_ = bf16[3,256,128]{2,1,0:T(8,128)(2,1)S(1)} collective-permute-done((bf16[3,256,128]{2,1,0:T(8,128)(2,1)S(1)}, bf16[3,256,128]{2,1,0:T(8,128)(2,1)S(1)}, u32[]{:S(2)}, u32[]{:S(2)}) %collective-permute-start.4) | collective-permute-done | bytes 196640 | tf_op jit(solution)/shard_map/ppermute | solution.py:119
  94.5 1.1 collective-permute-start.7
  95.7 5.8 %collective-permute-done.6.refs_4_ = bf16[3,256,128]{2,1,0:T(8,128)(2,1)S(1)} collective-permute-done((bf16[3,256,128]{2,1,0:T(8,128)(2,1)S(1)}, bf16[3,256,128]{2,1,0:T(8,128)(2,1)S(1)}, u32[]{:S(2)}, u32[]{:S(2)}) %collective-permute-start.6) | collective-permute-done | bytes 196640 | tf_op jit(solution)/shard_map/ppermute | solution.py:119
  102.1 3.6 %collective-permute-done.7.refs_5_ = bf16[3,256,128]{2,1,0:T(8,128)(2,1)S(1)} collective-permute-done((bf16[3,256,128]{2,1,0:T(8,128)(2,1)S(1)}, bf16[3,256,128]{2,1,0:T(8,128)(2,1)S(1)}, u32[]{:S(2)}, u32[]{:S(2)}) %collective-permute-start.7) | collective-permute-done | bytes 196640 | tf_op jit(solution)/shard_map/ppermute | solution.py:119
  106.3 3.1 %collective-permute-done.8.refs_6_ = bf16[3,256,128]{2,1,0:T(8,128)(2,1)S(1)} collective-permute-done((bf16[3,256,128]{2,1,0:T(8,128)(2,1)S(1)}, bf16[3,256,128]{2,1,0:T(8,128)(2,1)S(1)}, u32[]{:S(2)}, u32[]{:S(2)}) %collective-permute-start.8) | collective-permute-done | bytes 196640 | tf_op jit(solution)/shard_map/ppermute | solution.py:119
  109.9 1.6 %collective-permute-done.9.refs_7_ = bf16[3,256,128]{2,1,0:T(8,128)(2,1)S(1)} collective-permute-done((bf16[3,256,128]{2,1,0:T(8,128)(2,1)S(1)}, bf16[3,256,128]{2,1,0:T(8,128)(2,1)S(1)}, u32[]{:S(2)}, u32[]{:S(2)}) %collective-permute-start.9) | collective-permute-done | bytes 196640 | tf_op jit(solution)/shard_map/ppermute | solution.py:119
  111.5 13.0 %attend.1 = (bf16[3,128,128]{2,1,0:T(8,128)(2,1)S(1)}, bf16[3,128,128]{2,1,0:T(8,128)(2,1)S(1)}, bf16[3,128,128]{2,1,0:T(8,128)(2,1)S(1)}, bf16[3,128,128]{2,1,0:T(8,128)(2,1)S(1)}) custom-call(s32[4]{0:T(128)S(1)} %pad_add_fusion.1.place, s32[4,8]{1,0:T(4,128)S(1)} %pad_add_fusion.lists, bf16[3,256,128]{2,1,0:T(8,128)(2,1)S(1)} %get-tuple-element.18.refs_0_, ...), custom_call_target="tpu_custom_call" | custom-call | flops 2000000000 | bytes 3145728 | tf_op jit(solution)/shard_map/attend/pallas_call | solution.py:269
  124.5 3.1 %collective-permute-start.13 = (bf16[3,128,128]{2,1,0:T(8,128)(2,1)S(1)}, bf16[3,128,128]{2,1,0:T(8,128)(2,1)S(1)}, u32[]{:S(2)}, u32[]{:S(2)}) collective-permute-start(bf16[3,128,128]{2,1,0:T(8,128)(2,1)S(1)} %get-tuple-element.27), channel_id=1, source_target_pairs={{0,12},{1,13},{2,14},{3,15},{4,0},{5,1},{6,2},{7,3},{8,4},{9,5},{1... | collective-permute-start | bytes 294920 | tf_op jit(solution)/shard_map/ppermute | solution.py:119
  127.6 3.0 %collective-permute-done.13.refs_1_ = bf16[3,128,128]{2,1,0:T(8,128)(2,1)S(1)} collective-permute-done((bf16[3,128,128]{2,1,0:T(8,128)(2,1)S(1)}, bf16[3,128,128]{2,1,0:T(8,128)(2,1)S(1)}, u32[]{:S(2)}, u32[]{:S(2)}) %collective-permute-start.13) | collective-permute-done | bytes 98336 | tf_op jit(solution)/shard_map/ppermute | solution.py:119
  130.8 5.3 %collective-permute-done.14.refs_2_ = bf16[3,128,128]{2,1,0:T(8,128)(2,1)S(1)} collective-permute-done((bf16[3,128,128]{2,1,0:T(8,128)(2,1)S(1)}, bf16[3,128,128]{2,1,0:T(8,128)(2,1)S(1)}, u32[]{:S(2)}, u32[]{:S(2)}) %collective-permute-start.14) | collective-permute-done | bytes 98336 | tf_op jit(solution)/shard_map/ppermute | solution.py:119
  136.1 2.8 %collective-permute-start.15 = (bf16[3,128,128]{2,1,0:T(8,128)(2,1)S(1)}, bf16[3,128,128]{2,1,0:T(8,128)(2,1)S(1)}, u32[]{:S(2)}, u32[]{:S(2)}) collective-permute-start(bf16[3,128,128]{2,1,0:T(8,128)(2,1)S(1)} %get-tuple-element.29), channel_id=1, source_target_pairs={{0,4},{1,5},{2,6},{3,7},{4,8},{5,9},{6,10},{7,11},{8,12},{9,13},{1... | collective-permute-start | bytes 294920 | tf_op jit(solution)/shard_map/ppermute | solution.py:119
  138.9 4.1 %collective-permute-done.15.refs_3_ = bf16[3,128,128]{2,1,0:T(8,128)(2,1)S(1)} collective-permute-done((bf16[3,128,128]{2,1,0:T(8,128)(2,1)S(1)}, bf16[3,128,128]{2,1,0:T(8,128)(2,1)S(1)}, u32[]{:S(2)}, u32[]{:S(2)}) %collective-permute-start.15) | collective-permute-done | bytes 98336 | tf_op jit(solution)/shard_map/ppermute | solution.py:119
  143.1 7.6 %feed.1 = bf16[256,768]{1,0:T(8,128)(2,1)} custom-call(s32[4]{0:T(128)S(1)} %pad_add_fusion.1.place, f32[1,768]{1,0:T(1,128)S(1)} %broadcast_in_dim.6.gain, bf16[256,768]{1,0:T(8,128)(2,1)S(1)} %copy-done.8, bf16[3,128,128]{2,1,0:T(8,128)(2,1)S(1)} %get-tuple-element.26.refs_0_, bf16[3,128,128]{2,1,0:T(8,128)(2,1)S(1)} %collective-permute-done.13.refs_1_, ...), custom_call_target="tpu_custom_call" | custom-call | flops 3000000000 | bytes 12582912 | tf_op jit(solution)/shard_map/feed/pallas_call | solution.py:390
  (55 shorter events, 6.7 us)
Async XLA Ops:
  6.8 13.3 %collective-permute-start.17 = (bf16[432,384]{1,0:T(8,128)(2,1)S(1)}, bf16[432,384]{1,0:T(8,128)(2,1)S(1)}, u32[]{:S(2)}, u32[]{:S(2)}) collective-permute-start(bf16[432,384]{1,0:T(8,128)(2,1)S(1)} %get-tuple-element.30), channel_id=1, source_target_pairs={{0,12},{1,13},{2,14},{3,15},{4,0},{5,1},{6,2},{7,3},{8,4},{9,5},{1... | collective-permute-start | bytes 995336 | tf_op jit(solution)/shard_map/ppermute | solution.py:119
  12.0 15.1 %collective-permute-start.16 = (bf16[432,384]{1,0:T(8,128)(2,1)S(1)}, bf16[432,384]{1,0:T(8,128)(2,1)S(1)}, u32[]{:S(2)}, u32[]{:S(2)}) collective-permute-start(bf16[432,384]{1,0:T(8,128)(2,1)S(1)} %get-tuple-element.30), channel_id=1, source_target_pairs={{0,4},{1,5},{2,6},{3,7},{4,8},{5,9},{6,10},{7,11},{8,12},{9,13},{1... | collective-permute-start | bytes 995336 | tf_op jit(solution)/shard_map/ppermute | solution.py:119
  27.1 10.7 %collective-permute-start.18 = (bf16[2,432,384]{2,1,0:T(8,128)(2,1)S(1)}, bf16[2,432,384]{2,1,0:T(8,128)(2,1)S(1)}, u32[]{:S(2)}, u32[]{:S(2)}) collective-permute-start(bf16[2,432,384]{2,1,0:T(8,128)(2,1)S(1)} %get-tuple-element.32), channel_id=1, source_target_pairs={{0,16},{1,3},{2,18},{3,1},{4,20},{5,7},{6,22},{7,5},{8,24},{9,11},... | collective-permute-start | bytes 1990664 | tf_op jit(solution)/shard_map/ppermute | solution.py:119
  38.0 37.9 %collective-permute-start.19 = (bf16[2,2,432,384]{3,2,1,0:T(8,128)(2,1)S(1)}, bf16[2,2,432,384]{3,2,1,0:T(8,128)(2,1)S(1)}, u32[]{:S(2)}, u32[]{:S(2)}) collective-permute-start(bf16[2,2,432,384]{3,2,1,0:T(8,128)(2,1)S(1)} %pad_maximum_fusion.refs_7_), channel_id=1, source_target_pairs={{0,2},{1,17},{2,0},{3,19},{4,6},{5,21},{6,4},{7,23},{8,10},{9,25},... | collective-permute-start | bytes 3981320 | tf_op jit(solution)/shard_map/ppermute | solution.py:119
  39.6 15.5 %collective-permute-start.22 = (bf16[432,384]{1,0:T(8,128)(2,1)S(1)}, bf16[432,384]{1,0:T(8,128)(2,1)S(1)}, u32[]{:S(2)}, u32[]{:S(2)}) collective-permute-start(bf16[432,384]{1,0:T(8,128)(2,1)S(1)} %get-tuple-element.30), channel_id=1, source_target_pairs={{0,8},{1,9},{2,10},{3,11},{4,12},{5,13},{6,14},{7,15},{8,0},{9,1},... | collective-permute-start | bytes 995336 | tf_op jit(solution)/shard_map/ppermute | solution.py:119
  55.1 7.1 %collective-permute-start.23 = (bf16[1,432,384]{2,1,0:T(8,128)(2,1)S(1)}, bf16[1,432,384]{2,1,0:T(8,128)(2,1)S(1)}, u32[]{:S(2)}, u32[]{:S(2)}) collective-permute-start(bf16[1,432,384]{2,1,0:T(8,128)(2,1)S(1)} %bitcast.16), channel_id=1, source_target_pairs={{0,16},{1,3},{2,18},{3,1},{4,20},{5,7},{6,22},{7,5},{8,24},{9,11},... | collective-permute-start | bytes 995336 | tf_op jit(solution)/shard_map/ppermute | solution.py:119
  56.4 7.2 %collective-permute-start.2 = (s32[1,8]{1,0:T(1,128)S(1)}, s32[1,8]{1,0:T(1,128)S(1)}, u32[]{:S(2)}, u32[]{:S(2)}) collective-permute-start(s32[1,8]{1,0:T(1,128)S(1)} %add_bitcast_fusion), channel_id=1, source_target_pairs={{0,12},{1,13},{2,14},{3,15},{4,0},{5,1},{6,2},{7,3},{8,4},{9,5},{1... | collective-permute-start | bytes 104 | tf_op jit(solution)/shard_map/ppermute | solution.py:119
  57.7 18.2 %collective-permute-start.10 = (bf16[3,128,128]{2,1,0:T(8,128)(2,1)S(1)}, bf16[3,128,128]{2,1,0:T(8,128)(2,1)S(1)}, u32[]{:S(2)}, u32[]{:S(2)}) collective-permute-start(bf16[3,128,128]{2,1,0:T(8,128)(2,1)S(1)} %get-tuple-element.23), channel_id=1, source_target_pairs={{0,4},{1,5},{2,6},{3,7},{4,8},{5,9},{6,10},{7,11},{8,12},{9,13},{1... | collective-permute-start | bytes 294920 | tf_op jit(solution)/shard_map/ppermute | solution.py:119
  58.4 18.0 %collective-permute-start.11 = (bf16[3,128,128]{2,1,0:T(8,128)(2,1)S(1)}, bf16[3,128,128]{2,1,0:T(8,128)(2,1)S(1)}, u32[]{:S(2)}, u32[]{:S(2)}) collective-permute-start(bf16[3,128,128]{2,1,0:T(8,128)(2,1)S(1)} %get-tuple-element.24), channel_id=1, source_target_pairs={{0,8},{1,9},{2,10},{3,11},{4,12},{5,13},{6,14},{7,15},{8,0},{9,1},... | collective-permute-start | bytes 294920 | tf_op jit(solution)/shard_map/ppermute | solution.py:119
  62.3 14.2 %collective-permute-start.12 = (bf16[3,128,128]{2,1,0:T(8,128)(2,1)S(1)}, bf16[3,128,128]{2,1,0:T(8,128)(2,1)S(1)}, u32[]{:S(2)}, u32[]{:S(2)}) collective-permute-start(bf16[3,128,128]{2,1,0:T(8,128)(2,1)S(1)} %get-tuple-element.25), channel_id=1, source_target_pairs={{0,12},{1,13},{2,14},{3,15},{4,0},{5,1},{6,2},{7,3},{8,4},{9,5},{1... | collective-permute-start | bytes 294920 | tf_op jit(solution)/shard_map/ppermute | solution.py:119
  63.7 6.4 %collective-permute-start.1 = (s32[1,8]{1,0:T(1,128)S(1)}, s32[1,8]{1,0:T(1,128)S(1)}, u32[]{:S(2)}, u32[]{:S(2)}) collective-permute-start(s32[1,8]{1,0:T(1,128)S(1)} %add_bitcast_fusion), channel_id=1, source_target_pairs={{0,8},{1,9},{2,10},{3,11},{4,12},{5,13},{6,14},{7,15},{8,0},{9,1},... | collective-permute-start | bytes 104 | tf_op jit(solution)/shard_map/ppermute | solution.py:119
  70.1 5.3 %collective-permute-start = (s32[1,8]{1,0:T(1,128)S(1)}, s32[1,8]{1,0:T(1,128)S(1)}, u32[]{:S(2)}, u32[]{:S(2)}) collective-permute-start(s32[1,8]{1,0:T(1,128)S(1)} %add_bitcast_fusion), channel_id=1, source_target_pairs={{0,4},{1,5},{2,6},{3,7},{4,8},{5,9},{6,10},{7,11},{8,12},{9,13},{1... | collective-permute-start | bytes 104 | tf_op jit(solution)/shard_map/ppermute | solution.py:119
  75.4 33.9 %collective-permute-start.24 = (bf16[2,1,432,384]{3,2,1,0:T(8,128)(2,1)S(1)}, bf16[2,1,432,384]{3,2,1,0:T(8,128)(2,1)S(1)}, u32[]{:S(2)}, u32[]{:S(2)}) collective-permute-start(bf16[2,1,432,384]{3,2,1,0:T(8,128)(2,1)S(1)} %pad_maximum_fusion.2.refs_11_), channel_id=1, source_target_pairs={{0,2},{1,17},{2,0},{3,19},{4,6},{5,21},{6,4},{7,23},{8,10},{9,25},... | collective-permute-start | bytes 1990664 | tf_op jit(solution)/shard_map/ppermute | solution.py:119
  75.9 67.1 %collective-permute-start.20 = (bf16[2,2,432,384]{3,2,1,0:T(8,128)(2,1)S(1)}, bf16[2,2,432,384]{3,2,1,0:T(8,128)(2,1)S(1)}, u32[]{:S(2)}, u32[]{:S(2)}) collective-permute-start(bf16[2,2,432,384]{3,2,1,0:T(8,128)(2,1)S(1)} %pad_maximum_fusion.refs_7_), channel_id=1, source_target_pairs={{0,1},{1,0},{2,3},{3,2},{4,5},{5,4},{6,7},{7,6},{8,9},{9,8},{10,11... | collective-permute-start | bytes 3981320 | tf_op jit(solution)/shard_map/ppermute | solution.py:119
  75.9 67.1 %collective-permute-start.21 = (bf16[2,2,432,384]{3,2,1,0:T(8,128)(2,1)S(1)}, bf16[2,2,432,384]{3,2,1,0:T(8,128)(2,1)S(1)}, u32[]{:S(2)}, u32[]{:S(2)}) collective-permute-start(bf16[2,2,432,384]{3,2,1,0:T(8,128)(2,1)S(1)} %collective-permute-done.19.refs_8_), channel_id=1, source_target_pairs={{0,1},{1,0},{2,3},{3,2},{4,5},{5,4},{6,7},{7,6},{8,9},{9,8},{10,11... | collective-permute-start | bytes 3981320 | tf_op jit(solution)/shard_map/ppermute | solution.py:119
  76.5 9.7 %collective-permute-start.3 = (bf16[3,256,128]{2,1,0:T(8,128)(2,1)S(1)}, bf16[3,256,128]{2,1,0:T(8,128)(2,1)S(1)}, u32[]{:S(2)}, u32[]{:S(2)}) collective-permute-start(bf16[3,256,128]{2,1,0:T(8,128)(2,1)S(1)} %get-tuple-element.19), channel_id=1, source_target_pairs={{0,4},{1,5},{2,6},{3,7},{4,8},{5,9},{6,10},{7,11},{8,12},{9,13},{1... | collective-permute-start | bytes 589832 | tf_op jit(solution)/shard_map/ppermute | solution.py:119
  76.5 17.2 %collective-permute-start.4 = (bf16[3,256,128]{2,1,0:T(8,128)(2,1)S(1)}, bf16[3,256,128]{2,1,0:T(8,128)(2,1)S(1)}, u32[]{:S(2)}, u32[]{:S(2)}) collective-permute-start(bf16[3,256,128]{2,1,0:T(8,128)(2,1)S(1)} %get-tuple-element.20), channel_id=1, source_target_pairs={{0,8},{1,9},{2,10},{3,11},{4,12},{5,13},{6,14},{7,15},{8,0},{9,1},... | collective-permute-start | bytes 589832 | tf_op jit(solution)/shard_map/ppermute | solution.py:119
  86.1 8.4 %collective-permute-start.5 = (bf16[3,256,128]{2,1,0:T(8,128)(2,1)S(1)}, bf16[3,256,128]{2,1,0:T(8,128)(2,1)S(1)}, u32[]{:S(2)}, u32[]{:S(2)}) collective-permute-start(bf16[3,256,128]{2,1,0:T(8,128)(2,1)S(1)} %get-tuple-element.21), channel_id=1, source_target_pairs={{0,12},{1,13},{2,14},{3,15},{4,0},{5,1},{6,2},{7,3},{8,4},{9,5},{1... | collective-permute-start | bytes 589832 | tf_op jit(solution)/shard_map/ppermute | solution.py:119
  93.7 7.8 %collective-permute-start.6 = (bf16[3,256,128]{2,1,0:T(8,128)(2,1)S(1)}, bf16[3,256,128]{2,1,0:T(8,128)(2,1)S(1)}, u32[]{:S(2)}, u32[]{:S(2)}) collective-permute-start(bf16[3,256,128]{2,1,0:T(8,128)(2,1)S(1)} %get-tuple-element.18.refs_0_), channel_id=1, source_target_pairs={{0,16},{1,17},{2,18},{3,19},{4,20},{5,21},{6,22},{7,23},{8,24},{9,... | collective-permute-start | bytes 589832 | tf_op jit(solution)/shard_map/ppermute | solution.py:119
  94.5 11.2 %collective-permute-start.7 = (bf16[3,256,128]{2,1,0:T(8,128)(2,1)S(1)}, bf16[3,256,128]{2,1,0:T(8,128)(2,1)S(1)}, u32[]{:S(2)}, u32[]{:S(2)}) collective-permute-start(bf16[3,256,128]{2,1,0:T(8,128)(2,1)S(1)} %collective-permute-done.3.refs_1_), channel_id=1, source_target_pairs={{0,16},{1,17},{2,18},{3,19},{4,20},{5,21},{6,22},{7,23},{8,24},{9,... | collective-permute-start | bytes 589832 | tf_op jit(solution)/shard_map/ppermute | solution.py:119
  101.5 7.9 %collective-permute-start.8 = (bf16[3,256,128]{2,1,0:T(8,128)(2,1)S(1)}, bf16[3,256,128]{2,1,0:T(8,128)(2,1)S(1)}, u32[]{:S(2)}, u32[]{:S(2)}) collective-permute-start(bf16[3,256,128]{2,1,0:T(8,128)(2,1)S(1)} %collective-permute-done.4.refs_2_), channel_id=1, source_target_pairs={{0,16},{1,17},{2,18},{3,19},{4,20},{5,21},{6,22},{7,23},{8,24},{9,... | collective-permute-start | bytes 589832 | tf_op jit(solution)/shard_map/ppermute | solution.py:119
  105.7 5.8 %collective-permute-start.9 = (bf16[3,256,128]{2,1,0:T(8,128)(2,1)S(1)}, bf16[3,256,128]{2,1,0:T(8,128)(2,1)S(1)}, u32[]{:S(2)}, u32[]{:S(2)}) collective-permute-start(bf16[3,256,128]{2,1,0:T(8,128)(2,1)S(1)} %collective-permute-done.5.refs_3_), channel_id=1, source_target_pairs={{0,16},{1,17},{2,18},{3,19},{4,20},{5,21},{6,22},{7,23},{8,24},{9,... | collective-permute-start | bytes 589832 | tf_op jit(solution)/shard_map/ppermute | solution.py:119
  109.4 33.7 %collective-permute-start.25 = (bf16[2,1,432,384]{3,2,1,0:T(8,128)(2,1)S(1)}, bf16[2,1,432,384]{3,2,1,0:T(8,128)(2,1)S(1)}, u32[]{:S(2)}, u32[]{:S(2)}) collective-permute-start(bf16[2,1,432,384]{3,2,1,0:T(8,128)(2,1)S(1)} %pad_maximum_fusion.2.refs_11_), channel_id=1, source_target_pairs={{0,1},{1,0},{2,3},{3,2},{4,5},{5,4},{6,7},{7,6},{8,9},{9,8},{10,11... | collective-permute-start | bytes 1990664 | tf_op jit(solution)/shard_map/ppermute | solution.py:119
  109.4 33.7 %collective-permute-start.26 = (bf16[2,1,432,384]{3,2,1,0:T(8,128)(2,1)S(1)}, bf16[2,1,432,384]{3,2,1,0:T(8,128)(2,1)S(1)}, u32[]{:S(2)}, u32[]{:S(2)}) collective-permute-start(bf16[2,1,432,384]{3,2,1,0:T(8,128)(2,1)S(1)} %collective-permute-done.24.refs_12_), channel_id=1, source_target_pairs={{0,1},{1,0},{2,3},{3,2},{4,5},{5,4},{6,7},{7,6},{8,9},{9,8},{10,11... | collective-permute-start | bytes 1990664 | tf_op jit(solution)/shard_map/ppermute | solution.py:119
  111.5 27.4 %copy-start.9 = (f32[768]{0:T(1024)S(1)}, f32[768]{0:T(1024)}, u32[]{:S(2)}) copy-start(f32[768]{0:T(1024)} %param.15) | copy-start | bytes 9220
  111.5 31.6 %copy-start.1 = (bf16[192,3072]{1,0:T(8,128)(2,1)S(1)}, bf16[192,3072]{1,0:T(8,128)(2,1)}, u32[]{:S(2)}) copy-start(bf16[192,3072]{1,0:T(8,128)(2,1)} %refs_5_.1) | copy-start | bytes 3538948
  111.5 31.6 %copy-start.3 = (bf16[768,768]{1,0:T(8,128)(2,1)S(1)}, bf16[768,768]{1,0:T(8,128)(2,1)}, u32[]{:S(2)}) copy-start(bf16[768,768]{1,0:T(8,128)(2,1)} %refs_6_.1) | copy-start | bytes 3538948
  111.5 31.6 %copy-start.5 = (bf16[192,768]{1,0:T(8,128)(2,1)S(1)}, bf16[192,768]{1,0:T(8,128)(2,1)}, u32[]{:S(2)}) copy-start(bf16[192,768]{1,0:T(8,128)(2,1)} %refs_4_.1) | copy-start | bytes 884740
  111.5 31.6 %copy-start.8 = (bf16[256,768]{1,0:T(8,128)(2,1)S(1)}, bf16[256,768]{1,0:T(8,128)(2,1)}, u32[]{:S(2)}) copy-start(bf16[256,768]{1,0:T(8,128)(2,1)} %surface.1) | copy-start | bytes 1179652
  124.5 6.1 %collective-permute-start.13 = (bf16[3,128,128]{2,1,0:T(8,128)(2,1)S(1)}, bf16[3,128,128]{2,1,0:T(8,128)(2,1)S(1)}, u32[]{:S(2)}, u32[]{:S(2)}) collective-permute-start(bf16[3,128,128]{2,1,0:T(8,128)(2,1)S(1)} %get-tuple-element.27), channel_id=1, source_target_pairs={{0,12},{1,13},{2,14},{3,15},{4,0},{5,1},{6,2},{7,3},{8,4},{9,5},{1... | collective-permute-start | bytes 294920 | tf_op jit(solution)/shard_map/ppermute | solution.py:119
  130.6 5.5 %collective-permute-start.14 = (bf16[3,128,128]{2,1,0:T(8,128)(2,1)S(1)}, bf16[3,128,128]{2,1,0:T(8,128)(2,1)S(1)}, u32[]{:S(2)}, u32[]{:S(2)}) collective-permute-start(bf16[3,128,128]{2,1,0:T(8,128)(2,1)S(1)} %get-tuple-element.28), channel_id=1, source_target_pairs={{0,8},{1,9},{2,10},{3,11},{4,12},{5,13},{6,14},{7,15},{8,0},{9,1},... | collective-permute-start | bytes 294920 | tf_op jit(solution)/shard_map/ppermute | solution.py:119
  136.1 6.9 %collective-permute-start.15 = (bf16[3,128,128]{2,1,0:T(8,128)(2,1)S(1)}, bf16[3,128,128]{2,1,0:T(8,128)(2,1)S(1)}, u32[]{:S(2)}, u32[]{:S(2)}) collective-permute-start(bf16[3,128,128]{2,1,0:T(8,128)(2,1)S(1)} %get-tuple-element.29), channel_id=1, source_target_pairs={{0,4},{1,5},{2,6},{3,7},{4,8},{5,9},{6,10},{7,11},{8,12},{9,13},{1... | collective-permute-start | bytes 294920 | tf_op jit(solution)/shard_map/ppermute | solution.py:119
  (6 other events, 24.1 us)

commit v2 on v1

--- a/solution.py
+++ b/solution.py
@@ -106,9 +106,11 @@
 DEVICES = list(itertools.product(*(range(size) for size in SIZES)))
 ZS = 4
 HZ = HEADS // ZS
+NOTE = 16
 ANY = pl.BlockSpec(memory_space=pl.ANY)
 SMEM = pl.BlockSpec(memory_space=pltpu.SMEM)
 VMEM = pl.BlockSpec(memory_space=pltpu.VMEM)
+HBM = pl.BlockSpec(memory_space=pltpu.HBM)
 
 
 def flat(x, z, y, c):
@@ -123,6 +125,10 @@
     return lambda x, z, y, c: (x, (z + distance) % ZS, y, c)
 
 
+def both_ways(x, z, y, c):
+    return (x, (z + 1) % ZS, y, c) if c == 0 else (x, (z - 1) % ZS, y, c)
+
+
 def over_blk(x, z, y, c):
     return (1 - x, z, y, c)
 
@@ -139,154 +145,176 @@
     return (x, z, y, 1 - c)
 
 
-def pack_kernel(place, q_ref, kv_ref, out_w, up_w, down_w, *refs):
+def after(value, *earlier):
+    return lax.optimization_barrier((value,) + earlier)[0]
+
+
+def pack_kernel(place, listed, length, q_hbm, kv_hbm, out_w, up_w, down_w, *refs):
     kv_slots, q_slots, piece = refs[:ZS], refs[ZS : 2 * ZS], refs[2 * ZS]
-    kv_all, q_all, sems = refs[2 * ZS + 1 :]
-    x, z, y, c = place[0], place[1], place[2], place[3]
+    kv_all, q_all, q_ref, kv_ref, sems = refs[2 * ZS + 1 :]
+    x, z, y = place[0], place[1], place[2]
     p = 2 * x + y
-    m = 2 * p + c
     ro, cols = out_w.shape[0] // 4, out_w.shape[1] // 2
     ru, rd = up_w.shape[0], down_w.shape[0] // 8
     rows = [ro, ro + ru, ro + ru + rd]
     copies = [
-        pltpu.make_async_copy(
-            out_w.at[pl.ds(pl.multiple_of(p * ro, 16), ro), pl.ds(pl.multiple_of(c * cols, 128), cols)],
-            piece.at[pl.ds(0, ro)],
-            sems.at[0],
-        ),
-        pltpu.make_async_copy(
-            up_w.at[:, pl.ds(pl.multiple_of(m * cols, 128), cols)],
-            piece.at[pl.ds(rows[0], ru)],
-            sems.at[1],
-        ),
+        pltpu.make_async_copy(kv_hbm, kv_ref, sems.at[0]),
+        pltpu.make_async_copy(q_hbm, q_ref, sems.at[1]),
     ]
-    for half in range(2):
+    for e in range(2):
+        m = 2 * p + e
         copies.append(
             pltpu.make_async_copy(
-                down_w.at[pl.ds(pl.multiple_of(m * rd, 16), rd), pl.ds(half * cols, cols)],
-                piece.at[pl.ds(rows[1 + half], rd)],
-                sems.at[2 + half],
+                out_w.at[pl.ds(pl.multiple_of(p * ro, 16), ro), pl.ds(e * cols, cols)],
+                piece.at[e, pl.ds(0, ro)],
+                sems.at[2],
             )
         )
+        copies.append(
+            pltpu.make_async_copy(
+                up_w.at[:, pl.ds(pl.multiple_of(m * cols, 128), cols)],
+                piece.at[e, pl.ds(rows[0], ru)],
+                sems.at[2],
+            )
+        )
+        for half in range(2):
+            copies.append(
+                pltpu.make_async_copy(
+                    down_w.at[pl.ds(pl.multiple_of(m * rd, 16), rd), pl.ds(half * cols, cols)],
+                    piece.at[e, pl.ds(rows[1 + half], rd)],
+                    sems.at[2],
+                )
+            )
     for copy in copies:
         copy.start()
     n = q_ref.shape[0] // 2
+    lane = lax.broadcasted_iota(jnp.int32, (NOTE, 2 * HD), 1)
+    note = jnp.where(lane == LIST, length[0], 0)
+    for j in range(LIST):
+        note = jnp.where(lane == j, listed[0, j], note)
+    note = note.astype(jnp.float32).astype(jnp.bfloat16)
+    copies[0].wait()
     for head in range(HEADS):
         lanes = slice(head * HD, (head + 1) * HD)
         kv_all[head // HZ, head % HZ] = jnp.concatenate(
             [kv_ref[0, :, lanes], kv_ref[1, :, lanes]], axis=1
         )
-        q_all[head // HZ, head % HZ] = jnp.concatenate([q_ref[:n, lanes], q_ref[n:, lanes]], axis=1)
+    copies[1].wait()
+    for head in range(HEADS):
+        lanes = slice(head * HD, (head + 1) * HD)
+        q_all[head // HZ, (head % HZ) * n : (head % HZ + 1) * n] = jnp.concatenate(
+            [q_ref[:n, lanes], q_ref[n:, lanes]], axis=1
+        )
     for s in range(ZS):
         there = lax.rem(z + s, ZS)
         kv_slots[s][...] = kv_all[there]
-        q_slots[s][...] = q_all[there]
-    for copy in copies:
+        q_slots[s][: HZ * n] = q_all[there]
+        q_slots[s][HZ * n :] = note
+    for copy in copies[2:]:
         copy.wait()
 
 
-def packed(place, queries, keys_values, out_weight, up_weight, down_weight):
+def packed(place, listed, length, queries, keys_values, out_weight, up_weight, down_weight):
     rows, width = queries.shape
     cols = width // 2
     piece_rows = out_weight.shape[0] // 4 + up_weight.shape[0] + down_weight.shape[0] // 4
-    kv_shape, q_shape = (HZ, rows, 2 * HD), (HZ, rows // 2, 2 * HD)
+    kv_shape, q_rows = (HZ, rows, 2 * HD), HZ * rows // 2
     made = lambda shape: jax.ShapeDtypeStruct(shape, jnp.bfloat16)
     outs = pl.pallas_call(
         pack_kernel,
-        out_shape=[made(kv_shape)] * ZS + [made(q_shape)] * ZS + [made((piece_rows, cols))],
-        in_specs=[SMEM, VMEM, VMEM, ANY, ANY, ANY],
-        out_specs=[VMEM] * (2 * ZS) + [ANY],
+        out_shape=[made(kv_shape)] * ZS + [made((q_rows + NOTE, 2 * HD))] * ZS + [made((2, piece_rows, cols))],
+        in_specs=[SMEM] * 3 + [HBM] * 5,
+        out_specs=[VMEM] * (2 * ZS + 1),
         scratch_shapes=[
             pltpu.VMEM((ZS,) + kv_shape, jnp.bfloat16),
-            pltpu.VMEM((ZS,) + q_shape, jnp.bfloat16),
-            pltpu.SemaphoreType.DMA((4,)),
+            pltpu.VMEM((ZS, q_rows, 2 * HD), jnp.bfloat16),
+            pltpu.VMEM(queries.shape, jnp.bfloat16),
+            pltpu.VMEM(keys_values.shape, jnp.bfloat16),
+            pltpu.SemaphoreType.DMA((3,)),
         ],
-        compiler_params=pltpu.CompilerParams(vmem_limit_bytes=16 * MIB),
+        compiler_params=pltpu.CompilerParams(vmem_limit_bytes=58 * MIB),
         cost_estimate=pl.CostEstimate(flops=0, bytes_accessed=4 * MIB, transcendentals=0),
         name="pack_heads",
-    )(place, queries, keys_values, out_weight, up_weight, down_weight)
+    )(place, listed, length, queries, keys_values, out_weight, up_weight, down_weight)
     return outs[:ZS], outs[ZS : 2 * ZS], outs[2 * ZS]
 
 
-def attend_kernel(place, lists, *refs):
-    kv_near, kv_far, q_slots = refs[:ZS], refs[ZS : 2 * ZS], refs[2 * ZS : 3 * ZS]
-    out_slots, (blocks, sems) = refs[3 * ZS : 4 * ZS], refs[4 * ZS :]
+def attend_kernel(place, *refs):
+    held, q_ref, o_ref, blocks = refs[: 2 * ZS], refs[2 * ZS], refs[2 * ZS + 1], refs[2 * ZS + 2]
     x, z = place[0], place[1]
-    copies = []
-    for s in range(ZS):
-        source = lax.rem(z - s + ZS, ZS)
-        for side, held in ((x, kv_near[s]), (1 - x, kv_far[s])):
-            copies.append(
-                pltpu.make_async_copy(held, blocks.at[side * ZS + source], sems.at[len(copies)])
-            )
-    for copy in copies:
-        copy.start()
-    for copy in copies:
-        copy.wait()
-    n = q_slots[0].shape[1]
+    n = o_ref.shape[1]
+    note = q_ref[HZ * n :].astype(jnp.float32)
+    row = lax.broadcasted_iota(jnp.int32, note.shape, 0)
+    lane = lax.broadcasted_iota(jnp.int32, note.shape, 1)
+
+    def noted(j):
+        return jnp.max(jnp.where((row == 0) & (lane == j), note, 0.0)).astype(jnp.int32)
+
+    length = noted(LIST)
+    for j in range(LIST):
+        block = noted(j)
+        side, source = block // ZS, lax.rem(block, ZS)
+        at = jnp.where(side == x, 0, ZS) + lax.rem(z - source + ZS, ZS)
+        for i in range(2 * ZS):
+
+            @pl.when((at == i) & (j < length))
+            def _(i=i, j=j):
+                blocks[j] = held[i][...]
+
     low = lax.broadcasted_iota(jnp.int32, (n, 2 * HD), 1) < HD
     scale = LOG2E / HD**0.5
-    for s in range(ZS):
-
-        @pl.loop(0, HZ)
-        def _(h, s=s):
-            pair = q_slots[s][h]
-            results = []
-            for half in range(2):
-                q = pair if half == 0 else pltpu.roll(pair, HD, 1)
-                q = jnp.where(low, q, jnp.zeros_like(q))
-                scores = []
-                for j in range(LIST):
-                    kv = blocks[lists[s, j], h]
-                    raw = lax.dot_general(
-                        q, kv, (((1,), (1,)), ((), ())), preferred_element_type=jnp.float32
-                    )
-                    if j > 0:
-                        raw = jnp.where(j < lists[s, LIST], raw, -1e30)
-                    scores.append(raw)
-                top = scores[0]
-                for raw in scores[1:]:
-                    top = jnp.maximum(top, raw)
-                top = jnp.max(top, axis=1, keepdims=True)
-                total, acc = None, None
-                for j in range(LIST):
-                    weights = jnp.exp2((scores[j] - top) * scale)
-                    total = weights if j == 0 else total + weights
-                    part = jnp.dot(
-                        weights.astype(jnp.bfloat16),
-                        blocks[lists[s, j], h],
-                        preferred_element_type=jnp.float32,
-                    )
-                    acc = part if j == 0 else acc + part
-                results.append(acc / jnp.sum(total, axis=1, keepdims=True))
-            upper, lower = results
-            both = jnp.where(low, pltpu.roll(upper, HD, 1), lower)
-            out_slots[s][h] = both.astype(jnp.bfloat16)
-
-
-def attended(place, lists, kv_near, kv_far, q_slots):
-    kv_shape, q_shape = kv_near[0].shape, q_slots[0].shape
+
+    def attend(q, h, count):
+        scores = [
+            lax.dot_general(
+                q, blocks[j, h], (((1,), (1,)), ((), ())), preferred_element_type=jnp.float32
+            )
+            for j in range(count)
+        ]
+        top = functools.reduce(jnp.maximum, scores)
+        top = jnp.max(top, axis=1, keepdims=True)
+        total, acc = None, None
+        for j in range(count):
+            weights = jnp.exp2((scores[j] - top) * scale)
+            part = jnp.dot(
+                weights.astype(jnp.bfloat16), blocks[j, h], preferred_element_type=jnp.float32
+            )
+            total = weights if j == 0 else total + weights
+            acc = part if j == 0 else acc + part
+        return acc / jnp.sum(total, axis=1, keepdims=True)
+
+    for count in range(1, LIST + 1):
+
+        @pl.when(length == count)
+        def _(count=count):
+            for h in range(HZ):
+                pair = q_ref[h * n : (h + 1) * n]
+                none = jnp.zeros_like(pair)
+                upper = attend(jnp.where(low, pair, none), h, count)
+                lower = attend(jnp.where(low, pltpu.roll(pair, HD, 1), none), h, count)
+                o_ref[h] = jnp.where(low, pltpu.roll(upper, HD, 1), lower).astype(jnp.bfloat16)
+
+
+def attended(place, held, q):
+    kv_shape = held[0].shape
     return pl.pallas_call(
         attend_kernel,
-        out_shape=[jax.ShapeDtypeStruct(q_shape, jnp.bfloat16)] * ZS,
-        in_specs=[SMEM, SMEM] + [ANY] * (2 * ZS) + [VMEM] * ZS,
-        out_specs=[VMEM] * ZS,
-        scratch_shapes=[
-            pltpu.VMEM((2 * ZS,) + kv_shape, jnp.bfloat16),
-            pltpu.SemaphoreType.DMA((2 * ZS,)),
-        ],
+        out_shape=jax.ShapeDtypeStruct((HZ, kv_shape[1] // 2, 2 * HD), jnp.bfloat16),
+        in_specs=[SMEM] + [VMEM] * (2 * ZS + 1),
+        out_specs=VMEM,
+        scratch_shapes=[pltpu.VMEM((LIST,) + kv_shape, jnp.bfloat16)],
         compiler_params=pltpu.CompilerParams(vmem_limit_bytes=16 * MIB),
         cost_estimate=pl.CostEstimate(
-            flops=2 * 10**9, bytes_accessed=3 * MIB, transcendentals=3 * 10**6
+            flops=5 * 10**8, bytes_accessed=MIB, transcendentals=8 * 10**5
         ),
         name="attend",
-    )(place, lists, *kv_near, *kv_far, *q_slots)
-
-
-def feed_kernel(groups, place, gain, surface, *refs):
+    )(place, *held, q)
+
+
+def feed_kernel(place, gain, surface, *refs):
     ctx_slots, (out_w, up_w, down_w) = refs[:ZS], refs[ZS : ZS + 3]
     refs = refs[ZS + 3 :]
-    count = 2 * 2 * len(groups)
+    count = 4
     held, o_ref = refs[:count], refs[count]
     out_all, up_all, down_all, sems = refs[count + 1 :]
     x, z, y, c = place[0], place[1], place[2], place[3]
@@ -303,30 +331,32 @@
     copied(second, up_w, up_all.at[pl.ds(pl.multiple_of(z * ru, 16), ru)], 1)
     copied(third, down_w, down_all.at[pl.ds(pl.multiple_of(z * 8 * rd, 16), 8 * rd)], 2)
     at = 0
-    for slots in groups:
+    for split in range(2):
         for swapped in range(2):
             core = c if swapped == 0 else 1 - c
+            k = 2 if split else 1 + 2 * core
+            source = lax.rem(z - k + ZS, ZS)
+            slot_row = lax.rem(ZS - k, ZS) * rs
             fx, fy = jnp.where(core == 0, 1 - x, x), jnp.where(core == 0, y, 1 - y)
+            ref = held[at]
+            at += 1
             for later in range(2):
-                ref = held[at]
-                at += 1
-                for i, k in enumerate(slots):
-                    source = lax.rem(z - k + ZS, ZS)
-                    for e in range(2):
-                        px, py = (x, y) if e == 0 else (fx, fy)
-                        if later:
-                            px = jnp.where(core == 0, px, 1 - px)
-                            py = jnp.where(core == 0, 1 - py, py)
-                        p = 2 * px + py
-                        m = 2 * p + core
-                        piece = ref.at[e, i]
-                        slot_row = ((ZS - k) % ZS) * rs
+                for e in range(2):
+                    px, py = (x, y) if e == 0 else (fx, fy)
+                    if later:
+                        px = jnp.where(core == 0, px, 1 - px)
+                        py = jnp.where(core == 0, 1 - py, py)
+                    p = 2 * px + py
+                    for i in range(1 if split else 2):
+                        half = core if split else i
+                        m = 2 * p + half
+                        piece = ref.at[2 * later + e, i]
                         copied(
                             first,
                             piece.at[pl.ds(0, ro)],
                             out_all.at[
                                 pl.ds(pl.multiple_of(slot_row + p * ro, 16), ro),
-                                pl.ds(pl.multiple_of(core * cols, 128), cols),
+                                pl.ds(pl.multiple_of(half * cols, 128), cols),
                             ],
                             0,
                         )
@@ -339,13 +369,13 @@
                             ],
                             1,
                         )
-                        for half in range(2):
+                        for side in range(2):
                             copied(
                                 third,
-                                piece.at[pl.ds(rows[2 + half], rd)],
+                                piece.at[pl.ds(rows[2 + side], rd)],
                                 down_all.at[
                                     pl.ds(pl.multiple_of((source * 8 + m) * rd, 16), rd),
-                                    pl.ds(half * cols, cols),
+                                    pl.ds(side * cols, cols),
                                 ],
                                 2,
                             )
@@ -384,11 +414,11 @@
     o_ref[...] = total.astype(jnp.bfloat16)
 
 
-def fed(groups, place, gain, surface, ctx_slots, weights, held):
+def fed(place, gain, surface, ctx_slots, weights, held):
     out_weight, up_weight, down_weight = weights
     width, hidden_units = up_weight.shape[0] * ZS, up_weight.shape[1]
     return pl.pallas_call(
-        functools.partial(feed_kernel, groups),
+        feed_kernel,
         out_shape=jax.ShapeDtypeStruct(surface.shape, jnp.bfloat16),
         in_specs=[SMEM, VMEM, VMEM] + [VMEM] * ZS + [ANY] * (3 + len(held)),
         out_specs=VMEM,
@@ -418,40 +448,48 @@
     list_lengths,
 ):
     place = jnp.stack([lax.axis_index(axis) for axis in AXES]).astype(jnp.int32)
-    entries = jnp.concatenate([block_lists[0], list_lengths, jnp.zeros(3, jnp.int32)])[None, :]
     kv_slots, q_slots, piece = packed(
-        place, queries, keys_values, out_weight, up_weight, down_weight
-    )
-    shifts = (1, 3, 2)
-    lists, near, q_got = {0: entries}, {0: kv_slots[0]}, {0: q_slots[0]}
-    far = {0: sent(kv_slots[0], over_blk)}
-    for s in shifts:
-        near[s] = sent(kv_slots[s], along_head(s))
-    for s in shifts:
-        q_got[s] = sent(q_slots[s], along_head(s))
-        lists[s] = sent(entries, along_head(s))
-    for s in shifts:
-        far[s] = sent(near[s], over_blk)
-
-    groups = ((1, 3), (2,))
-    held = []
-    for slots in groups:
-        mine = jnp.stack([sent(piece, along_head(k)) for k in slots])
-        pair = jnp.stack([mine, sent(mine, plane_first)])
-        other = sent(pair, plane_second)
-        held += [pair, other, sent(pair, other_core), sent(other, other_core)]
-
-    order = range(ZS)
-    ctx = attended(
-        place,
-        jnp.concatenate([lists[s] for s in order]),
-        [near[s] for s in order],
-        [far[s] for s in order],
-        [q_got[s] for s in order],
-    )
-    ctx_slots = [ctx[0]] + [sent(ctx[s], along_head(-s)) for s in range(1, ZS)]
+        place, block_lists, list_lengths, queries, keys_values, out_weight, up_weight, down_weight
+    )
+    core = place[3]
+    kv_slots, q_slots = list(kv_slots), list(q_slots)
+    near, q, far = {0: kv_slots[0]}, {0: q_slots[0]}, {}
+    w13 = sent(piece, both_ways)
+    far[0] = sent(kv_slots[0], over_blk)
+    near[1], near[3] = (sent(kv_slots[s], along_head(s)) for s in (1, 3))
+    w13, near[1], near[3], far[0], kv_slots[2] = lax.optimization_barrier(
+        (w13, near[1], near[3], far[0], kv_slots[2])
+    )
+    first13 = sent(w13, plane_first)
+    far13 = sent(jnp.stack([near[1], near[3]]), over_blk)
+    near[2] = sent(kv_slots[2], along_head(2))
+    w2 = sent(lax.dynamic_index_in_dim(w13, core, 0, keepdims=True), both_ways)
+    first13, far13, near[2], w2, q_slots[1], q_slots[2], q_slots[3] = lax.optimization_barrier(
+        (first13, far13, near[2], w2, q_slots[1], q_slots[2], q_slots[3])
+    )
+    far[1], far[3] = far13[0], far13[1]
+    pair13 = jnp.stack([w13, first13])
+    second13 = sent(pair13, plane_second)
+    far[2] = sent(near[2], over_blk)
+    for s in (2, 1, 3):
+        q[s] = sent(q_slots[s], along_head(s))
+    first2 = sent(w2, plane_first)
+    first2, q[1], q[2], q[3], far[2], second13 = lax.optimization_barrier((first2, q[1], q[2], q[3], far[2], second13))
+    pair2 = jnp.stack([w2, first2])
+    second2 = sent(pair2, plane_second)
+    blocks = [near[s] for s in range(ZS)] + [far[s] for s in range(ZS)]
+    ctx_slots, ctxs = {}, []
+    for s in (2, 1, 3, 0):
+        ctx = attended(place, blocks, q[s])
+        ctxs.append(ctx)
+        ctx_slots[s] = sent(ctx, along_head(-s)) if s else ctx
+    all13 = jnp.concatenate([pair13, second13])
+    core13 = sent(all13, other_core)
+    all2 = jnp.concatenate([after(pair2, *ctxs[:3]), second2])
+    held = [all13, core13, all2, sent(all2, other_core)]
     weights = (out_weight, up_weight, down_weight)
-    return fed(groups, place, norm_gain[None, :], surface, ctx_slots, weights, held)
+    ctx_slots = [ctx_slots[s] for s in range(ZS)]
+    return fed(place, norm_gain[None, :], surface, ctx_slots, weights, held)
 
 
 def solution(mesh):

time: 151 us -> 108 us (0.72)
  waiting for transfers between devices: 98.3 us -> 42.9 us
  starting transfers between devices: 23.8 us -> 38.2 us
  local copies, waits for them, and re-layouts: 5.66 us -> 0.31 us
  Pallas kernels: 21.7 us -> 24.4 us
    ppermute x27 -> x20, waiting for transfers between devices: 98.3 us -> 42.9 us  [sent(): lax.ppermute(value, AXES, [(flat(*d), flat(*route(*d))) for d in DEVICES])]
    ppermute x27 -> x20, starting transfers between devices: 23.8 us -> 38.2 us  [sent(): lax.ppermute(value, AXES, [(flat(*d), flat(*route(*d))) for d in DEVICES])]
    unnamed x22 -> x25, local copies, waits for them, and re-layouts: 5.66 us -> 0.13 us
    pallas_call x3 -> x6, Pallas kernels: 21.7 us -> 24.4 us  [the longest x4 13.3 us: attended(): pl.pallas_call(attend_kernel, out_shape=jax.ShapeDtypeStruct((HZ, kv_shap...]
  transfers between devices with their start and end apart: 27 -> 20, of which waited for: 17 -> 8; matrix products, arithmetic and copies ran while one was open for 0% -> 0% of each run, Pallas kernels for 9% -> 12%
where the time goes in v2:
time: 108 us
  waiting for transfers between devices  42.9 us (40%)
  starting transfers between devices  38.2 us (35%)
  Pallas kernels  24.4 us (23%)
  other arithmetic  1.25 us (1%)
  between operations  1.1 us (1%)
    ppermute x20, waiting for transfers between devices, sent(): lax.ppermute(value, AXES, [(flat(*d), flat(*route(*d))) for d in DEVICES])  42.9 us
    ppermute x20, starting transfers between devices, sent(): lax.ppermute(value, AXES, [(flat(*d), flat(*route(*d))) for d in DEVICES])  38.2 us
    pallas_call x4, Pallas kernels, attended(): pl.pallas_call(attend_kernel, out_shape=jax.ShapeDtypeStruct((HZ, kv_shap...  13.3 us
    pallas_call x1, Pallas kernels, fed(): pl.pallas_call(feed_kernel, out_shape=jax.ShapeDtypeStruct(surface.shape,...  7.57 us
    pallas_call x1, Pallas kernels, packed(): pl.pallas_call(pack_kernel, out_shape=[made(kv_shape)] * ZS + [made((q_ro...  3.57 us
  transfers between devices with their start and end apart: 20, of which 8 were waited for; matrix products, arithmetic and copies ran while one was open for 0% of the time, Pallas kernels for 12%

profile of v2, /device:TPU:0, one launch (start us, length us, event | category | flops | bytes accessed | tf_op | source)
XLA Modules:
  0.0 108.2 jit_solution(4831494713382394114)
XLA Ops:
  0.7 0.7 pad_add_fusion.place
  1.3 3.6 %pack_heads.1 = (bf16[3,256,128]{2,1,0:T(8,128)(2,1)}, bf16[3,256,128]{2,1,0:T(8,128)(2,1)}, bf16[3,256,128]{2,1,0:T(8,128)(2,1)}, bf16[3,256,128]{2,1,0:T(8,128...) custom-call(s32[4]{0:T(128)} %pad_add_fusion.place, ...), custom_call_target="tpu_custom_call" | custom-call | bytes 4194304 | tf_op jit(solution)/shard_map/pack_heads/pallas_call | solution.py:223
  4.9 3.1 %collective-permute-start = (bf16[2,432,384]{2,1,0:T(8,128)(2,1)}, bf16[2,432,384]{2,1,0:T(8,128)(2,1)S(1)}, u32[]{:S(2)}, u32[]{:S(2)}) collective-permute-start(bf16[2,432,384]{2,1,0:T(8,128)(2,1)} %get-tuple-element.34), channel_id=1, source_target_pairs={{0,4},{1,13},{2,6},{3,15},{4,8},{5,1},{6,10},{7,3},{8,12},{9,5},{1... | collective-permute-start | bytes 1990664 | tf_op jit(solution)/shard_map/ppermute | solution.py:121
  8.0 1.6 %collective-permute-start.1 = (bf16[3,256,128]{2,1,0:T(8,128)(2,1)}, bf16[3,256,128]{2,1,0:T(8,128)(2,1)S(1)}, u32[]{:S(2)}, u32[]{:S(2)}) collective-permute-start(bf16[3,256,128]{2,1,0:T(8,128)(2,1)} %get-tuple-element.35), channel_id=1, source_target_pairs={{0,4},{1,5},{2,6},{3,7},{4,8},{5,9},{6,10},{7,11},{8,12},{9,13},{1... | collective-permute-start | bytes 589832 | tf_op jit(solution)/shard_map/ppermute | solution.py:121
  9.5 2.2 %collective-permute-start.2 = (bf16[3,256,128]{2,1,0:T(8,128)(2,1)}, bf16[3,256,128]{2,1,0:T(8,128)(2,1)S(1)}, u32[]{:S(2)}, u32[]{:S(2)}) collective-permute-start(bf16[3,256,128]{2,1,0:T(8,128)(2,1)} %get-tuple-element.36), channel_id=1, source_target_pairs={{0,12},{1,13},{2,14},{3,15},{4,0},{5,1},{6,2},{7,3},{8,4},{9,5},{1... | collective-permute-start | bytes 589832 | tf_op jit(solution)/shard_map/ppermute | solution.py:121
  11.8 1.5 %collective-permute-start.3 = (bf16[3,256,128]{2,1,0:T(8,128)(2,1)}, bf16[3,256,128]{2,1,0:T(8,128)(2,1)S(1)}, u32[]{:S(2)}, u32[]{:S(2)}) collective-permute-start(bf16[3,256,128]{2,1,0:T(8,128)(2,1)} %get-tuple-element.33.refs_0_), channel_id=1, source_target_pairs={{0,16},{1,17},{2,18},{3,19},{4,20},{5,21},{6,22},{7,23},{8,24},{9,... | collective-permute-start | bytes 589832 | tf_op jit(solution)/shard_map/ppermute | solution.py:121
  13.3 16.9 %collective-permute-done.1.refs_1_ = bf16[3,256,128]{2,1,0:T(8,128)(2,1)S(1)} collective-permute-done((bf16[3,256,128]{2,1,0:T(8,128)(2,1)}, bf16[3,256,128]{2,1,0:T(8,128)(2,1)S(1)}, u32[]{:S(2)}, u32[]{:S(2)}) %collective-permute-start.1) | collective-permute-done | bytes 196640 | tf_op jit(solution)/shard_map/ppermute | solution.py:121
  30.1 1.0 collective-permute-done.2.refs_3_
  31.1 1.5 %collective-permute-start.4 = (bf16[2,432,384]{2,1,0:T(8,128)(2,1)S(1)}, bf16[2,432,384]{2,1,0:T(8,128)(2,1)S(1)}, u32[]{:S(2)}, u32[]{:S(2)}) collective-permute-start(bf16[2,432,384]{2,1,0:T(8,128)(2,1)S(1)} %collective-permute-done), channel_id=1, source_target_pairs={{0,16},{1,3},{2,18},{3,1},{4,20},{5,7},{6,22},{7,5},{8,24},{9,11},... | collective-permute-start | bytes 1990664 | tf_op jit(solution)/shard_map/ppermute | solution.py:121
  32.7 0.6 collective-permute-start.5
  33.4 4.7 %collective-permute-start.6 = (bf16[3,256,128]{2,1,0:T(8,128)(2,1)S(1)}, bf16[3,256,128]{2,1,0:T(8,128)(2,1)S(1)}, u32[]{:S(2)}, u32[]{:S(2)}) collective-permute-start(bf16[3,256,128]{2,1,0:T(8,128)(2,1)S(1)} %copy-done.8), channel_id=1, source_target_pairs={{0,8},{1,9},{2,10},{3,11},{4,12},{5,13},{6,14},{7,15},{8,0},{9,1},... | collective-permute-start | bytes 589832 | tf_op jit(solution)/shard_map/ppermute | solution.py:121
  38.1 13.1 %collective-permute-done.6.refs_2_ = bf16[3,256,128]{2,1,0:T(8,128)(2,1)S(1)} collective-permute-done((bf16[3,256,128]{2,1,0:T(8,128)(2,1)S(1)}, bf16[3,256,128]{2,1,0:T(8,128)(2,1)S(1)}, u32[]{:S(2)}, u32[]{:S(2)}) %collective-permute-start.6) | collective-permute-done | bytes 196640 | tf_op jit(solution)/shard_map/ppermute | solution.py:121
  51.4 1.8 %collective-permute-start.13 = (bf16[2,2,432,384]{3,2,1,0:T(8,128)(2,1)S(1)}, bf16[2,2,432,384]{3,2,1,0:T(8,128)(2,1)S(1)}, u32[]{:S(2)}, u32[]{:S(2)}) collective-permute-start(bf16[2,2,432,384]{3,2,1,0:T(8,128)(2,1)S(1)} %pad_maximum_fusion.1), channel_id=1, source_target_pairs={{0,2},{1,17},{2,0},{3,19},{4,6},{5,21},{6,4},{7,23},{8,10},{9,25},... | collective-permute-start | bytes 3981320 | tf_op jit(solution)/shard_map/ppermute | solution.py:121
  53.2 1.5 %collective-permute-start.8 = (bf16[1,432,384]{2,1,0:T(8,128)(2,1)S(1)}, bf16[1,432,384]{2,1,0:T(8,128)(2,1)S(1)}, u32[]{:S(2)}, u32[]{:S(2)}) collective-permute-start(bf16[1,432,384]{2,1,0:T(8,128)(2,1)S(1)} %collective-permute-done.7), channel_id=1, source_target_pairs={{0,16},{1,3},{2,18},{3,1},{4,20},{5,7},{6,22},{7,5},{8,24},{9,11},... | collective-permute-start | bytes 995336 | tf_op jit(solution)/shard_map/ppermute | solution.py:121
  54.7 1.5 %collective-permute-start.9 = (bf16[400,128]{1,0:T(8,128)(2,1)S(1)}, bf16[400,128]{1,0:T(8,128)(2,1)S(1)}, u32[]{:S(2)}, u32[]{:S(2)}) collective-permute-start(bf16[400,128]{1,0:T(8,128)(2,1)S(1)} %copy-done.11), channel_id=1, source_target_pairs={{0,4},{1,5},{2,6},{3,7},{4,8},{5,9},{6,10},{7,11},{8,12},{9,13},{1... | collective-permute-start | bytes 307208 | tf_op jit(solution)/shard_map/ppermute | solution.py:121
  56.3 1.2 %collective-permute-start.12 = (bf16[3,256,128]{2,1,0:T(8,128)(2,1)S(1)}, bf16[3,256,128]{2,1,0:T(8,128)(2,1)S(1)}, u32[]{:S(2)}, u32[]{:S(2)}) collective-permute-start(bf16[3,256,128]{2,1,0:T(8,128)(2,1)S(1)} %collective-permute-done.6.refs_2_), channel_id=1, source_target_pairs={{0,16},{1,17},{2,18},{3,19},{4,20},{5,21},{6,22},{7,23},{8,24},{9,... | collective-permute-start | bytes 589832 | tf_op jit(solution)/shard_map/ppermute | solution.py:121
  57.5 3.4 %collective-permute-start.10 = (bf16[400,128]{1,0:T(8,128)(2,1)S(1)}, bf16[400,128]{1,0:T(8,128)(2,1)S(1)}, u32[]{:S(2)}, u32[]{:S(2)}) collective-permute-start(bf16[400,128]{1,0:T(8,128)(2,1)S(1)} %copy-done.10), channel_id=1, source_target_pairs={{0,8},{1,9},{2,10},{3,11},{4,12},{5,13},{6,14},{7,15},{8,0},{9,1},... | collective-permute-start | bytes 307208 | tf_op jit(solution)/shard_map/ppermute | solution.py:121
  60.9 2.1 %collective-permute-done.9.refs_8_ = bf16[400,128]{1,0:T(8,128)(2,1)S(1)} collective-permute-done((bf16[400,128]{1,0:T(8,128)(2,1)S(1)}, bf16[400,128]{1,0:T(8,128)(2,1)S(1)}, u32[]{:S(2)}, u32[]{:S(2)}) %collective-permute-start.9) | collective-permute-done | bytes 102432 | tf_op jit(solution)/shard_map/ppermute | solution.py:121
  63.0 3.7 %collective-permute-start.11 = (bf16[400,128]{1,0:T(8,128)(2,1)S(1)}, bf16[400,128]{1,0:T(8,128)(2,1)S(1)}, u32[]{:S(2)}, u32[]{:S(2)}) collective-permute-start(bf16[400,128]{1,0:T(8,128)(2,1)S(1)} %copy-done.9), channel_id=1, source_target_pairs={{0,12},{1,13},{2,14},{3,15},{4,0},{5,1},{6,2},{7,3},{8,4},{9,5},{1... | collective-permute-start | bytes 307208 | tf_op jit(solution)/shard_map/ppermute | solution.py:121
  66.7 2.2 %collective-permute-done.11.refs_8_ = bf16[400,128]{1,0:T(8,128)(2,1)S(1)} collective-permute-done((bf16[400,128]{1,0:T(8,128)(2,1)S(1)}, bf16[400,128]{1,0:T(8,128)(2,1)S(1)}, u32[]{:S(2)}, u32[]{:S(2)}) %collective-permute-start.11) | collective-permute-done | bytes 102432 | tf_op jit(solution)/shard_map/ppermute | solution.py:121
  68.9 3.9 %collective-permute-done.13 = bf16[2,2,432,384]{3,2,1,0:T(8,128)(2,1)S(1)} collective-permute-done((bf16[2,2,432,384]{3,2,1,0:T(8,128)(2,1)S(1)}, bf16[2,2,432,384]{3,2,1,0:T(8,128)(2,1)S(1)}, u32[]{:S(2)}, u32[]{:S(2)}) %collective-permute-start.13) | collective-permute-done | bytes 1327136 | tf_op jit(solution)/shard_map/ppermute | solution.py:121
  73.2 5.3 %collective-permute-start.17 = (bf16[4,2,432,384]{3,2,1,0:T(8,128)(2,1)S(1)}, bf16[4,2,432,384]{3,2,1,0:T(8,128)(2,1)S(1)}, u32[]{:S(2)}, u32[]{:S(2)}) collective-permute-start(bf16[4,2,432,384]{3,2,1,0:T(8,128)(2,1)S(1)} %pad_maximum_fusion.refs_7_), channel_id=1, source_target_pairs={{0,1},{1,0},{2,3},{3,2},{4,5},{5,4},{6,7},{7,6},{8,9},{9,8},{10,11... | collective-permute-start | bytes 7962632 | tf_op jit(solution)/shard_map/ppermute | solution.py:121
  78.6 0.6 collective-permute-start.18
  79.2 3.6 %attend.5 = bf16[3,128,128]{2,1,0:T(8,128)(2,1)S(1)} custom-call(s32[4]{0:T(128)S(1)} %copy-done.4, bf16[3,256,128]{2,1,0:T(8,128)(2,1)S(1)} %copy-done.5, bf16[3,256,128]{2,1,0:T(8,128)(2,1)S(1)} %collective-permute-done.1.refs_1_, bf16[3,256,128]{2,1,0:T(8,128)(2,1)S(1)} %collective-permute-done.6.refs_2_, ...), custom_call_target="tpu_custom_call" | custom-call | flops 500000000 | bytes 1048576 | tf_op jit(solution)/shard_map/attend/pallas_call | solution.py:300
  82.8 3.8 %attend.6 = bf16[3,128,128]{2,1,0:T(8,128)(2,1)S(1)} custom-call(s32[4]{0:T(128)S(1)} %copy-done.4, bf16[3,256,128]{2,1,0:T(8,128)(2,1)S(1)} %copy-done.5, bf16[3,256,128]{2,1,0:T(8,128)(2,1)S(1)} %collective-permute-done.1.refs_1_, bf16[3,256,128]{2,1,0:T(8,128)(2,1)S(1)} %collective-permute-done.6.refs_2_, ...), custom_call_target="tpu_custom_call" | custom-call | flops 500000000 | bytes 1048576 | tf_op jit(solution)/shard_map/attend/pallas_call | solution.py:300
  86.6 2.1 %attend.7 = bf16[3,128,128]{2,1,0:T(8,128)(2,1)S(1)} custom-call(s32[4]{0:T(128)S(1)} %copy-done.4, bf16[3,256,128]{2,1,0:T(8,128)(2,1)S(1)} %copy-done.5, bf16[3,256,128]{2,1,0:T(8,128)(2,1)S(1)} %collective-permute-done.1.refs_1_, bf16[3,256,128]{2,1,0:T(8,128)(2,1)S(1)} %collective-permute-done.6.refs_2_, ...), custom_call_target="tpu_custom_call" | custom-call | flops 500000000 | bytes 1048576 | tf_op jit(solution)/shard_map/attend/pallas_call | solution.py:300
  88.8 0.5 collective-permute-done.18
  89.6 1.2 %collective-permute-start.15 = (bf16[3,128,128]{2,1,0:T(8,128)(2,1)S(1)}, bf16[3,128,128]{2,1,0:T(8,128)(2,1)S(1)}, u32[]{:S(2)}, u32[]{:S(2)}) collective-permute-start(bf16[3,128,128]{2,1,0:T(8,128)(2,1)S(1)} %attend.6), channel_id=1, source_target_pairs={{0,8},{1,9},{2,10},{3,11},{4,12},{5,13},{6,14},{7,15},{8,0},{9,1},... | collective-permute-start | bytes 294920 | tf_op jit(solution)/shard_map/ppermute | solution.py:121
  90.8 2.6 %collective-permute-start.14 = (bf16[3,128,128]{2,1,0:T(8,128)(2,1)S(1)}, bf16[3,128,128]{2,1,0:T(8,128)(2,1)S(1)}, u32[]{:S(2)}, u32[]{:S(2)}) collective-permute-start(bf16[3,128,128]{2,1,0:T(8,128)(2,1)S(1)} %attend.5), channel_id=1, source_target_pairs={{0,12},{1,13},{2,14},{3,15},{4,0},{5,1},{6,2},{7,3},{8,4},{9,5},{1... | collective-permute-start | bytes 294920 | tf_op jit(solution)/shard_map/ppermute | solution.py:121
  93.4 3.8 %attend.4.refs_0_ = bf16[3,128,128]{2,1,0:T(8,128)(2,1)S(1)} custom-call(s32[4]{0:T(128)S(1)} %copy-done.4, bf16[3,256,128]{2,1,0:T(8,128)(2,1)S(1)} %copy-done.5, bf16[3,256,128]{2,1,0:T(8,128)(2,1)S(1)} %collective-permute-done.1.refs_1_, bf16[3,256,128]{2,1,0:T(8,128)(2,1)S(1)} %collective-permute-done.6.refs_2_, ...), custom_call_target="tpu_custom_call" | custom-call | flops 500000000 | bytes 1048576 | tf_op jit(solution)/shard_map/attend/pallas_call | solution.py:300
  97.2 3.2 %collective-permute-done.15.refs_2_ = bf16[3,128,128]{2,1,0:T(8,128)(2,1)S(1)} collective-permute-done((bf16[3,128,128]{2,1,0:T(8,128)(2,1)S(1)}, bf16[3,128,128]{2,1,0:T(8,128)(2,1)S(1)}, u32[]{:S(2)}, u32[]{:S(2)}) %collective-permute-start.15) | collective-permute-done | bytes 98336 | tf_op jit(solution)/shard_map/ppermute | solution.py:121
  100.5 7.6 %feed.1 = bf16[256,768]{1,0:T(8,128)(2,1)} custom-call(s32[4]{0:T(128)S(1)} %copy-done.4, f32[1,768]{1,0:T(1,128)S(1)} %broadcast_in_dim.3.gain, bf16[256,768]{1,0:T(8,128)(2,1)S(1)} %copy-done.3, bf16[3,128,128]{2,1,0:T(8,128)(2,1)S(1)} %attend.4.refs_0_, bf16[3,128,128]{2,1,0:T(8,128)(2,1)S(1)} %collective-permute-done.14.refs_1_, ...), custom_call_target="tpu_custom_call" | custom-call | flops 3000000000 | bytes 12582912 | tf_op jit(solution)/shard_map/feed/pallas_call | solution.py:420
  (48 shorter events, 1.1 us)
Async XLA Ops:
  4.9 28.5 %copy-start.8 = (bf16[3,256,128]{2,1,0:T(8,128)(2,1)S(1)}, bf16[3,256,128]{2,1,0:T(8,128)(2,1)}, u32[]{:S(2)}) copy-start(bf16[3,256,128]{2,1,0:T(8,128)(2,1)} %get-tuple-element.41) | copy-start | bytes 589828
  4.9 26.2 %collective-permute-start = (bf16[2,432,384]{2,1,0:T(8,128)(2,1)}, bf16[2,432,384]{2,1,0:T(8,128)(2,1)S(1)}, u32[]{:S(2)}, u32[]{:S(2)}) collective-permute-start(bf16[2,432,384]{2,1,0:T(8,128)(2,1)} %get-tuple-element.34), channel_id=1, source_target_pairs={{0,4},{1,13},{2,6},{3,15},{4,8},{5,1},{6,10},{7,3},{8,12},{9,5},{1... | collective-permute-start | bytes 1990664 | tf_op jit(solution)/shard_map/ppermute | solution.py:121
  8.0 22.2 %collective-permute-start.1 = (bf16[3,256,128]{2,1,0:T(8,128)(2,1)}, bf16[3,256,128]{2,1,0:T(8,128)(2,1)S(1)}, u32[]{:S(2)}, u32[]{:S(2)}) collective-permute-start(bf16[3,256,128]{2,1,0:T(8,128)(2,1)} %get-tuple-element.35), channel_id=1, source_target_pairs={{0,4},{1,5},{2,6},{3,7},{4,8},{5,9},{6,10},{7,11},{8,12},{9,13},{1... | collective-permute-start | bytes 589832 | tf_op jit(solution)/shard_map/ppermute | solution.py:121
  9.5 21.6 %collective-permute-start.2 = (bf16[3,256,128]{2,1,0:T(8,128)(2,1)}, bf16[3,256,128]{2,1,0:T(8,128)(2,1)S(1)}, u32[]{:S(2)}, u32[]{:S(2)}) collective-permute-start(bf16[3,256,128]{2,1,0:T(8,128)(2,1)} %get-tuple-element.36), channel_id=1, source_target_pairs={{0,12},{1,13},{2,14},{3,15},{4,0},{5,1},{6,2},{7,3},{8,4},{9,5},{1... | collective-permute-start | bytes 589832 | tf_op jit(solution)/shard_map/ppermute | solution.py:121
  11.8 19.3 %collective-permute-start.3 = (bf16[3,256,128]{2,1,0:T(8,128)(2,1)}, bf16[3,256,128]{2,1,0:T(8,128)(2,1)S(1)}, u32[]{:S(2)}, u32[]{:S(2)}) collective-permute-start(bf16[3,256,128]{2,1,0:T(8,128)(2,1)} %get-tuple-element.33.refs_0_), channel_id=1, source_target_pairs={{0,16},{1,17},{2,18},{3,19},{4,20},{5,21},{6,22},{7,23},{8,24},{9,... | collective-permute-start | bytes 589832 | tf_op jit(solution)/shard_map/ppermute | solution.py:121
  31.1 20.1 %collective-permute-start.4 = (bf16[2,432,384]{2,1,0:T(8,128)(2,1)S(1)}, bf16[2,432,384]{2,1,0:T(8,128)(2,1)S(1)}, u32[]{:S(2)}, u32[]{:S(2)}) collective-permute-start(bf16[2,432,384]{2,1,0:T(8,128)(2,1)S(1)} %collective-permute-done), channel_id=1, source_target_pairs={{0,16},{1,3},{2,18},{3,1},{4,20},{5,7},{6,22},{7,5},{8,24},{9,11},... | collective-permute-start | bytes 1990664 | tf_op jit(solution)/shard_map/ppermute | solution.py:121
  32.7 18.6 %collective-permute-start.5 = (bf16[2,3,256,128]{3,2,1,0:T(8,128)(2,1)S(1)}, bf16[2,3,256,128]{3,2,1,0:T(8,128)(2,1)S(1)}, u32[]{:S(2)}, u32[]{:S(2)}) collective-permute-start(bf16[2,3,256,128]{3,2,1,0:T(8,128)(2,1)S(1)} %pad_maximum_fusion.3), channel_id=1, source_target_pairs={{0,16},{1,17},{2,18},{3,19},{4,20},{5,21},{6,22},{7,23},{8,24},{9,... | collective-permute-start | bytes 1179656 | tf_op jit(solution)/shard_map/ppermute | solution.py:121
  33.3 17.9 %collective-permute-start.7 = (bf16[1,432,384]{2,1,0:T(8,128)(2,1)S(1)}, bf16[1,432,384]{2,1,0:T(8,128)(2,1)S(1)}, u32[]{:S(2)}, u32[]{:S(2)}) collective-permute-start(bf16[1,432,384]{2,1,0:T(8,128)(2,1)S(1)} %constant_dynamic-slice_fusion), channel_id=1, source_target_pairs={{0,4},{1,13},{2,6},{3,15},{4,8},{5,1},{6,10},{7,3},{8,12},{9,5},{1... | collective-permute-start | bytes 995336 | tf_op jit(solution)/shard_map/ppermute | solution.py:121
  33.4 17.8 %collective-permute-start.6 = (bf16[3,256,128]{2,1,0:T(8,128)(2,1)S(1)}, bf16[3,256,128]{2,1,0:T(8,128)(2,1)S(1)}, u32[]{:S(2)}, u32[]{:S(2)}) collective-permute-start(bf16[3,256,128]{2,1,0:T(8,128)(2,1)S(1)} %copy-done.8), channel_id=1, source_target_pairs={{0,8},{1,9},{2,10},{3,11},{4,12},{5,13},{6,14},{7,15},{8,0},{9,1},... | collective-permute-start | bytes 589832 | tf_op jit(solution)/shard_map/ppermute | solution.py:121
  51.3 3.5 %copy-start.11 = (bf16[400,128]{1,0:T(8,128)(2,1)S(1)}, bf16[400,128]{1,0:T(8,128)(2,1)}, u32[]{:S(2)}) copy-start(bf16[400,128]{1,0:T(8,128)(2,1)} %get-tuple-element.49) | copy-start | bytes 307204
  51.3 6.2 %copy-start.10 = (bf16[400,128]{1,0:T(8,128)(2,1)S(1)}, bf16[400,128]{1,0:T(8,128)(2,1)}, u32[]{:S(2)}) copy-start(bf16[400,128]{1,0:T(8,128)(2,1)} %get-tuple-element.50) | copy-start | bytes 307204
  51.3 11.7 %copy-start.9 = (bf16[400,128]{1,0:T(8,128)(2,1)S(1)}, bf16[400,128]{1,0:T(8,128)(2,1)}, u32[]{:S(2)}) copy-start(bf16[400,128]{1,0:T(8,128)(2,1)} %get-tuple-element.51) | copy-start | bytes 307204
  51.4 21.4 %collective-permute-start.13 = (bf16[2,2,432,384]{3,2,1,0:T(8,128)(2,1)S(1)}, bf16[2,2,432,384]{3,2,1,0:T(8,128)(2,1)S(1)}, u32[]{:S(2)}, u32[]{:S(2)}) collective-permute-start(bf16[2,2,432,384]{3,2,1,0:T(8,128)(2,1)S(1)} %pad_maximum_fusion.1), channel_id=1, source_target_pairs={{0,2},{1,17},{2,0},{3,19},{4,6},{5,21},{6,4},{7,23},{8,10},{9,25},... | collective-permute-start | bytes 3981320 | tf_op jit(solution)/shard_map/ppermute | solution.py:121
  53.2 15.7 %collective-permute-start.8 = (bf16[1,432,384]{2,1,0:T(8,128)(2,1)S(1)}, bf16[1,432,384]{2,1,0:T(8,128)(2,1)S(1)}, u32[]{:S(2)}, u32[]{:S(2)}) collective-permute-start(bf16[1,432,384]{2,1,0:T(8,128)(2,1)S(1)} %collective-permute-done.7), channel_id=1, source_target_pairs={{0,16},{1,3},{2,18},{3,1},{4,20},{5,7},{6,22},{7,5},{8,24},{9,11},... | collective-permute-start | bytes 995336 | tf_op jit(solution)/shard_map/ppermute | solution.py:121
  54.7 8.2 %collective-permute-start.9 = (bf16[400,128]{1,0:T(8,128)(2,1)S(1)}, bf16[400,128]{1,0:T(8,128)(2,1)S(1)}, u32[]{:S(2)}, u32[]{:S(2)}) collective-permute-start(bf16[400,128]{1,0:T(8,128)(2,1)S(1)} %copy-done.11), channel_id=1, source_target_pairs={{0,4},{1,5},{2,6},{3,7},{4,8},{5,9},{6,10},{7,11},{8,12},{9,13},{1... | collective-permute-start | bytes 307208 | tf_op jit(solution)/shard_map/ppermute | solution.py:121
  56.3 12.6 %collective-permute-start.12 = (bf16[3,256,128]{2,1,0:T(8,128)(2,1)S(1)}, bf16[3,256,128]{2,1,0:T(8,128)(2,1)S(1)}, u32[]{:S(2)}, u32[]{:S(2)}) collective-permute-start(bf16[3,256,128]{2,1,0:T(8,128)(2,1)S(1)} %collective-permute-done.6.refs_2_), channel_id=1, source_target_pairs={{0,16},{1,17},{2,18},{3,19},{4,20},{5,21},{6,22},{7,23},{8,24},{9,... | collective-permute-start | bytes 589832 | tf_op jit(solution)/shard_map/ppermute | solution.py:121
  57.5 9.2 %collective-permute-start.10 = (bf16[400,128]{1,0:T(8,128)(2,1)S(1)}, bf16[400,128]{1,0:T(8,128)(2,1)S(1)}, u32[]{:S(2)}, u32[]{:S(2)}) collective-permute-start(bf16[400,128]{1,0:T(8,128)(2,1)S(1)} %copy-done.10), channel_id=1, source_target_pairs={{0,8},{1,9},{2,10},{3,11},{4,12},{5,13},{6,14},{7,15},{8,0},{9,1},... | collective-permute-start | bytes 307208 | tf_op jit(solution)/shard_map/ppermute | solution.py:121
  63.0 5.9 %collective-permute-start.11 = (bf16[400,128]{1,0:T(8,128)(2,1)S(1)}, bf16[400,128]{1,0:T(8,128)(2,1)S(1)}, u32[]{:S(2)}, u32[]{:S(2)}) collective-permute-start(bf16[400,128]{1,0:T(8,128)(2,1)S(1)} %copy-done.9), channel_id=1, source_target_pairs={{0,12},{1,13},{2,14},{3,15},{4,0},{5,1},{6,2},{7,3},{8,4},{9,5},{1... | collective-permute-start | bytes 307208 | tf_op jit(solution)/shard_map/ppermute | solution.py:121
  73.2 6.0 %copy-start.4 = (s32[4]{0:T(128)S(1)}, s32[4]{0:T(128)}, u32[]{:S(2)}) copy-start(s32[4]{0:T(128)} %pad_add_fusion.place) | copy-start | bytes 52
  73.2 6.0 %copy-start.5 = (bf16[3,256,128]{2,1,0:T(8,128)(2,1)S(1)}, bf16[3,256,128]{2,1,0:T(8,128)(2,1)}, u32[]{:S(2)}) copy-start(bf16[3,256,128]{2,1,0:T(8,128)(2,1)} %get-tuple-element.33.refs_0_) | copy-start | bytes 589828
  73.2 27.2 %collective-permute-start.17 = (bf16[4,2,432,384]{3,2,1,0:T(8,128)(2,1)S(1)}, bf16[4,2,432,384]{3,2,1,0:T(8,128)(2,1)S(1)}, u32[]{:S(2)}, u32[]{:S(2)}) collective-permute-start(bf16[4,2,432,384]{3,2,1,0:T(8,128)(2,1)S(1)} %pad_maximum_fusion.refs_7_), channel_id=1, source_target_pairs={{0,1},{1,0},{2,3},{3,2},{4,5},{5,4},{6,7},{7,6},{8,9},{9,8},{10,11... | collective-permute-start | bytes 7962632 | tf_op jit(solution)/shard_map/ppermute | solution.py:121
  78.6 10.7 %collective-permute-start.18 = (bf16[2,1,432,384]{3,2,1,0:T(8,128)(2,1)S(1)}, bf16[2,1,432,384]{3,2,1,0:T(8,128)(2,1)S(1)}, u32[]{:S(2)}, u32[]{:S(2)}) collective-permute-start(bf16[2,1,432,384]{3,2,1,0:T(8,128)(2,1)S(1)} %pad_maximum_fusion.2), channel_id=1, source_target_pairs={{0,2},{1,17},{2,0},{3,19},{4,6},{5,21},{6,4},{7,23},{8,10},{9,25},... | collective-permute-start | bytes 1990664 | tf_op jit(solution)/shard_map/ppermute | solution.py:121
  88.7 4.7 %copy-start.7 = (f32[768]{0:T(1024)S(1)}, f32[768]{0:T(1024)}, u32[]{:S(2)}) copy-start(f32[768]{0:T(1024)} %param.15) | copy-start | bytes 9220
  88.7 4.7 %copy-start.6 = (bf16[400,128]{1,0:T(8,128)(2,1)S(1)}, bf16[400,128]{1,0:T(8,128)(2,1)}, u32[]{:S(2)}) copy-start(bf16[400,128]{1,0:T(8,128)(2,1)} %get-tuple-element.54.refs_8_) | copy-start | bytes 307204
  88.8 11.6 %copy-start = (bf16[192,3072]{1,0:T(8,128)(2,1)S(1)}, bf16[192,3072]{1,0:T(8,128)(2,1)}, u32[]{:S(2)}) copy-start(bf16[192,3072]{1,0:T(8,128)(2,1)} %refs_5_.1) | copy-start | bytes 3538948
  88.8 11.6 %copy-start.1 = (bf16[768,768]{1,0:T(8,128)(2,1)S(1)}, bf16[768,768]{1,0:T(8,128)(2,1)}, u32[]{:S(2)}) copy-start(bf16[768,768]{1,0:T(8,128)(2,1)} %refs_6_.1) | copy-start | bytes 3538948
  88.8 11.6 %copy-start.2 = (bf16[192,768]{1,0:T(8,128)(2,1)S(1)}, bf16[192,768]{1,0:T(8,128)(2,1)}, u32[]{:S(2)}) copy-start(bf16[192,768]{1,0:T(8,128)(2,1)} %refs_4_.1) | copy-start | bytes 884740
  88.8 11.6 %copy-start.3 = (bf16[256,768]{1,0:T(8,128)(2,1)S(1)}, bf16[256,768]{1,0:T(8,128)(2,1)}, u32[]{:S(2)}) copy-start(bf16[256,768]{1,0:T(8,128)(2,1)} %surface.1) | copy-start | bytes 1179652
  89.4 11.0 %collective-permute-start.19 = (bf16[4,1,432,384]{3,2,1,0:T(8,128)(2,1)S(1)}, bf16[4,1,432,384]{3,2,1,0:T(8,128)(2,1)S(1)}, u32[]{:S(2)}, u32[]{:S(2)}) collective-permute-start(bf16[4,1,432,384]{3,2,1,0:T(8,128)(2,1)S(1)} %constant_dynamic-update-slice_fusion.refs_9_), channel_id=1, source_target_pairs={{0,1},{1,0},{2,3},{3,2},{4,5},{5,4},{6,7},{7,6},{8,9},{9,8},{10,11... | collective-permute-start | bytes 3981320 | tf_op jit(solution)/shard_map/ppermute | solution.py:121
  89.5 7.7 %collective-permute-start.16 = (bf16[3,128,128]{2,1,0:T(8,128)(2,1)S(1)}, bf16[3,128,128]{2,1,0:T(8,128)(2,1)S(1)}, u32[]{:S(2)}, u32[]{:S(2)}) collective-permute-start(bf16[3,128,128]{2,1,0:T(8,128)(2,1)S(1)} %attend.7), channel_id=1, source_target_pairs={{0,4},{1,5},{2,6},{3,7},{4,8},{5,9},{6,10},{7,11},{8,12},{9,13},{1... | collective-permute-start | bytes 294920 | tf_op jit(solution)/shard_map/ppermute | solution.py:121
  89.6 10.8 %collective-permute-start.15 = (bf16[3,128,128]{2,1,0:T(8,128)(2,1)S(1)}, bf16[3,128,128]{2,1,0:T(8,128)(2,1)S(1)}, u32[]{:S(2)}, u32[]{:S(2)}) collective-permute-start(bf16[3,128,128]{2,1,0:T(8,128)(2,1)S(1)} %attend.6), channel_id=1, source_target_pairs={{0,8},{1,9},{2,10},{3,11},{4,12},{5,13},{6,14},{7,15},{8,0},{9,1},... | collective-permute-start | bytes 294920 | tf_op jit(solution)/shard_map/ppermute | solution.py:121
  90.8 9.6 %collective-permute-start.14 = (bf16[3,128,128]{2,1,0:T(8,128)(2,1)S(1)}, bf16[3,128,128]{2,1,0:T(8,128)(2,1)S(1)}, u32[]{:S(2)}, u32[]{:S(2)}) collective-permute-start(bf16[3,128,128]{2,1,0:T(8,128)(2,1)S(1)} %attend.5), channel_id=1, source_target_pairs={{0,12},{1,13},{2,14},{3,15},{4,0},{5,1},{6,2},{7,3},{8,4},{9,5},{1... | collective-permute-start | bytes 294920 | tf_op jit(solution)/shard_map/ppermute | solution.py:121

commit v3 on v2

v3 whole, which is shorter than its diff:
```python
import functools
import itertools

import jax
import jax.numpy as jnp
from jax import lax
from jax.experimental import pallas as pl
from jax.experimental.pallas import tpu as pltpu
from jax.sharding import Mesh
from jax.sharding import PartitionSpec as P

HEADS = 12
HD = 64
LIST = 4
MIB = 1024 * 1024
LOG2E = 1.4426950408889634


def passed_along(block, axis, distance):
    devices = range(lax.axis_size(axis))
    route = [((i - distance) % len(devices), i) for i in devices]
    return lax.ppermute(block, axis, route)


def fold_rows(running, left_side, portion):
    return running + jnp.dot(left_side, portion, preferred_element_type=jnp.float32)


def ring_shards(
    queries,
    keys_values,
    surface,
    out_weight,
    up_weight,
    down_weight,
    norm_gain,
    block_lists,
    list_lengths,
):
    row_count, feature_width = queries.shape
    query_blocks = block_lists.shape[0]
    block_rows = row_count // query_blocks
    loop_size = lax.axis_size(("blk", "head"))
    cycle_reach = min(3, (loop_size - 1) // 2)
    own_index = lax.axis_index(("blk", "head"))
    query_heads = queries.reshape(query_blocks, block_rows, HEADS, HD)
    score_scale = 1.0 / HD**0.5
    entry_live = jnp.arange(LIST, dtype=jnp.int32)[None, :] < list_lengths[:, None]
    start_state = (
        jnp.full((query_blocks, HEADS, block_rows), -1e30, jnp.float32),
        jnp.zeros((query_blocks, HEADS, block_rows), jnp.float32),
        jnp.zeros((query_blocks, HEADS, block_rows, HD), jnp.float32),
    )

    def absorb(softmax_state, anchor_pair, source):
        listed = jnp.any((block_lists == source) & entry_live, axis=1)
        running_max, running_sum, running_acc = softmax_state
        block_keys = anchor_pair[0].reshape(block_rows, HEADS, HD)
        block_values = anchor_pair[1].reshape(block_rows, HEADS, HD)
        scores = (
            jnp.einsum(
                "bqhd,khd->bhqk", query_heads, block_keys, preferred_element_type=jnp.float32
            )
            * score_scale
        )
        block_max = jnp.max(scores, axis=3)
        new_max = jnp.where(listed[:, None, None], jnp.maximum(running_max, block_max), running_max)
        ratio = jnp.exp(running_max - new_max)
        weights_exp = jnp.where(
            listed[:, None, None, None], jnp.exp(scores - new_max[..., None]), 0.0
        )
        new_sum = running_sum * ratio + jnp.sum(weights_exp, axis=3)
        probs = weights_exp.astype(jnp.bfloat16)
        new_acc = running_acc * ratio[..., None] + jnp.einsum(
            "bhqk,khd->bhqd", probs, block_values, preferred_element_type=jnp.float32
        )
        return (new_max, new_sum, new_acc)

    moving = passed_along(keys_values, ("blk", "head"), -cycle_reach)
    source = (own_index + cycle_reach) % loop_size
    softmax_state = absorb(start_state, moving, source)
    for cycle_turn in range(2 * cycle_reach):
        moving = passed_along(moving, ("blk", "head"), 1)
        source = (source - 1) % loop_size
        softmax_state = absorb(softmax_state, moving, source)
    final_max, final_sum, final_acc = softmax_state
    context = final_acc / final_sum[..., None]
    context = (
        jnp.transpose(context, (0, 2, 1, 3)).reshape(row_count, feature_width).astype(jnp.bfloat16)
    )
    residual = surface.astype(jnp.float32)
    hidden = fold_rows(residual, context, lax.all_gather(out_weight, "head", axis=0, tiled=True))
    mean_square = jnp.mean(hidden * hidden, axis=1, keepdims=True)
    normed = (hidden * lax.rsqrt(mean_square + 1e-05) * norm_gain[None, :]).astype(jnp.bfloat16)
    up_start = jnp.zeros((row_count, up_weight.shape[1]), jnp.float32)
    pre_gelu = fold_rows(up_start, normed, lax.all_gather(up_weight, "head", axis=0, tiled=True))
    activated = jax.nn.gelu(pre_gelu, approximate=True).astype(jnp.bfloat16)
    mixed_out = fold_rows(
        hidden, activated, lax.all_gather(down_weight, "head", axis=0, tiled=True)
    )
    return mixed_out.astype(jnp.bfloat16)


AXES = ("blk", "head", "side", "core")
SIZES = (2, 4, 2, 2)
DEVICES = list(itertools.product(*(range(size) for size in SIZES)))
ZS = 4
HZ = HEADS // ZS
NOTE = 16
ANY = pl.BlockSpec(memory_space=pl.ANY)
SMEM = pl.BlockSpec(memory_space=pltpu.SMEM)
VMEM = pl.BlockSpec(memory_space=pltpu.VMEM)
HBM = pl.BlockSpec(memory_space=pltpu.HBM)


def flat(x, z, y, c):
    return ((x * SIZES[1] + z) * SIZES[2] + y) * SIZES[3] + c


def sent(value, route):
    return lax.ppermute(value, AXES, [(flat(*d), flat(*route(*d))) for d in DEVICES])


def along_head(distance):
    return lambda x, z, y, c: (x, (z + distance) % ZS, y, c)


def both_ways(x, z, y, c):
    return (x, (z + 1) % ZS, y, c) if c == 0 else (x, (z - 1) % ZS, y, c)


def over_blk(x, z, y, c):
    return (1 - x, z, y, c)


def plane_first(x, z, y, c):
    return (1 - x, z, y, c) if c == 0 else (x, z, 1 - y, c)


def plane_second(x, z, y, c):
    return (x, z, 1 - y, c) if c == 0 else (1 - x, z, y, c)


def other_core(x, z, y, c):
    return (x, z, y, 1 - c)


def after(value, *earlier):
    return lax.optimization_barrier((value,) + earlier)[0]


def pack_kernel(listed_hbm, length_hbm, q_hbm, kv_hbm, out_w, up_w, down_w, *refs):
    kv_slots, q_slots, piece = refs[:ZS], refs[ZS : 2 * ZS], refs[2 * ZS]
    kv_all, q_all, q_ref, kv_ref, listed, length, sems = refs[2 * ZS + 1 :]
    x, z, y = (lax.axis_index(axis) for axis in AXES[:3])
    p = 2 * x + y
    ro, cols = out_w.shape[0] // 4, out_w.shape[1] // 2
    ru, rd = up_w.shape[0], down_w.shape[0] // 8
    rows = [ro, ro + ru, ro + ru + rd]
    copies = [
        pltpu.make_async_copy(kv_hbm, kv_ref, sems.at[0]),
        pltpu.make_async_copy(q_hbm, q_ref, sems.at[1]),
        pltpu.make_async_copy(listed_hbm, listed, sems.at[3]),
        pltpu.make_async_copy(length_hbm, length, sems.at[4]),
    ]
    for e in range(2):
        m = 2 * p + e
        copies.append(
            pltpu.make_async_copy(
                out_w.at[pl.ds(pl.multiple_of(p * ro, 16), ro), pl.ds(e * cols, cols)],
                piece.at[e, pl.ds(0, ro)],
                sems.at[2],
            )
        )
        copies.append(
            pltpu.make_async_copy(
                up_w.at[:, pl.ds(pl.multiple_of(m * cols, 128), cols)],
                piece.at[e, pl.ds(rows[0], ru)],
                sems.at[2],
            )
        )
        for half in range(2):
            copies.append(
                pltpu.make_async_copy(
                    down_w.at[pl.ds(pl.multiple_of(m * rd, 16), rd), pl.ds(half * cols, cols)],
                    piece.at[e, pl.ds(rows[1 + half], rd)],
                    sems.at[2],
                )
            )
    for copy in copies:
        copy.start()
    n = q_ref.shape[0] // 2
    copies[0].wait()
    for pair in range(HEADS // 2):
        lanes = slice(pair * 2 * HD, (pair + 1) * 2 * HD)
        keys, values = kv_ref[0, :, lanes], kv_ref[1, :, lanes]
        even, odd = 2 * pair, 2 * pair + 1
        low = lax.broadcasted_iota(jnp.int32, keys.shape, 1) < HD
        kv_all[even // HZ, even % HZ] = jnp.where(low, keys, pltpu.roll(values, HD, 1))
        kv_all[odd // HZ, odd % HZ] = jnp.where(low, pltpu.roll(keys, HD, 1), values)
    copies[1].wait()
    for pair in range(HEADS // 2):
        lanes = slice(pair * 2 * HD, (pair + 1) * 2 * HD)
        upper, lower = q_ref[:n, lanes], q_ref[n:, lanes]
        even, odd = 2 * pair, 2 * pair + 1
        low = lax.broadcasted_iota(jnp.int32, upper.shape, 1) < HD
        q_all[even // HZ, (even % HZ) * n : (even % HZ + 1) * n] = jnp.where(
            low, upper, pltpu.roll(lower, HD, 1)
        )
        q_all[odd // HZ, (odd % HZ) * n : (odd % HZ + 1) * n] = jnp.where(
            low, pltpu.roll(upper, HD, 1), lower
        )
    copies[2].wait()
    copies[3].wait()
    lane = lax.broadcasted_iota(jnp.int32, (NOTE, 2 * HD), 1)
    note = jnp.where(lane == LIST, length[0], 0)
    for j in range(LIST):
        note = jnp.where(lane == j, listed[0, j], note)
    note = note.astype(jnp.float32).astype(jnp.bfloat16)
    for s in range(ZS):
        there = lax.rem(z + s, ZS)
        kv_slots[s][...] = kv_all[there]
        q_slots[s][: HZ * n] = q_all[there]
        q_slots[s][HZ * n :] = note
    for copy in copies[4:]:
        copy.wait()


def packed(listed, length, queries, keys_values, out_weight, up_weight, down_weight):
    rows, width = queries.shape
    cols = width // 2
    piece_rows = out_weight.shape[0] // 4 + up_weight.shape[0] + down_weight.shape[0] // 4
    kv_shape, q_rows = (HZ, rows, 2 * HD), HZ * rows // 2
    made = lambda shape: jax.ShapeDtypeStruct(shape, jnp.bfloat16)
    outs = pl.pallas_call(
        pack_kernel,
        out_shape=[made(kv_shape)] * ZS + [made((q_rows + NOTE, 2 * HD))] * ZS + [made((2, piece_rows, cols))],
        in_specs=[HBM] * 7,
        out_specs=[VMEM] * (2 * ZS + 1),
        scratch_shapes=[
            pltpu.VMEM((ZS,) + kv_shape, jnp.bfloat16),
            pltpu.VMEM((ZS, q_rows, 2 * HD), jnp.bfloat16),
            pltpu.VMEM(queries.shape, jnp.bfloat16),
            pltpu.VMEM(keys_values.shape, jnp.bfloat16),
            pltpu.SMEM(listed.shape, jnp.int32),
            pltpu.SMEM(length.shape, jnp.int32),
            pltpu.SemaphoreType.DMA((5,)),
        ],
        compiler_params=pltpu.CompilerParams(vmem_limit_bytes=55 * MIB),
        cost_estimate=pl.CostEstimate(flops=0, bytes_accessed=4 * MIB, transcendentals=0),
        name="pack_heads",
    )(listed, length, queries, keys_values, out_weight, up_weight, down_weight)
    return outs[:ZS], outs[ZS : 2 * ZS], outs[2 * ZS]


def attend_kernel(blocks, *refs):
    q_refs, o_refs = refs[: len(refs) // 2], refs[len(refs) // 2 :]
    x, z = (lax.axis_index(axis) for axis in AXES[:2])
    n = o_refs[0].shape[1]
    low = lax.broadcasted_iota(jnp.int32, (n, 2 * HD), 1) < HD
    key_lanes = lax.broadcasted_iota(jnp.int32, (2 * n, 2 * HD), 1) < HD
    scale = LOG2E / HD**0.5
    row = lax.broadcasted_iota(jnp.int32, (NOTE, 2 * HD), 0)
    lane = lax.broadcasted_iota(jnp.int32, (NOTE, 2 * HD), 1)
    digit = jnp.left_shift(1, 3 * jnp.minimum(lane, LIST))
    digit = jnp.where((row == 0) & (lane <= LIST), digit, 0).astype(jnp.float32)
    codes = [
        jnp.sum(q_ref[HZ * n :].astype(jnp.float32) * digit).astype(jnp.int32) for q_ref in q_refs
    ]
    for q_ref, o_ref, code in zip(q_refs, o_refs, codes):
        at = []
        for j in range(LIST):
            block = jnp.bitwise_and(jnp.right_shift(code, 3 * j), 7)
            side, source = block // ZS, lax.rem(block, ZS)
            at.append(jnp.where(side == x, 0, ZS) + lax.rem(z - source + ZS, ZS))
        length = jnp.right_shift(code, 3 * LIST)

        def scored(h, count, q_ref=q_ref, at=at):
            pair = q_ref[h * n : (h + 1) * n]
            none = jnp.zeros_like(pair)
            q = jnp.concatenate(
                [jnp.where(low, pair, none), jnp.where(low, pltpu.roll(pair, HD, 1), none)], axis=0
            )
            scores = [
                lax.dot_general(
                    q, blocks[at[j], h], (((1,), (1,)), ((), ())), preferred_element_type=jnp.float32
                )
                for j in range(count)
            ]
            return scores, jnp.max(functools.reduce(jnp.maximum, scores), axis=1, keepdims=True)

        def summed(h, count, scores, top, o_ref=o_ref, at=at):
            acc = None
            for j in range(count):
                weights = jnp.exp2((scores[j] - top) * scale).astype(jnp.bfloat16)
                values = blocks[at[j], h]
                values = jnp.where(key_lanes, jnp.ones_like(values), values)
                part = jnp.dot(weights, values, preferred_element_type=jnp.float32)
                acc = part if j == 0 else acc + part
            result = acc / pltpu.roll(acc, HD, 1)
            upper, lower = result[:n], result[n:]
            o_ref[h] = jnp.where(low, pltpu.roll(upper, HD, 1), lower).astype(jnp.bfloat16)

        for count in range(1, LIST + 1):

            @pl.when(length == count)
            def _(count=count, scored=scored, summed=summed):
                held = [scored(h, count) for h in range(HZ)]
                for h in range(HZ):
                    summed(h, count, *held[h])


def attended(blocks, queries):
    made = jax.ShapeDtypeStruct((HZ, blocks.shape[2] // 2, 2 * HD), jnp.bfloat16)
    return pl.pallas_call(
        attend_kernel,
        out_shape=[made] * len(queries),
        in_specs=[VMEM] * (1 + len(queries)),
        out_specs=[VMEM] * len(queries),
        compiler_params=pltpu.CompilerParams(vmem_limit_bytes=16 * MIB),
        cost_estimate=pl.CostEstimate(
            flops=5 * 10**8, bytes_accessed=MIB, transcendentals=8 * 10**5
        ),
        name="attend",
    )(blocks, *queries)


def laid(copies, ref, swapped, stage, shapes, into, sems):
    x, z, y, c = (lax.axis_index(axis) for axis in AXES)
    out_all, up_all, down_all = into
    (rs, width), ru, rd = shapes
    cols, ro = width // 2, rs // 4
    rows = [ro, ro + ru, ro + ru + rd]
    core = 1 - c if swapped else c
    first_x, first_y = jnp.where(core == 0, 1 - x, x), jnp.where(core == 0, y, 1 - y)
    second_x, second_y = jnp.where(core == 0, x, 1 - x), jnp.where(core == 0, 1 - y, y)
    mine, far = (x, y), (1 - x, 1 - y)
    first, second = (first_x, first_y), (second_x, second_y)
    near_k = 1 + 2 * core
    if stage == 0:
        pieces = [(near_k, mine, 0), (near_k, mine, 1), (near_k, first, 0), (near_k, first, 1)]
        pieces += [(2, mine, core)]
    elif stage == 1:
        pieces = [(near_k, far, 0), (near_k, far, 1), (near_k, second, 0), (2, first, core)]
    else:
        pieces = [(near_k, second, 1), (2, second, core), (2, far, core)]
    for at, (k, (px, py), half) in enumerate(pieces):
        source = lax.rem(z - k + ZS, ZS)
        slot_row = lax.rem(ZS - k, ZS) * rs
        p = 2 * px + py
        m = 2 * p + half
        piece = ref.at[at]
        copies.append(
            pltpu.make_async_copy(
                piece.at[pl.ds(0, ro)],
                out_all.at[
                    pl.ds(pl.multiple_of(slot_row + p * ro, 16), ro),
                    pl.ds(pl.multiple_of(half * cols, 128), cols),
                ],
                sems.at[0],
            )
        )
        copies.append(
            pltpu.make_async_copy(
                piece.at[pl.ds(rows[0], ru)],
                up_all.at[
                    pl.ds(pl.multiple_of(source * ru, 16), ru),
                    pl.ds(pl.multiple_of(m * cols, 128), cols),
                ],
                sems.at[1],
            )
        )
        for side in range(2):
            copies.append(
                pltpu.make_async_copy(
                    piece.at[pl.ds(rows[1 + side], rd)],
                    down_all.at[
                        pl.ds(pl.multiple_of((source * 8 + m) * rd, 16), rd),
                        pl.ds(side * cols, cols),
                    ],
                    sems.at[2],
                )
            )


def gather_kernel(out_w, up_w, down_w, *refs):
    held, refs = refs[:5], refs[5:]
    out_all, up_all, down_all, sems = refs
    z = lax.axis_index("head")
    rs, ru, rd = out_w.shape[0], up_w.shape[0], down_w.shape[0]
    copies = [
        pltpu.make_async_copy(out_w, out_all.at[pl.ds(0, rs)], sems.at[0]),
        pltpu.make_async_copy(
            up_w, up_all.at[pl.ds(pl.multiple_of(z * ru, 16), ru)], sems.at[1]
        ),
        pltpu.make_async_copy(
            down_w, down_all.at[pl.ds(pl.multiple_of(z * rd, 16), rd)], sems.at[2]
        ),
    ]
    shapes = (out_w.shape, ru, rd // 8)
    for at, ref in enumerate(held):
        laid(copies, ref, at % 2 == 1, at // 2, shapes, refs[:3], sems)
    for copy in copies:
        copy.start()
    for copy in copies:
        copy.wait()


def gathered(out_weight, up_weight, down_weight, *held):
    width, hidden_units = up_weight.shape[0] * ZS, up_weight.shape[1]
    made = lambda *shape: jax.ShapeDtypeStruct(shape, jnp.bfloat16)
    return pl.pallas_call(
        gather_kernel,
        out_shape=[made(width, width), made(width, hidden_units), made(hidden_units, width)],
        in_specs=[ANY] * (3 + len(held)),
        out_specs=[VMEM] * 3,
        scratch_shapes=[pltpu.SemaphoreType.DMA((3,))],
        compiler_params=pltpu.CompilerParams(vmem_limit_bytes=20 * MIB),
        cost_estimate=pl.CostEstimate(flops=0, bytes_accessed=12 * MIB, transcendentals=0),
        name="gather",
    )(out_weight, up_weight, down_weight, *held)


def feed_kernel(gain, surface, *refs):
    ctx_slots, refs = refs[:ZS], refs[ZS + 3 :]
    late_swapped, o_ref, out_all, up_all, down_all, sems = refs
    width, hidden_units = up_all.shape
    copies = []
    shapes = ((width // ZS, width), width // ZS, hidden_units // ZS // 8)
    laid(copies, late_swapped, True, 2, shapes, (out_all, up_all, down_all), sems)
    first = [copies[i] for i in range(len(copies)) if i % 4 == 0]
    second = [copies[i] for i in range(len(copies)) if i % 4 == 1]
    third = [copies[i] for i in range(len(copies)) if i % 4 > 1]
    for copy in first + second + third:
        copy.start()

    tiles = [ctx_slots[s][h] for s in range(ZS) for h in range(HZ)]
    low = lax.broadcasted_iota(jnp.int32, tiles[0].shape, 1) < HD
    upper, lower = [], []
    for left, right in zip(tiles[::2], tiles[1::2]):
        upper.append(jnp.where(low, left, pltpu.roll(right, HD, 1)))
        lower.append(jnp.where(low, pltpu.roll(left, HD, 1), right))
    context = jnp.concatenate(
        [jnp.concatenate(upper, axis=1), jnp.concatenate(lower, axis=1)], axis=0
    )
    for copy in first:
        copy.wait()
    hidden = surface[...].astype(jnp.float32) + jnp.dot(
        context, out_all[...], preferred_element_type=jnp.float32
    )
    mean_square = jnp.mean(hidden * hidden, axis=1, keepdims=True)
    normed = (hidden * lax.rsqrt(mean_square + 1e-05) * gain[...]).astype(jnp.bfloat16)
    for copy in second:
        copy.wait()
    total = hidden
    for step in range(hidden_units // width):
        pre = jnp.dot(
            normed, up_all[:, step * width : (step + 1) * width], preferred_element_type=jnp.float32
        )
        act = jax.nn.gelu(pre, approximate=True).astype(jnp.bfloat16)
        if step == 0:
            for copy in third:
                copy.wait()
        total = total + jnp.dot(
            act, down_all[step * width : (step + 1) * width, :], preferred_element_type=jnp.float32
        )
    o_ref[...] = total.astype(jnp.bfloat16)


def fed(gain, surface, ctx_slots, weights, late_swapped):
    outs = pl.pallas_call(
        feed_kernel,
        out_shape=[jax.ShapeDtypeStruct(v.shape, jnp.bfloat16) for v in (surface, *weights)],
        in_specs=[VMEM, VMEM] + [VMEM] * (ZS + 3) + [ANY],
        out_specs=[VMEM] * 4,
        scratch_shapes=[pltpu.SemaphoreType.DMA((3,))],
        input_output_aliases={2 + ZS: 1, 3 + ZS: 2, 4 + ZS: 3},
        compiler_params=pltpu.CompilerParams(vmem_limit_bytes=30 * MIB),
        cost_estimate=pl.CostEstimate(
            flops=3 * 10**9, bytes_accessed=12 * MIB, transcendentals=10**6
        ),
        name="feed",
    )(gain, surface, *ctx_slots, *weights, late_swapped)
    return outs[0]


def split_shards(
    queries,
    keys_values,
    surface,
    out_weight,
    up_weight,
    down_weight,
    norm_gain,
    block_lists,
    list_lengths,
):
    kv_slots, q_slots, piece = packed(
        block_lists, list_lengths, queries, keys_values, out_weight, up_weight, down_weight
    )
    core = lax.axis_index("core")
    kv_slots, q_slots = list(kv_slots), list(q_slots)
    near, q, far = {0: kv_slots[0]}, {0: q_slots[0]}, {}
    w13 = sent(piece, both_ways)
    far[0] = sent(kv_slots[0], over_blk)
    near[1], near[3] = (sent(kv_slots[s], along_head(s)) for s in (1, 3))
    w13, near[1], near[3], far[0], kv_slots[2] = lax.optimization_barrier(
        (w13, near[1], near[3], far[0], kv_slots[2])
    )
    first13 = sent(w13, plane_first)
    far13 = sent(jnp.stack([near[1], near[3]]), over_blk)
    near[2] = sent(kv_slots[2], along_head(2))
    w2 = sent(lax.dynamic_index_in_dim(w13, core, 0, keepdims=True), both_ways)
    first13, far13, near[2], w2, q_slots[1], q_slots[2], q_slots[3] = lax.optimization_barrier(
        (first13, far13, near[2], w2, q_slots[1], q_slots[2], q_slots[3])
    )
    far[1], far[3] = far13[0], far13[1]
    far[2] = sent(near[2], over_blk)
    away = (2, 1, 3)
    for s in away:
        q[s] = sent(q_slots[s], along_head(s))
    more13 = sent(jnp.concatenate([first13, w13[:1]]), plane_second)
    more2 = sent(lax.dynamic_index_in_dim(first13, core, 0, keepdims=True), both_ways)
    early = jnp.concatenate([w13, first13, w2])
    early_swapped = sent(early, other_core)
    blocks = jnp.stack([near[s] for s in range(ZS)] + [far[s] for s in range(ZS)])
    ctx_slots = dict(zip(away, attended(blocks, [q[s] for s in away])))
    more13, more2 = after(more13, ctx_slots[2], early_swapped), after(more2, ctx_slots[2])
    late = sent(jnp.concatenate([w13[1:], w2, more2]), plane_second)
    for s in away:
        ctx_slots[s] = sent(ctx_slots[s], along_head(-s))
    (ctx_slots[0],) = attended(blocks, [q[0]])
    mid = jnp.concatenate([more13, more2])
    mid_swapped = sent(mid, other_core)
    held = [early, early_swapped, mid, mid_swapped, late]
    late = after(late, ctx_slots[0], ctx_slots[1], ctx_slots[2], ctx_slots[3])
    late_swapped = sent(late, other_core)
    whole = gathered(out_weight, up_weight, down_weight, *held)
    ctx_slots = [ctx_slots[s] for s in range(ZS)]
    return fed(norm_gain[None, :], surface, ctx_slots, whole, late_swapped)


def solution(mesh):
    sizes = (mesh.shape["blk"], mesh.shape["head"], mesh.shape["bend"])
    if sizes == (2, 4, 4):
        mesh = Mesh(mesh.devices.reshape(SIZES), AXES)
        parts, shards = ("side", "core"), split_shards
    else:
        parts, shards = ("bend",), ring_shards
    rows = parts + ("blk", "head")
    return jax.shard_map(
        shards,
        mesh=mesh,
        in_specs=(
            P(rows, None),
            P(None, rows, None),
            P(rows, None),
            P("head", None),
            P("head", None),
            P("head", None),
            P(),
            P(rows, None),
            P(rows),
        ),
        out_specs=P(rows, None),
        check_vma=False,
    )
```

time: 108 us -> 94.9 us (0.88)
  Pallas kernels: 24.4 us -> 14.3 us
  starting transfers between devices: 38.2 us -> 30.9 us
  waiting for transfers between devices: 42.9 us -> 46.3 us
  local copies, waits for them, and re-layouts: 0.31 us -> 1.74 us
    pallas_call x5 -> x4, Pallas kernels: 20.8 us -> 11.4 us  [the longest x1 4.96 us: fed(): pl.pallas_call(feed_kernel, out_shape=[jax.ShapeDtypeStruct(v.shape, jnp....]
    ppermute x20 -> x21, starting transfers between devices: 38.2 us -> 30.9 us  [sent(): lax.ppermute(value, AXES, [(flat(*d), flat(*route(*d))) for d in DEVICES])]
    ppermute x20 -> x21, waiting for transfers between devices: 42.9 us -> 46.3 us  [sent(): lax.ppermute(value, AXES, [(flat(*d), flat(*route(*d))) for d in DEVICES])]
    unnamed x25 -> x28, local copies, waits for them, and re-layouts: 0.13 us -> 1.47 us
  transfers between devices with their start and end apart: 20 -> 21, of which waited for: 8 -> 11; matrix products, arithmetic and copies ran while one was open for 0% -> 2% of each run, Pallas kernels for 12% -> 7%
where the time goes in v3:
time: 94.9 us; the launch traced here: 94.7 us
  waiting for transfers between devices  46.3 us (49%)
  starting transfers between devices  30.9 us (33%)
  Pallas kernels  14.3 us (15%)
  local copies, waits for them, and re-layouts  1.74 us (2%)
  between operations  1.12 us (1%)
    ppermute x21, waiting for transfers between devices, sent(): lax.ppermute(value, AXES, [(flat(*d), flat(*route(*d))) for d in DEVICES])  46.3 us
    ppermute x21, starting transfers between devices, sent(): lax.ppermute(value, AXES, [(flat(*d), flat(*route(*d))) for d in DEVICES])  30.9 us
    pallas_call x1, Pallas kernels, fed(): pl.pallas_call(feed_kernel, out_shape=[jax.ShapeDtypeStruct(v.shape, jnp....  4.96 us
    pallas_call x2, Pallas kernels, attended(): pl.pallas_call(attend_kernel, out_shape=[made] * len(queries), in_specs=[...  4.3 us
    pallas_call x1, Pallas kernels, packed(): pl.pallas_call(pack_kernel, out_shape=[made(kv_shape)] * ZS + [made((q_ro...  2.97 us
    pallas_call x1, Pallas kernels, gathered(): pl.pallas_call(gather_kernel, out_shape=[made(width, width), made(width,...  2.11 us
  transfers between devices with their start and end apart: 21, of which 11 were waited for; matrix products, arithmetic and copies ran while one was open for 2% of the time, Pallas kernels for 7%

profile of v3, /device:TPU:0, one launch (start us, length us, event | category | flops | bytes accessed | tf_op | source)
XLA Modules:
  0.0 94.7 jit_solution(10620138247443554321)
XLA Ops:
  0.7 3.0 %pack_heads.1 = (bf16[3,256,128]{2,1,0:T(8,128)(2,1)}, bf16[3,256,128]{2,1,0:T(8,128)(2,1)}, bf16[3,256,128]{2,1,0:T(8,128)(2,1)}, bf16[3,256,128]{2,1,0:T(8,128...) custom-call(s32[1,4]{1,0:T(1,128)} %listed_hbm.1, ...), custom_call_target="tpu_custom_call" | custom-call | bytes 4194304 | tf_op jit(solution)/shard_map/pack_heads/pallas_call | solution.py:235
  3.6 3.1 %collective-permute-start = (bf16[2,432,384]{2,1,0:T(8,128)(2,1)}, bf16[2,432,384]{2,1,0:T(8,128)(2,1)S(1)}, u32[]{:S(2)}, u32[]{:S(2)}) collective-permute-start(bf16[2,432,384]{2,1,0:T(8,128)(2,1)} %get-tuple-element.37), channel_id=1, source_target_pairs={{0,4},{1,13},{2,6},{3,15},{4,8},{5,1},{6,10},{7,3},{8,12},{9,5},{1... | collective-permute-start | bytes 1990664 | tf_op jit(solution)/shard_map/ppermute | solution.py:121
  6.7 1.6 %collective-permute-start.1 = (bf16[3,256,128]{2,1,0:T(8,128)(2,1)}, bf16[3,256,128]{2,1,0:T(8,128)(2,1)S(1)}, u32[]{:S(2)}, u32[]{:S(2)}) collective-permute-start(bf16[3,256,128]{2,1,0:T(8,128)(2,1)} %get-tuple-element.38), channel_id=1, source_target_pairs={{0,4},{1,5},{2,6},{3,7},{4,8},{5,9},{6,10},{7,11},{8,12},{9,13},{1... | collective-permute-start | bytes 589832 | tf_op jit(solution)/shard_map/ppermute | solution.py:121
  8.3 2.2 %collective-permute-start.2 = (bf16[3,256,128]{2,1,0:T(8,128)(2,1)}, bf16[3,256,128]{2,1,0:T(8,128)(2,1)S(1)}, u32[]{:S(2)}, u32[]{:S(2)}) collective-permute-start(bf16[3,256,128]{2,1,0:T(8,128)(2,1)} %get-tuple-element.39), channel_id=1, source_target_pairs={{0,12},{1,13},{2,14},{3,15},{4,0},{5,1},{6,2},{7,3},{8,4},{9,5},{1... | collective-permute-start | bytes 589832 | tf_op jit(solution)/shard_map/ppermute | solution.py:121
  10.5 1.5 %collective-permute-start.3 = (bf16[3,256,128]{2,1,0:T(8,128)(2,1)}, bf16[3,256,128]{2,1,0:T(8,128)(2,1)S(1)}, u32[]{:S(2)}, u32[]{:S(2)}) collective-permute-start(bf16[3,256,128]{2,1,0:T(8,128)(2,1)} %get-tuple-element.36), channel_id=1, source_target_pairs={{0,16},{1,17},{2,18},{3,19},{4,20},{5,21},{6,22},{7,23},{8,24},{9,... | collective-permute-start | bytes 589832 | tf_op jit(solution)/shard_map/ppermute | solution.py:121
  12.0 1.0 %bitcast_dynamic-update-slice_fusion.3 = bf16[8,3,256,128]{3,2,1,0:T(8,128)(2,1)S(1)} fusion(bf16[3,256,128]{2,1,0:T(8,128)(2,1)} %get-tuple-element.36), kind=kLoop, calls=%fused_computation.6 | loop fusion | bytes 393216
  13.0 15.9 %collective-permute-done.1 = bf16[3,256,128]{2,1,0:T(8,128)(2,1)S(1)} collective-permute-done((bf16[3,256,128]{2,1,0:T(8,128)(2,1)}, bf16[3,256,128]{2,1,0:T(8,128)(2,1)S(1)}, u32[]{:S(2)}, u32[]{:S(2)}) %collective-permute-start.1) | collective-permute-done | bytes 196640 | tf_op jit(solution)/shard_map/ppermute | solution.py:121
  28.9 1.0 %collective-permute-done.2 = bf16[3,256,128]{2,1,0:T(8,128)(2,1)S(1)} collective-permute-done((bf16[3,256,128]{2,1,0:T(8,128)(2,1)}, bf16[3,256,128]{2,1,0:T(8,128)(2,1)S(1)}, u32[]{:S(2)}, u32[]{:S(2)}) %collective-permute-start.2) | collective-permute-done | bytes 196640 | tf_op jit(solution)/shard_map/ppermute | solution.py:121
  29.9 3.1 %collective-permute-start.6 = (bf16[3,256,128]{2,1,0:T(8,128)(2,1)}, bf16[3,256,128]{2,1,0:T(8,128)(2,1)S(1)}, u32[]{:S(2)}, u32[]{:S(2)}) collective-permute-start(bf16[3,256,128]{2,1,0:T(8,128)(2,1)} %get-tuple-element.44), channel_id=1, source_target_pairs={{0,8},{1,9},{2,10},{3,11},{4,12},{5,13},{6,14},{7,15},{8,0},{9,1},... | collective-permute-start | bytes 589832 | tf_op jit(solution)/shard_map/ppermute | solution.py:121
  33.0 1.5 %collective-permute-start.4 = (bf16[2,432,384]{2,1,0:T(8,128)(2,1)S(1)}, bf16[2,432,384]{2,1,0:T(8,128)(2,1)S(1)}, u32[]{:S(2)}, u32[]{:S(2)}) collective-permute-start(bf16[2,432,384]{2,1,0:T(8,128)(2,1)S(1)} %collective-permute-done), channel_id=1, source_target_pairs={{0,16},{1,3},{2,18},{3,1},{4,20},{5,7},{6,22},{7,5},{8,24},{9,11},... | collective-permute-start | bytes 1990664 | tf_op jit(solution)/shard_map/ppermute | solution.py:121
  35.3 1.7 %collective-permute-start.7 = (bf16[1,432,384]{2,1,0:T(8,128)(2,1)S(1)}, bf16[1,432,384]{2,1,0:T(8,128)(2,1)S(1)}, u32[]{:S(2)}, u32[]{:S(2)}) collective-permute-start(bf16[1,432,384]{2,1,0:T(8,128)(2,1)S(1)} %get-tuple-element.69), channel_id=1, source_target_pairs={{0,4},{1,13},{2,6},{3,15},{4,8},{5,1},{6,10},{7,3},{8,12},{9,5},{1... | collective-permute-start | bytes 995336 | tf_op jit(solution)/shard_map/ppermute | solution.py:121
  37.0 8.7 %collective-permute-done.6 = bf16[3,256,128]{2,1,0:T(8,128)(2,1)S(1)} collective-permute-done((bf16[3,256,128]{2,1,0:T(8,128)(2,1)}, bf16[3,256,128]{2,1,0:T(8,128)(2,1)S(1)}, u32[]{:S(2)}, u32[]{:S(2)}) %collective-permute-start.6) | collective-permute-done | bytes 196640 | tf_op jit(solution)/shard_map/ppermute | solution.py:121
  45.7 1.5 %collective-permute-done.7 = bf16[1,432,384]{2,1,0:T(8,128)(2,1)S(1)} collective-permute-done((bf16[1,432,384]{2,1,0:T(8,128)(2,1)S(1)}, bf16[1,432,384]{2,1,0:T(8,128)(2,1)S(1)}, u32[]{:S(2)}, u32[]{:S(2)}) %collective-permute-start.7) | collective-permute-done | bytes 331808 | tf_op jit(solution)/shard_map/ppermute | solution.py:121
  47.3 4.2 %collective-permute-done.5 = bf16[2,3,256,128]{3,2,1,0:T(8,128)(2,1)S(1)} collective-permute-done((bf16[2,3,256,128]{3,2,1,0:T(8,128)(2,1)S(1)}, bf16[2,3,256,128]{3,2,1,0:T(8,128)(2,1)S(1)}, u32[]{:S(2)}, u32[]{:S(2)}) %collective-permute-start.5) | collective-permute-done | bytes 393248 | tf_op jit(solution)/shard_map/ppermute | solution.py:121
  51.5 0.7 collective-permute-start.9
  52.2 1.6 %collective-permute-start.10 = (bf16[400,128]{1,0:T(8,128)(2,1)S(1)}, bf16[400,128]{1,0:T(8,128)(2,1)S(1)}, u32[]{:S(2)}, u32[]{:S(2)}) collective-permute-start(bf16[400,128]{1,0:T(8,128)(2,1)S(1)} %copy-done.7), channel_id=1, source_target_pairs={{0,4},{1,5},{2,6},{3,7},{4,8},{5,9},{6,10},{7,11},{8,12},{9,13},{1... | collective-permute-start | bytes 307208 | tf_op jit(solution)/shard_map/ppermute | solution.py:121
  53.8 1.5 %collective-permute-start.8 = (bf16[3,256,128]{2,1,0:T(8,128)(2,1)S(1)}, bf16[3,256,128]{2,1,0:T(8,128)(2,1)S(1)}, u32[]{:S(2)}, u32[]{:S(2)}) collective-permute-start(bf16[3,256,128]{2,1,0:T(8,128)(2,1)S(1)} %collective-permute-done.6), channel_id=1, source_target_pairs={{0,16},{1,17},{2,18},{3,19},{4,20},{5,21},{6,22},{7,23},{8,24},{9,... | collective-permute-start | bytes 589832 | tf_op jit(solution)/shard_map/ppermute | solution.py:121
  55.3 1.2 %collective-permute-start.17 = (bf16[1,432,384]{2,1,0:T(8,128)(2,1)S(1)}, bf16[1,432,384]{2,1,0:T(8,128)(2,1)S(1)}, u32[]{:S(2)}, u32[]{:S(2)}) collective-permute-start(bf16[1,432,384]{2,1,0:T(8,128)(2,1)S(1)} %constant_dynamic-slice_fusion), channel_id=1, source_target_pairs={{0,4},{1,13},{2,6},{3,15},{4,8},{5,1},{6,10},{7,3},{8,12},{9,5},{1... | collective-permute-start | bytes 995336 | tf_op jit(solution)/shard_map/ppermute | solution.py:121
  57.1 2.4 %collective-permute-done.8 = bf16[3,256,128]{2,1,0:T(8,128)(2,1)S(1)} collective-permute-done((bf16[3,256,128]{2,1,0:T(8,128)(2,1)S(1)}, bf16[3,256,128]{2,1,0:T(8,128)(2,1)S(1)}, u32[]{:S(2)}, u32[]{:S(2)}) %collective-permute-start.8) | collective-permute-done | bytes 196640 | tf_op jit(solution)/shard_map/ppermute | solution.py:121
  59.5 1.7 %collective-permute-start.16 = (bf16[3,432,384]{2,1,0:T(8,128)(2,1)S(1)}, bf16[3,432,384]{2,1,0:T(8,128)(2,1)S(1)}, u32[]{:S(2)}, u32[]{:S(2)}) collective-permute-start(bf16[3,432,384]{2,1,0:T(8,128)(2,1)S(1)} %pad_maximum_fusion), channel_id=1, source_target_pairs={{0,2},{1,17},{2,0},{3,19},{4,6},{5,21},{6,4},{7,23},{8,10},{9,25},... | collective-permute-start | bytes 2985992 | tf_op jit(solution)/shard_map/ppermute | solution.py:121
  61.2 1.9 %collective-permute-start.11 = (bf16[400,128]{1,0:T(8,128)(2,1)S(1)}, bf16[400,128]{1,0:T(8,128)(2,1)S(1)}, u32[]{:S(2)}, u32[]{:S(2)}) collective-permute-start(bf16[400,128]{1,0:T(8,128)(2,1)S(1)} %copy-done.6), channel_id=1, source_target_pairs={{0,12},{1,13},{2,14},{3,15},{4,0},{5,1},{6,2},{7,3},{8,4},{9,5},{1... | collective-permute-start | bytes 307208 | tf_op jit(solution)/shard_map/ppermute | solution.py:121
  63.2 4.9 %collective-permute-done.11.refs_2_ = bf16[400,128]{1,0:T(8,128)(2,1)S(1)} collective-permute-done((bf16[400,128]{1,0:T(8,128)(2,1)S(1)}, bf16[400,128]{1,0:T(8,128)(2,1)S(1)}, u32[]{:S(2)}, u32[]{:S(2)}) %collective-permute-start.11) | collective-permute-done | bytes 102432 | tf_op jit(solution)/shard_map/ppermute | solution.py:121
  68.1 2.8 %attend.3 = (bf16[3,128,128]{2,1,0:T(8,128)(2,1)S(1)}, bf16[3,128,128]{2,1,0:T(8,128)(2,1)S(1)}, bf16[3,128,128]{2,1,0:T(8,128)(2,1)S(1)}) custom-call(bf16[8,3,256,128]{3,2,1,0:T(8,128)(2,1)S(1)} %slice_dynamic-update-slice_fusion.blocks, bf16[400,128]{1,0:T(8,128)(2,1)S(1)} %collective-permute-done.9.refs_0_, ...), custom_call_target="tpu_custom_call" | custom-call | flops 500000000 | bytes 1048576 | tf_op jit(solution)/shard_map/attend/pallas_call | solution.py:315
  71.1 1.5 %collective-permute-start.19 = (bf16[3,432,384]{2,1,0:T(8,128)(2,1)S(1)}, bf16[3,432,384]{2,1,0:T(8,128)(2,1)S(1)}, u32[]{:S(2)}, u32[]{:S(2)}) collective-permute-start(bf16[3,432,384]{2,1,0:T(8,128)(2,1)S(1)} %pad_maximum_fusion.1), channel_id=1, source_target_pairs={{0,2},{1,17},{2,0},{3,19},{4,6},{5,21},{6,4},{7,23},{8,10},{9,25},... | collective-permute-start | bytes 2985992 | tf_op jit(solution)/shard_map/ppermute | solution.py:121
  72.6 1.1 %collective-permute-done.16 = bf16[3,432,384]{2,1,0:T(8,128)(2,1)S(1)} collective-permute-done((bf16[3,432,384]{2,1,0:T(8,128)(2,1)S(1)}, bf16[3,432,384]{2,1,0:T(8,128)(2,1)S(1)}, u32[]{:S(2)}, u32[]{:S(2)}) %collective-permute-start.16) | collective-permute-done | bytes 995360 | tf_op jit(solution)/shard_map/ppermute | solution.py:121
  74.0 2.3 %collective-permute-start.12 = (bf16[3,128,128]{2,1,0:T(8,128)(2,1)S(1)}, bf16[3,128,128]{2,1,0:T(8,128)(2,1)S(1)}, u32[]{:S(2)}, u32[]{:S(2)}) collective-permute-start(bf16[3,128,128]{2,1,0:T(8,128)(2,1)S(1)} %get-tuple-element.55), channel_id=1, source_target_pairs={{0,12},{1,13},{2,14},{3,15},{4,0},{5,1},{6,2},{7,3},{8,4},{9,5},{1... | collective-permute-start | bytes 294920 | tf_op jit(solution)/shard_map/ppermute | solution.py:121
  76.3 3.0 %collective-permute-start.13 = (bf16[3,128,128]{2,1,0:T(8,128)(2,1)S(1)}, bf16[3,128,128]{2,1,0:T(8,128)(2,1)S(1)}, u32[]{:S(2)}, u32[]{:S(2)}) collective-permute-start(bf16[3,128,128]{2,1,0:T(8,128)(2,1)S(1)} %get-tuple-element.56), channel_id=1, source_target_pairs={{0,8},{1,9},{2,10},{3,11},{4,12},{5,13},{6,14},{7,15},{8,0},{9,1},... | collective-permute-start | bytes 294920 | tf_op jit(solution)/shard_map/ppermute | solution.py:121
  79.3 1.5 %attend.2.refs_0_ = bf16[3,128,128]{2,1,0:T(8,128)(2,1)S(1)} custom-call(bf16[8,3,256,128]{3,2,1,0:T(8,128)(2,1)S(1)} %slice_dynamic-update-slice_fusion.blocks, bf16[400,128]{1,0:T(8,128)(2,1)S(1)} %copy-done.4), custom_call_target="tpu_custom_call" | custom-call | flops 500000000 | bytes 1048576 | tf_op jit(solution)/shard_map/attend/pallas_call | solution.py:315
  80.8 3.7 %collective-permute-done.14.refs_3_ = bf16[3,128,128]{2,1,0:T(8,128)(2,1)S(1)} collective-permute-done((bf16[3,128,128]{2,1,0:T(8,128)(2,1)S(1)}, bf16[3,128,128]{2,1,0:T(8,128)(2,1)S(1)}, u32[]{:S(2)}, u32[]{:S(2)}) %collective-permute-start.14) | collective-permute-done | bytes 98336 | tf_op jit(solution)/shard_map/ppermute | solution.py:121
  84.5 2.5 %collective-permute-done.13.refs_2_ = bf16[3,128,128]{2,1,0:T(8,128)(2,1)S(1)} collective-permute-done((bf16[3,128,128]{2,1,0:T(8,128)(2,1)S(1)}, bf16[3,128,128]{2,1,0:T(8,128)(2,1)S(1)}, u32[]{:S(2)}, u32[]{:S(2)}) %collective-permute-start.13) | collective-permute-done | bytes 98336 | tf_op jit(solution)/shard_map/ppermute | solution.py:121
  87.1 2.1 %gather.1 = (bf16[768,768]{1,0:T(8,128)(2,1)S(1)}, bf16[768,3072]{1,0:T(8,128)(2,1)S(1)}, bf16[3072,768]{1,0:T(8,128)(2,1)S(1)}) custom-call(bf16[192,768]{1,0:T(8,128)(2,1)S(1)} %copy-done.2, bf16[192,3072]{1,0:T(8,128)(2,1)S(1)} %copy-done, bf16[768,768]{1,0:T(8,128)(2,1)S(1)} %copy-done.1, ...), custom_call_target="tpu_custom_call" | custom-call | bytes 12582912 | tf_op jit(solution)/shard_map/gather/pallas_call | solution.py:412
  89.6 5.0 %feed.1 = (bf16[256,768]{1,0:T(8,128)(2,1)}, bf16[768,768]{1,0:T(8,128)(2,1)S(1)}, bf16[768,3072]{1,0:T(8,128)(2,1)S(1)}, bf16[3072,768]{1,0:T(8,128)(2,1)S(1)}) custom-call(f32[1,768]{1,0:T(1,128)S(1)} %broadcast_in_dim.3.gain, bf16[256,768]{1,0:T(8,128)(2,1)S(1)} %copy-done.3, ...), custom_call_target="tpu_custom_call", output_to_operand_aliasing={{1}: (6, {}), {2}: (7, {}), {3}: (8, {})} | custom-call | flops 3000000000 | bytes 12582912 | tf_op jit(solution)/shard_map/feed/pallas_call | solution.py:471
  (52 shorter events, 2.2 us)
Async XLA Ops:
  3.6 26.2 %collective-permute-start = (bf16[2,432,384]{2,1,0:T(8,128)(2,1)}, bf16[2,432,384]{2,1,0:T(8,128)(2,1)S(1)}, u32[]{:S(2)}, u32[]{:S(2)}) collective-permute-start(bf16[2,432,384]{2,1,0:T(8,128)(2,1)} %get-tuple-element.37), channel_id=1, source_target_pairs={{0,4},{1,13},{2,6},{3,15},{4,8},{5,1},{6,10},{7,3},{8,12},{9,5},{1... | collective-permute-start | bytes 1990664 | tf_op jit(solution)/shard_map/ppermute | solution.py:121
  6.7 22.2 %collective-permute-start.1 = (bf16[3,256,128]{2,1,0:T(8,128)(2,1)}, bf16[3,256,128]{2,1,0:T(8,128)(2,1)S(1)}, u32[]{:S(2)}, u32[]{:S(2)}) collective-permute-start(bf16[3,256,128]{2,1,0:T(8,128)(2,1)} %get-tuple-element.38), channel_id=1, source_target_pairs={{0,4},{1,5},{2,6},{3,7},{4,8},{5,9},{6,10},{7,11},{8,12},{9,13},{1... | collective-permute-start | bytes 589832 | tf_op jit(solution)/shard_map/ppermute | solution.py:121
  8.3 21.6 %collective-permute-start.2 = (bf16[3,256,128]{2,1,0:T(8,128)(2,1)}, bf16[3,256,128]{2,1,0:T(8,128)(2,1)S(1)}, u32[]{:S(2)}, u32[]{:S(2)}) collective-permute-start(bf16[3,256,128]{2,1,0:T(8,128)(2,1)} %get-tuple-element.39), channel_id=1, source_target_pairs={{0,12},{1,13},{2,14},{3,15},{4,0},{5,1},{6,2},{7,3},{8,4},{9,5},{1... | collective-permute-start | bytes 589832 | tf_op jit(solution)/shard_map/ppermute | solution.py:121
  10.5 19.3 %collective-permute-start.3 = (bf16[3,256,128]{2,1,0:T(8,128)(2,1)}, bf16[3,256,128]{2,1,0:T(8,128)(2,1)S(1)}, u32[]{:S(2)}, u32[]{:S(2)}) collective-permute-start(bf16[3,256,128]{2,1,0:T(8,128)(2,1)} %get-tuple-element.36), channel_id=1, source_target_pairs={{0,16},{1,17},{2,18},{3,19},{4,20},{5,21},{6,22},{7,23},{8,24},{9,... | collective-permute-start | bytes 589832 | tf_op jit(solution)/shard_map/ppermute | solution.py:121
  29.9 15.8 %collective-permute-start.6 = (bf16[3,256,128]{2,1,0:T(8,128)(2,1)}, bf16[3,256,128]{2,1,0:T(8,128)(2,1)S(1)}, u32[]{:S(2)}, u32[]{:S(2)}) collective-permute-start(bf16[3,256,128]{2,1,0:T(8,128)(2,1)} %get-tuple-element.44), channel_id=1, source_target_pairs={{0,8},{1,9},{2,10},{3,11},{4,12},{5,13},{6,14},{7,15},{8,0},{9,1},... | collective-permute-start | bytes 589832 | tf_op jit(solution)/shard_map/ppermute | solution.py:121
  33.0 18.4 %collective-permute-start.4 = (bf16[2,432,384]{2,1,0:T(8,128)(2,1)S(1)}, bf16[2,432,384]{2,1,0:T(8,128)(2,1)S(1)}, u32[]{:S(2)}, u32[]{:S(2)}) collective-permute-start(bf16[2,432,384]{2,1,0:T(8,128)(2,1)S(1)} %collective-permute-done), channel_id=1, source_target_pairs={{0,16},{1,3},{2,18},{3,1},{4,20},{5,7},{6,22},{7,5},{8,24},{9,11},... | collective-permute-start | bytes 1990664 | tf_op jit(solution)/shard_map/ppermute | solution.py:121
  34.5 16.9 %copy-start.8 = (bf16[400,128]{1,0:T(8,128)(2,1)S(1)}, bf16[400,128]{1,0:T(8,128)(2,1)}, u32[]{:S(2)}) copy-start(bf16[400,128]{1,0:T(8,128)(2,1)} %get-tuple-element.52) | copy-start | bytes 307204
  34.6 17.6 %copy-start.7 = (bf16[400,128]{1,0:T(8,128)(2,1)S(1)}, bf16[400,128]{1,0:T(8,128)(2,1)}, u32[]{:S(2)}) copy-start(bf16[400,128]{1,0:T(8,128)(2,1)} %get-tuple-element.53) | copy-start | bytes 307204
  34.6 16.9 %collective-permute-start.5 = (bf16[2,3,256,128]{3,2,1,0:T(8,128)(2,1)S(1)}, bf16[2,3,256,128]{3,2,1,0:T(8,128)(2,1)S(1)}, u32[]{:S(2)}, u32[]{:S(2)}) collective-permute-start(bf16[2,3,256,128]{3,2,1,0:T(8,128)(2,1)S(1)} %pad_maximum_fusion.2), channel_id=1, source_target_pairs={{0,16},{1,17},{2,18},{3,19},{4,20},{5,21},{6,22},{7,23},{8,24},{9,... | collective-permute-start | bytes 1179656 | tf_op jit(solution)/shard_map/ppermute | solution.py:121
  35.3 12.0 %collective-permute-start.7 = (bf16[1,432,384]{2,1,0:T(8,128)(2,1)S(1)}, bf16[1,432,384]{2,1,0:T(8,128)(2,1)S(1)}, u32[]{:S(2)}, u32[]{:S(2)}) collective-permute-start(bf16[1,432,384]{2,1,0:T(8,128)(2,1)S(1)} %get-tuple-element.69), channel_id=1, source_target_pairs={{0,4},{1,13},{2,6},{3,15},{4,8},{5,1},{6,10},{7,3},{8,12},{9,5},{1... | collective-permute-start | bytes 995336 | tf_op jit(solution)/shard_map/ppermute | solution.py:121
  51.5 9.8 %collective-permute-start.9 = (bf16[400,128]{1,0:T(8,128)(2,1)S(1)}, bf16[400,128]{1,0:T(8,128)(2,1)S(1)}, u32[]{:S(2)}, u32[]{:S(2)}) collective-permute-start(bf16[400,128]{1,0:T(8,128)(2,1)S(1)} %copy-done.8), channel_id=1, source_target_pairs={{0,8},{1,9},{2,10},{3,11},{4,12},{5,13},{6,14},{7,15},{8,0},{9,1},... | collective-permute-start | bytes 307208 | tf_op jit(solution)/shard_map/ppermute | solution.py:121
  52.2 11.0 %collective-permute-start.10 = (bf16[400,128]{1,0:T(8,128)(2,1)S(1)}, bf16[400,128]{1,0:T(8,128)(2,1)S(1)}, u32[]{:S(2)}, u32[]{:S(2)}) collective-permute-start(bf16[400,128]{1,0:T(8,128)(2,1)S(1)} %copy-done.7), channel_id=1, source_target_pairs={{0,4},{1,5},{2,6},{3,7},{4,8},{5,9},{6,10},{7,11},{8,12},{9,13},{1... | collective-permute-start | bytes 307208 | tf_op jit(solution)/shard_map/ppermute | solution.py:121
  53.8 5.7 %collective-permute-start.8 = (bf16[3,256,128]{2,1,0:T(8,128)(2,1)S(1)}, bf16[3,256,128]{2,1,0:T(8,128)(2,1)S(1)}, u32[]{:S(2)}, u32[]{:S(2)}) collective-permute-start(bf16[3,256,128]{2,1,0:T(8,128)(2,1)S(1)} %collective-permute-done.6), channel_id=1, source_target_pairs={{0,16},{1,17},{2,18},{3,19},{4,20},{5,21},{6,22},{7,23},{8,24},{9,... | collective-permute-start | bytes 589832 | tf_op jit(solution)/shard_map/ppermute | solution.py:121
  55.3 15.6 %collective-permute-start.17 = (bf16[1,432,384]{2,1,0:T(8,128)(2,1)S(1)}, bf16[1,432,384]{2,1,0:T(8,128)(2,1)S(1)}, u32[]{:S(2)}, u32[]{:S(2)}) collective-permute-start(bf16[1,432,384]{2,1,0:T(8,128)(2,1)S(1)} %constant_dynamic-slice_fusion), channel_id=1, source_target_pairs={{0,4},{1,13},{2,6},{3,15},{4,8},{5,1},{6,10},{7,3},{8,12},{9,5},{1... | collective-permute-start | bytes 995336 | tf_op jit(solution)/shard_map/ppermute | solution.py:121
  56.8 16.9 %collective-permute-start.15 = (bf16[5,432,384]{2,1,0:T(8,128)(2,1)S(1)}, bf16[5,432,384]{2,1,0:T(8,128)(2,1)S(1)}, u32[]{:S(2)}, u32[]{:S(2)}) collective-permute-start(bf16[5,432,384]{2,1,0:T(8,128)(2,1)S(1)} %constant_dynamic-update-slice_fusion.2.refs_0_), channel_id=1, source_target_pairs={{0,1},{1,0},{2,3},{3,2},{4,5},{5,4},{6,7},{7,6},{8,9},{9,8},{10,11... | collective-permute-start | bytes 4976648 | tf_op jit(solution)/shard_map/ppermute | solution.py:121
  56.9 4.4 %copy-start.6 = (bf16[400,128]{1,0:T(8,128)(2,1)S(1)}, bf16[400,128]{1,0:T(8,128)(2,1)}, u32[]{:S(2)}) copy-start(bf16[400,128]{1,0:T(8,128)(2,1)} %get-tuple-element.54) | copy-start | bytes 307204
  59.5 14.2 %collective-permute-start.16 = (bf16[3,432,384]{2,1,0:T(8,128)(2,1)S(1)}, bf16[3,432,384]{2,1,0:T(8,128)(2,1)S(1)}, u32[]{:S(2)}, u32[]{:S(2)}) collective-permute-start(bf16[3,432,384]{2,1,0:T(8,128)(2,1)S(1)} %pad_maximum_fusion), channel_id=1, source_target_pairs={{0,2},{1,17},{2,0},{3,19},{4,6},{5,21},{6,4},{7,23},{8,10},{9,25},... | collective-permute-start | bytes 2985992 | tf_op jit(solution)/shard_map/ppermute | solution.py:121
  61.2 6.8 %collective-permute-start.11 = (bf16[400,128]{1,0:T(8,128)(2,1)S(1)}, bf16[400,128]{1,0:T(8,128)(2,1)S(1)}, u32[]{:S(2)}, u32[]{:S(2)}) collective-permute-start(bf16[400,128]{1,0:T(8,128)(2,1)S(1)} %copy-done.6), channel_id=1, source_target_pairs={{0,12},{1,13},{2,14},{3,15},{4,0},{5,1},{6,2},{7,3},{8,4},{9,5},{1... | collective-permute-start | bytes 307208 | tf_op jit(solution)/shard_map/ppermute | solution.py:121
  71.1 8.2 %copy-start.4 = (bf16[400,128]{1,0:T(8,128)(2,1)S(1)}, bf16[400,128]{1,0:T(8,128)(2,1)}, u32[]{:S(2)}) copy-start(bf16[400,128]{1,0:T(8,128)(2,1)} %get-tuple-element.51.refs_0_) | copy-start | bytes 307204
  71.1 15.9 %collective-permute-start.19 = (bf16[3,432,384]{2,1,0:T(8,128)(2,1)S(1)}, bf16[3,432,384]{2,1,0:T(8,128)(2,1)S(1)}, u32[]{:S(2)}, u32[]{:S(2)}) collective-permute-start(bf16[3,432,384]{2,1,0:T(8,128)(2,1)S(1)} %pad_maximum_fusion.1), channel_id=1, source_target_pairs={{0,2},{1,17},{2,0},{3,19},{4,6},{5,21},{6,4},{7,23},{8,10},{9,25},... | collective-permute-start | bytes 2985992 | tf_op jit(solution)/shard_map/ppermute | solution.py:121
  73.7 13.3 %copy-start.2 = (bf16[192,768]{1,0:T(8,128)(2,1)S(1)}, bf16[192,768]{1,0:T(8,128)(2,1)}, u32[]{:S(2)}) copy-start(bf16[192,768]{1,0:T(8,128)(2,1)} %out_w.3) | copy-start | bytes 884740
  73.8 13.2 %copy-start.5 = (f32[768]{0:T(1024)S(1)}, f32[768]{0:T(1024)}, u32[]{:S(2)}) copy-start(f32[768]{0:T(1024)} %param.15) | copy-start | bytes 9220
  73.8 13.2 %copy-start = (bf16[192,3072]{1,0:T(8,128)(2,1)S(1)}, bf16[192,3072]{1,0:T(8,128)(2,1)}, u32[]{:S(2)}) copy-start(bf16[192,3072]{1,0:T(8,128)(2,1)} %up_w.3) | copy-start | bytes 3538948
  73.8 13.2 %copy-start.1 = (bf16[768,768]{1,0:T(8,128)(2,1)S(1)}, bf16[768,768]{1,0:T(8,128)(2,1)}, u32[]{:S(2)}) copy-start(bf16[768,768]{1,0:T(8,128)(2,1)} %down_w.3) | copy-start | bytes 3538948
  73.9 13.1 %collective-permute-start.18 = (bf16[4,432,384]{2,1,0:T(8,128)(2,1)S(1)}, bf16[4,432,384]{2,1,0:T(8,128)(2,1)S(1)}, u32[]{:S(2)}, u32[]{:S(2)}) collective-permute-start(bf16[4,432,384]{2,1,0:T(8,128)(2,1)S(1)} %constant_dynamic-update-slice_fusion.5.refs_2_), channel_id=1, source_target_pairs={{0,1},{1,0},{2,3},{3,2},{4,5},{5,4},{6,7},{7,6},{8,9},{9,8},{10,11... | collective-permute-start | bytes 3981320 | tf_op jit(solution)/shard_map/ppermute | solution.py:121
  74.0 6.8 %collective-permute-start.12 = (bf16[3,128,128]{2,1,0:T(8,128)(2,1)S(1)}, bf16[3,128,128]{2,1,0:T(8,128)(2,1)S(1)}, u32[]{:S(2)}, u32[]{:S(2)}) collective-permute-start(bf16[3,128,128]{2,1,0:T(8,128)(2,1)S(1)} %get-tuple-element.55), channel_id=1, source_target_pairs={{0,12},{1,13},{2,14},{3,15},{4,0},{5,1},{6,2},{7,3},{8,4},{9,5},{1... | collective-permute-start | bytes 294920 | tf_op jit(solution)/shard_map/ppermute | solution.py:121
  76.3 8.2 %collective-permute-start.14 = (bf16[3,128,128]{2,1,0:T(8,128)(2,1)S(1)}, bf16[3,128,128]{2,1,0:T(8,128)(2,1)S(1)}, u32[]{:S(2)}, u32[]{:S(2)}) collective-permute-start(bf16[3,128,128]{2,1,0:T(8,128)(2,1)S(1)} %get-tuple-element.57), channel_id=1, source_target_pairs={{0,4},{1,5},{2,6},{3,7},{4,8},{5,9},{6,10},{7,11},{8,12},{9,13},{1... | collective-permute-start | bytes 294920 | tf_op jit(solution)/shard_map/ppermute | solution.py:121
  76.3 10.7 %collective-permute-start.13 = (bf16[3,128,128]{2,1,0:T(8,128)(2,1)S(1)}, bf16[3,128,128]{2,1,0:T(8,128)(2,1)S(1)}, u32[]{:S(2)}, u32[]{:S(2)}) collective-permute-start(bf16[3,128,128]{2,1,0:T(8,128)(2,1)S(1)} %get-tuple-element.56), channel_id=1, source_target_pairs={{0,8},{1,9},{2,10},{3,11},{4,12},{5,13},{6,14},{7,15},{8,0},{9,1},... | collective-permute-start | bytes 294920 | tf_op jit(solution)/shard_map/ppermute | solution.py:121
  87.0 2.6 %collective-permute-start.20 = (bf16[3,432,384]{2,1,0:T(8,128)(2,1)S(1)}, bf16[3,432,384]{2,1,0:T(8,128)(2,1)S(1)}, u32[]{:S(2)}, u32[]{:S(2)}) collective-permute-start(bf16[3,432,384]{2,1,0:T(8,128)(2,1)S(1)} %collective-permute-done.19.refs_4_), channel_id=1, source_target_pairs={{0,1},{1,0},{2,3},{3,2},{4,5},{5,4},{6,7},{7,6},{8,9},{9,8},{10,11... | collective-permute-start | bytes 2985992 | tf_op jit(solution)/shard_map/ppermute | solution.py:121
  87.0 2.6 %copy-start.3 = (bf16[256,768]{1,0:T(8,128)(2,1)S(1)}, bf16[256,768]{1,0:T(8,128)(2,1)}, u32[]{:S(2)}) copy-start(bf16[256,768]{1,0:T(8,128)(2,1)} %surface.1) | copy-start | bytes 1179652

commit v4 on v3

--- a/solution.py
+++ b/solution.py
@@ -121,12 +121,8 @@
     return lax.ppermute(value, AXES, [(flat(*d), flat(*route(*d))) for d in DEVICES])
 
 
-def along_head(distance):
-    return lambda x, z, y, c: (x, (z + distance) % ZS, y, c)
-
-
-def both_ways(x, z, y, c):
-    return (x, (z + 1) % ZS, y, c) if c == 0 else (x, (z - 1) % ZS, y, c)
+def across_head(slot):
+    return lambda x, z, y, c: (x, z ^ slot, y, c)
 
 
 def over_blk(x, z, y, c):
@@ -152,8 +148,9 @@
 def pack_kernel(listed_hbm, length_hbm, q_hbm, kv_hbm, out_w, up_w, down_w, *refs):
     kv_slots, q_slots, piece = refs[:ZS], refs[ZS : 2 * ZS], refs[2 * ZS]
     kv_all, q_all, q_ref, kv_ref, listed, length, sems = refs[2 * ZS + 1 :]
-    x, z, y = (lax.axis_index(axis) for axis in AXES[:3])
+    x, z, y, c = (lax.axis_index(axis) for axis in AXES)
     p = 2 * x + y
+    m = 2 * p + c
     ro, cols = out_w.shape[0] // 4, out_w.shape[1] // 2
     ru, rd = up_w.shape[0], down_w.shape[0] // 8
     rows = [ro, ro + ru, ro + ru + rd]
@@ -163,30 +160,26 @@
         pltpu.make_async_copy(listed_hbm, listed, sems.at[3]),
         pltpu.make_async_copy(length_hbm, length, sems.at[4]),
     ]
-    for e in range(2):
-        m = 2 * p + e
+    copies += [
+        pltpu.make_async_copy(
+            out_w.at[pl.ds(pl.multiple_of(p * ro, 16), ro), pl.ds(pl.multiple_of(c * cols, 128), cols)],
+            piece.at[0, pl.ds(0, ro)],
+            sems.at[2],
+        ),
+        pltpu.make_async_copy(
+            up_w.at[:, pl.ds(pl.multiple_of(m * cols, 128), cols)],
+            piece.at[0, pl.ds(rows[0], ru)],
+            sems.at[2],
+        ),
+    ]
+    for side in range(2):
         copies.append(
             pltpu.make_async_copy(
-                out_w.at[pl.ds(pl.multiple_of(p * ro, 16), ro), pl.ds(e * cols, cols)],
-                piece.at[e, pl.ds(0, ro)],
+                down_w.at[pl.ds(pl.multiple_of(m * rd, 16), rd), pl.ds(side * cols, cols)],
+                piece.at[0, pl.ds(rows[1 + side], rd)],
                 sems.at[2],
             )
         )
-        copies.append(
-            pltpu.make_async_copy(
-                up_w.at[:, pl.ds(pl.multiple_of(m * cols, 128), cols)],
-                piece.at[e, pl.ds(rows[0], ru)],
-                sems.at[2],
-            )
-        )
-        for half in range(2):
-            copies.append(
-                pltpu.make_async_copy(
-                    down_w.at[pl.ds(pl.multiple_of(m * rd, 16), rd), pl.ds(half * cols, cols)],
-                    piece.at[e, pl.ds(rows[1 + half], rd)],
-                    sems.at[2],
-                )
-            )
     for copy in copies:
         copy.start()
     n = q_ref.shape[0] // 2
@@ -218,7 +211,7 @@
         note = jnp.where(lane == j, listed[0, j], note)
     note = note.astype(jnp.float32).astype(jnp.bfloat16)
     for s in range(ZS):
-        there = lax.rem(z + s, ZS)
+        there = jnp.bitwise_xor(z, s)
         kv_slots[s][...] = kv_all[there]
         q_slots[s][: HZ * n] = q_all[there]
         q_slots[s][HZ * n :] = note
@@ -234,7 +227,7 @@
     made = lambda shape: jax.ShapeDtypeStruct(shape, jnp.bfloat16)
     outs = pl.pallas_call(
         pack_kernel,
-        out_shape=[made(kv_shape)] * ZS + [made((q_rows + NOTE, 2 * HD))] * ZS + [made((2, piece_rows, cols))],
+        out_shape=[made(kv_shape)] * ZS + [made((q_rows + NOTE, 2 * HD))] * ZS + [made((1, piece_rows, cols))],
         in_specs=[HBM] * 7,
         out_specs=[VMEM] * (2 * ZS + 1),
         scratch_shapes=[
@@ -272,7 +265,7 @@
         for j in range(LIST):
             block = jnp.bitwise_and(jnp.right_shift(code, 3 * j), 7)
             side, source = block // ZS, lax.rem(block, ZS)
-            at.append(jnp.where(side == x, 0, ZS) + lax.rem(z - source + ZS, ZS))
+            at.append(jnp.where(side == x, 0, ZS) + jnp.bitwise_xor(z, source))
         length = jnp.right_shift(code, 3 * LIST)
 
         def scored(h, count, q_ref=q_ref, at=at):
@@ -325,7 +318,7 @@
     )(blocks, *queries)
 
 
-def laid(copies, ref, swapped, stage, shapes, into, sems):
+def laid(copies, ref, swapped, later, shapes, into, sems):
     x, z, y, c = (lax.axis_index(axis) for axis in AXES)
     out_all, up_all, down_all = into
     (rs, width), ru, rd = shapes
@@ -336,26 +329,23 @@
     second_x, second_y = jnp.where(core == 0, x, 1 - x), jnp.where(core == 0, 1 - y, y)
     mine, far = (x, y), (1 - x, 1 - y)
     first, second = (first_x, first_y), (second_x, second_y)
-    near_k = 1 + 2 * core
-    if stage == 0:
-        pieces = [(near_k, mine, 0), (near_k, mine, 1), (near_k, first, 0), (near_k, first, 1)]
-        pieces += [(2, mine, core)]
-    elif stage == 1:
-        pieces = [(near_k, far, 0), (near_k, far, 1), (near_k, second, 0), (2, first, core)]
+    if later:
+        pieces = [(2, second), (3, second), (3, far)]
     else:
-        pieces = [(near_k, second, 1), (2, second, core), (2, far, core)]
-    for at, (k, (px, py), half) in enumerate(pieces):
-        source = lax.rem(z - k + ZS, ZS)
-        slot_row = lax.rem(ZS - k, ZS) * rs
+        pieces = [(k, who) for who in (mine, first, far) for k in (1, 2)]
+        pieces += [(1, second), (3, mine), (3, first)]
+    for at, (k, (px, py)) in enumerate(pieces):
+        source = jnp.bitwise_xor(z, k)
+        slot_row = k * rs
         p = 2 * px + py
-        m = 2 * p + half
+        m = 2 * p + core
         piece = ref.at[at]
         copies.append(
             pltpu.make_async_copy(
                 piece.at[pl.ds(0, ro)],
                 out_all.at[
                     pl.ds(pl.multiple_of(slot_row + p * ro, 16), ro),
-                    pl.ds(pl.multiple_of(half * cols, 128), cols),
+                    pl.ds(pl.multiple_of(core * cols, 128), cols),
                 ],
                 sems.at[0],
             )
@@ -383,8 +373,7 @@
             )
 
 
-def gather_kernel(out_w, up_w, down_w, *refs):
-    held, refs = refs[:5], refs[5:]
+def gather_kernel(out_w, up_w, down_w, early, early_swapped, late, *refs):
     out_all, up_all, down_all, sems = refs
     z = lax.axis_index("head")
     rs, ru, rd = out_w.shape[0], up_w.shape[0], down_w.shape[0]
@@ -398,8 +387,9 @@
         ),
     ]
     shapes = (out_w.shape, ru, rd // 8)
-    for at, ref in enumerate(held):
-        laid(copies, ref, at % 2 == 1, at // 2, shapes, refs[:3], sems)
+    laid(copies, early, False, False, shapes, refs[:3], sems)
+    laid(copies, early_swapped, True, False, shapes, refs[:3], sems)
+    laid(copies, late, False, True, shapes, refs[:3], sems)
     for copy in copies:
         copy.start()
     for copy in copies:
@@ -427,7 +417,7 @@
     width, hidden_units = up_all.shape
     copies = []
     shapes = ((width // ZS, width), width // ZS, hidden_units // ZS // 8)
-    laid(copies, late_swapped, True, 2, shapes, (out_all, up_all, down_all), sems)
+    laid(copies, late_swapped, True, True, shapes, (out_all, up_all, down_all), sems)
     first = [copies[i] for i in range(len(copies)) if i % 4 == 0]
     second = [copies[i] for i in range(len(copies)) if i % 4 == 1]
     third = [copies[i] for i in range(len(copies)) if i % 4 > 1]
@@ -498,44 +488,41 @@
     kv_slots, q_slots, piece = packed(
         block_lists, list_lengths, queries, keys_values, out_weight, up_weight, down_weight
     )
-    core = lax.axis_index("core")
     kv_slots, q_slots = list(kv_slots), list(q_slots)
     near, q, far = {0: kv_slots[0]}, {0: q_slots[0]}, {}
-    w13 = sent(piece, both_ways)
+    w12 = jnp.concatenate([sent(piece, across_head(k)) for k in (1, 2)])
     far[0] = sent(kv_slots[0], over_blk)
-    near[1], near[3] = (sent(kv_slots[s], along_head(s)) for s in (1, 3))
-    w13, near[1], near[3], far[0], kv_slots[2] = lax.optimization_barrier(
-        (w13, near[1], near[3], far[0], kv_slots[2])
-    )
-    first13 = sent(w13, plane_first)
+    near[1], near[3] = (sent(kv_slots[s], across_head(s)) for s in (1, 3))
+    w12, near[1], near[3], far[0], kv_slots[2] = lax.optimization_barrier(
+        (w12, near[1], near[3], far[0], kv_slots[2])
+    )
+    first12 = sent(w12, plane_first)
     far13 = sent(jnp.stack([near[1], near[3]]), over_blk)
-    near[2] = sent(kv_slots[2], along_head(2))
-    w2 = sent(lax.dynamic_index_in_dim(w13, core, 0, keepdims=True), both_ways)
-    first13, far13, near[2], w2, q_slots[1], q_slots[2], q_slots[3] = lax.optimization_barrier(
-        (first13, far13, near[2], w2, q_slots[1], q_slots[2], q_slots[3])
-    )
+    near[2] = sent(kv_slots[2], across_head(2))
+    w3 = sent(w12[1:], across_head(1))
+    near[2], w3, q_slots[1], q_slots[2], q_slots[3] = lax.optimization_barrier(
+        (near[2], w3, q_slots[1], q_slots[2], q_slots[3])
+    )
+    far[2] = sent(near[2], over_blk)
+    more12 = sent(jnp.concatenate([first12, w12[:1]]), plane_second)
+    first12, far13, near[2], w3 = lax.optimization_barrier((first12, far13, near[2], w3))
     far[1], far[3] = far13[0], far13[1]
-    far[2] = sent(near[2], over_blk)
     away = (2, 1, 3)
     for s in away:
-        q[s] = sent(q_slots[s], along_head(s))
-    more13 = sent(jnp.concatenate([first13, w13[:1]]), plane_second)
-    more2 = sent(lax.dynamic_index_in_dim(first13, core, 0, keepdims=True), both_ways)
-    early = jnp.concatenate([w13, first13, w2])
-    early_swapped = sent(early, other_core)
+        q[s] = sent(q_slots[s], across_head(s))
+    more3 = sent(first12[1:], across_head(1))
     blocks = jnp.stack([near[s] for s in range(ZS)] + [far[s] for s in range(ZS)])
     ctx_slots = dict(zip(away, attended(blocks, [q[s] for s in away])))
-    more13, more2 = after(more13, ctx_slots[2], early_swapped), after(more2, ctx_slots[2])
-    late = sent(jnp.concatenate([w13[1:], w2, more2]), plane_second)
+    more12, more3 = after(more12, ctx_slots[2]), after(more3, ctx_slots[2])
+    early = jnp.concatenate([w12, first12, more12, w3, more3])
+    late = sent(jnp.concatenate([w12[1:], w3, more3]), plane_second)
     for s in away:
-        ctx_slots[s] = sent(ctx_slots[s], along_head(-s))
+        ctx_slots[s] = sent(ctx_slots[s], across_head(s))
     (ctx_slots[0],) = attended(blocks, [q[0]])
-    mid = jnp.concatenate([more13, more2])
-    mid_swapped = sent(mid, other_core)
-    held = [early, early_swapped, mid, mid_swapped, late]
+    early_swapped = sent(after(early, ctx_slots[0]), other_core)
     late = after(late, ctx_slots[0], ctx_slots[1], ctx_slots[2], ctx_slots[3])
     late_swapped = sent(late, other_core)
-    whole = gathered(out_weight, up_weight, down_weight, *held)
+    whole = gathered(out_weight, up_weight, down_weight, early, early_swapped, late)
     ctx_slots = [ctx_slots[s] for s in range(ZS)]
     return fed(norm_gain[None, :], surface, ctx_slots, whole, late_swapped)
 

time: 94.9 us -> 91.1 us (0.960)
  starting transfers between devices: 30.9 us -> 23.8 us
  waiting for transfers between devices: 46.3 us -> 49.4 us
    ppermute x21, starting transfers between devices: 30.9 us -> 23.8 us  [sent(): lax.ppermute(value, AXES, [(flat(*d), flat(*route(*d))) for d in DEVICES])]
    ppermute x21, waiting for transfers between devices: 46.3 us -> 49.4 us  [sent(): lax.ppermute(value, AXES, [(flat(*d), flat(*route(*d))) for d in DEVICES])]
  transfers between devices with their start and end apart: 21 -> 21, of which waited for: 11 -> 13; matrix products, arithmetic and copies ran while one was open for 2% -> 2% of each run, Pallas kernels for 7% -> 7%
where the time goes in v4:
time: 91.1 us; the launch traced here: 90.9 us
  waiting for transfers between devices  49.4 us (54%)
  starting transfers between devices  23.8 us (26%)
  Pallas kernels  14.5 us (16%)
  local copies, waits for them, and re-layouts  1.82 us (2%)
  between operations  1.13 us (1%)
    ppermute x21, waiting for transfers between devices, sent(): lax.ppermute(value, AXES, [(flat(*d), flat(*route(*d))) for d in DEVICES])  49.4 us
    ppermute x21, starting transfers between devices, sent(): lax.ppermute(value, AXES, [(flat(*d), flat(*route(*d))) for d in DEVICES])  23.8 us
    pallas_call x1, Pallas kernels, fed(): pl.pallas_call(feed_kernel, out_shape=[jax.ShapeDtypeStruct(v.shape, jnp....  4.96 us
    pallas_call x2, Pallas kernels, attended(): pl.pallas_call(attend_kernel, out_shape=[made] * len(queries), in_specs=[...  4.6 us
    pallas_call x1, Pallas kernels, packed(): pl.pallas_call(pack_kernel, out_shape=[made(kv_shape)] * ZS + [made((q_ro...  2.84 us
    pallas_call x1, Pallas kernels, gathered(): pl.pallas_call(gather_kernel, out_shape=[made(width, width), made(width,...  2.06 us
  transfers between devices with their start and end apart: 21, of which 13 were waited for; matrix products, arithmetic and copies ran while one was open for 2% of the time, Pallas kernels for 7%

profile of v4, /device:TPU:0, one launch (start us, length us, event | category | flops | bytes accessed | tf_op | source)
XLA Modules:
  0.0 90.9 jit_solution(13026498805414128001)
XLA Ops:
  0.7 2.8 %pack_heads.1 = (bf16[3,256,128]{2,1,0:T(8,128)(2,1)}, bf16[3,256,128]{2,1,0:T(8,128)(2,1)}, bf16[3,256,128]{2,1,0:T(8,128)(2,1)}, bf16[3,256,128]{2,1,0:T(8,128...) custom-call(s32[1,4]{1,0:T(1,128)} %listed_hbm.1, ...), custom_call_target="tpu_custom_call" | custom-call | bytes 4194304 | tf_op jit(solution)/shard_map/pack_heads/pallas_call | solution.py:228
  3.5 4.1 %collective-permute-start.1 = (bf16[1,432,384]{2,1,0:T(8,128)(2,1)}, bf16[1,432,384]{2,1,0:T(8,128)(2,1)S(1)}, u32[]{:S(2)}, u32[]{:S(2)}) collective-permute-start(bf16[1,432,384]{2,1,0:T(8,128)(2,1)} %get-tuple-element.40), channel_id=1, source_target_pairs={{0,8},{1,9},{2,10},{3,11},{4,12},{5,13},{6,14},{7,15},{8,0},{9,1},... | collective-permute-start | bytes 995336 | tf_op jit(solution)/shard_map/ppermute | solution.py:121
  7.6 1.6 %collective-permute-start = (bf16[1,432,384]{2,1,0:T(8,128)(2,1)}, bf16[1,432,384]{2,1,0:T(8,128)(2,1)S(1)}, u32[]{:S(2)}, u32[]{:S(2)}) collective-permute-start(bf16[1,432,384]{2,1,0:T(8,128)(2,1)} %get-tuple-element.40), channel_id=1, source_target_pairs={{0,4},{1,5},{2,6},{3,7},{4,0},{5,1},{6,2},{7,3},{8,12},{9,13},{10,... | collective-permute-start | bytes 995336 | tf_op jit(solution)/shard_map/ppermute | solution.py:121
  9.2 0.4 collective-permute-start.2
  9.6 1.3 %collective-permute-start.3 = (bf16[3,256,128]{2,1,0:T(8,128)(2,1)}, bf16[3,256,128]{2,1,0:T(8,128)(2,1)S(1)}, u32[]{:S(2)}, u32[]{:S(2)}) collective-permute-start(bf16[3,256,128]{2,1,0:T(8,128)(2,1)} %get-tuple-element.42), channel_id=1, source_target_pairs={{0,12},{1,13},{2,14},{3,15},{4,8},{5,9},{6,10},{7,11},{8,4},{9,5},... | collective-permute-start | bytes 589832 | tf_op jit(solution)/shard_map/ppermute | solution.py:121
  11.0 1.5 %collective-permute-start.4 = (bf16[3,256,128]{2,1,0:T(8,128)(2,1)}, bf16[3,256,128]{2,1,0:T(8,128)(2,1)S(1)}, u32[]{:S(2)}, u32[]{:S(2)}) collective-permute-start(bf16[3,256,128]{2,1,0:T(8,128)(2,1)} %get-tuple-element.39), channel_id=1, source_target_pairs={{0,16},{1,17},{2,18},{3,19},{4,20},{5,21},{6,22},{7,23},{8,24},{9,... | collective-permute-start | bytes 589832 | tf_op jit(solution)/shard_map/ppermute | solution.py:121
  12.5 1.0 %bitcast_dynamic-update-slice_fusion.3 = bf16[8,3,256,128]{3,2,1,0:T(8,128)(2,1)S(1)} fusion(bf16[3,256,128]{2,1,0:T(8,128)(2,1)} %get-tuple-element.39), kind=kLoop, calls=%fused_computation.7 | loop fusion | bytes 393216
  13.5 10.1 %collective-permute-done.1 = bf16[1,432,384]{2,1,0:T(8,128)(2,1)S(1)} collective-permute-done((bf16[1,432,384]{2,1,0:T(8,128)(2,1)}, bf16[1,432,384]{2,1,0:T(8,128)(2,1)S(1)}, u32[]{:S(2)}, u32[]{:S(2)}) %collective-permute-start.1) | collective-permute-done | bytes 331808 | tf_op jit(solution)/shard_map/ppermute | solution.py:121
  23.6 0.9 collective-permute-done
  24.6 3.0 %collective-permute-done.2 = bf16[3,256,128]{2,1,0:T(8,128)(2,1)S(1)} collective-permute-done((bf16[3,256,128]{2,1,0:T(8,128)(2,1)}, bf16[3,256,128]{2,1,0:T(8,128)(2,1)S(1)}, u32[]{:S(2)}, u32[]{:S(2)}) %collective-permute-start.2) | collective-permute-done | bytes 196640 | tf_op jit(solution)/shard_map/ppermute | solution.py:121
  27.5 4.7 %collective-permute-done.3 = bf16[3,256,128]{2,1,0:T(8,128)(2,1)S(1)} collective-permute-done((bf16[3,256,128]{2,1,0:T(8,128)(2,1)}, bf16[3,256,128]{2,1,0:T(8,128)(2,1)S(1)}, u32[]{:S(2)}, u32[]{:S(2)}) %collective-permute-start.3) | collective-permute-done | bytes 196640 | tf_op jit(solution)/shard_map/ppermute | solution.py:121
  32.3 1.5 %collective-permute-start.5 = (bf16[2,432,384]{2,1,0:T(8,128)(2,1)S(1)}, bf16[2,432,384]{2,1,0:T(8,128)(2,1)S(1)}, u32[]{:S(2)}, u32[]{:S(2)}) collective-permute-start(bf16[2,432,384]{2,1,0:T(8,128)(2,1)S(1)} %pad_maximum_fusion.2), channel_id=1, source_target_pairs={{0,16},{1,3},{2,18},{3,1},{4,20},{5,7},{6,22},{7,5},{8,24},{9,11},... | collective-permute-start | bytes 1990664 | tf_op jit(solution)/shard_map/ppermute | solution.py:121
  33.8 0.6 collective-permute-start.6
  34.6 3.0 %collective-permute-start.8 = (bf16[1,432,384]{2,1,0:T(8,128)(2,1)S(1)}, bf16[1,432,384]{2,1,0:T(8,128)(2,1)S(1)}, u32[]{:S(2)}, u32[]{:S(2)}) collective-permute-start(bf16[1,432,384]{2,1,0:T(8,128)(2,1)S(1)} %get-tuple-element.74), channel_id=1, source_target_pairs={{0,4},{1,5},{2,6},{3,7},{4,0},{5,1},{6,2},{7,3},{8,12},{9,13},{10,... | collective-permute-start | bytes 995336 | tf_op jit(solution)/shard_map/ppermute | solution.py:121
  37.7 8.1 %collective-permute-done.7 = bf16[3,256,128]{2,1,0:T(8,128)(2,1)S(1)} collective-permute-done((bf16[3,256,128]{2,1,0:T(8,128)(2,1)S(1)}, bf16[3,256,128]{2,1,0:T(8,128)(2,1)S(1)}, u32[]{:S(2)}, u32[]{:S(2)}) %collective-permute-start.7) | collective-permute-done | bytes 196640 | tf_op jit(solution)/shard_map/ppermute | solution.py:121
  45.8 3.1 %collective-permute-done.8 = bf16[1,432,384]{2,1,0:T(8,128)(2,1)S(1)} collective-permute-done((bf16[1,432,384]{2,1,0:T(8,128)(2,1)S(1)}, bf16[1,432,384]{2,1,0:T(8,128)(2,1)S(1)}, u32[]{:S(2)}, u32[]{:S(2)}) %collective-permute-start.8) | collective-permute-done | bytes 331808 | tf_op jit(solution)/shard_map/ppermute | solution.py:121
  49.2 1.8 %collective-permute-start.11 = (bf16[400,128]{1,0:T(8,128)(2,1)S(1)}, bf16[400,128]{1,0:T(8,128)(2,1)S(1)}, u32[]{:S(2)}, u32[]{:S(2)}) collective-permute-start(bf16[400,128]{1,0:T(8,128)(2,1)S(1)} %copy-done.8), channel_id=1, source_target_pairs={{0,4},{1,5},{2,6},{3,7},{4,0},{5,1},{6,2},{7,3},{8,12},{9,13},{10,... | collective-permute-start | bytes 307208 | tf_op jit(solution)/shard_map/ppermute | solution.py:121
  51.0 2.3 %collective-permute-start.12 = (bf16[400,128]{1,0:T(8,128)(2,1)S(1)}, bf16[400,128]{1,0:T(8,128)(2,1)S(1)}, u32[]{:S(2)}, u32[]{:S(2)}) collective-permute-start(bf16[400,128]{1,0:T(8,128)(2,1)S(1)} %copy-done.7), channel_id=1, source_target_pairs={{0,12},{1,13},{2,14},{3,15},{4,8},{5,9},{6,10},{7,11},{8,4},{9,5},... | collective-permute-start | bytes 307208 | tf_op jit(solution)/shard_map/ppermute | solution.py:121
  53.3 0.5 collective-permute-start.9
  54.0 0.6 collective-permute-start.16
  54.7 6.4 %collective-permute-done.9 = bf16[3,256,128]{2,1,0:T(8,128)(2,1)S(1)} collective-permute-done((bf16[3,256,128]{2,1,0:T(8,128)(2,1)S(1)}, bf16[3,256,128]{2,1,0:T(8,128)(2,1)S(1)}, u32[]{:S(2)}, u32[]{:S(2)}) %collective-permute-start.9) | collective-permute-done | bytes 196640 | tf_op jit(solution)/shard_map/ppermute | solution.py:121
  61.2 1.5 %attend.2.refs_0_ = bf16[3,128,128]{2,1,0:T(8,128)(2,1)S(1)} custom-call(bf16[8,3,256,128]{3,2,1,0:T(8,128)(2,1)S(1)} %slice_dynamic-update-slice_fusion.blocks, bf16[400,128]{1,0:T(8,128)(2,1)S(1)} %copy-done.4), custom_call_target="tpu_custom_call" | custom-call | flops 500000000 | bytes 1048576 | tf_op jit(solution)/shard_map/attend/pallas_call | solution.py:308
  62.7 3.1 %attend.3 = (bf16[3,128,128]{2,1,0:T(8,128)(2,1)S(1)}, bf16[3,128,128]{2,1,0:T(8,128)(2,1)S(1)}, bf16[3,128,128]{2,1,0:T(8,128)(2,1)S(1)}) custom-call(bf16[8,3,256,128]{3,2,1,0:T(8,128)(2,1)S(1)} %slice_dynamic-update-slice_fusion.blocks, bf16[400,128]{1,0:T(8,128)(2,1)S(1)} %collective-permute-done.10.refs_0_, ...), custom_call_target="tpu_custom_call" | custom-call | flops 500000000 | bytes 1048576 | tf_op jit(solution)/shard_map/attend/pallas_call | solution.py:308
  66.0 2.3 %collective-permute-done.17 = bf16[1,432,384]{2,1,0:T(8,128)(2,1)S(1)} collective-permute-done((bf16[1,432,384]{2,1,0:T(8,128)(2,1)S(1)}, bf16[1,432,384]{2,1,0:T(8,128)(2,1)S(1)}, u32[]{:S(2)}, u32[]{:S(2)}) %collective-permute-start.17) | collective-permute-done | bytes 331808 | tf_op jit(solution)/shard_map/ppermute | solution.py:121
  68.9 0.5 collective-permute-start.19
  69.4 1.5 %collective-permute-start.15 = (bf16[3,128,128]{2,1,0:T(8,128)(2,1)S(1)}, bf16[3,128,128]{2,1,0:T(8,128)(2,1)S(1)}, u32[]{:S(2)}, u32[]{:S(2)}) collective-permute-start(bf16[3,128,128]{2,1,0:T(8,128)(2,1)S(1)} %get-tuple-element.62), channel_id=1, source_target_pairs={{0,12},{1,13},{2,14},{3,15},{4,8},{5,9},{6,10},{7,11},{8,4},{9,5},... | collective-permute-start | bytes 294920 | tf_op jit(solution)/shard_map/ppermute | solution.py:121
  71.0 1.9 %collective-permute-start.14 = (bf16[3,128,128]{2,1,0:T(8,128)(2,1)S(1)}, bf16[3,128,128]{2,1,0:T(8,128)(2,1)S(1)}, u32[]{:S(2)}, u32[]{:S(2)}) collective-permute-start(bf16[3,128,128]{2,1,0:T(8,128)(2,1)S(1)} %get-tuple-element.61), channel_id=1, source_target_pairs={{0,8},{1,9},{2,10},{3,11},{4,12},{5,13},{6,14},{7,15},{8,0},{9,1},... | collective-permute-start | bytes 294920 | tf_op jit(solution)/shard_map/ppermute | solution.py:121
  72.9 2.0 %collective-permute-done.13.refs_1_ = bf16[3,128,128]{2,1,0:T(8,128)(2,1)S(1)} collective-permute-done((bf16[3,128,128]{2,1,0:T(8,128)(2,1)S(1)}, bf16[3,128,128]{2,1,0:T(8,128)(2,1)S(1)}, u32[]{:S(2)}, u32[]{:S(2)}) %collective-permute-start.13) | collective-permute-done | bytes 98336 | tf_op jit(solution)/shard_map/ppermute | solution.py:121
  74.9 1.9 %collective-permute-done.15.refs_3_ = bf16[3,128,128]{2,1,0:T(8,128)(2,1)S(1)} collective-permute-done((bf16[3,128,128]{2,1,0:T(8,128)(2,1)S(1)}, bf16[3,128,128]{2,1,0:T(8,128)(2,1)S(1)}, u32[]{:S(2)}, u32[]{:S(2)}) %collective-permute-start.15) | collective-permute-done | bytes 98336 | tf_op jit(solution)/shard_map/ppermute | solution.py:121
  76.8 6.0 %collective-permute-done.14.refs_2_ = bf16[3,128,128]{2,1,0:T(8,128)(2,1)S(1)} collective-permute-done((bf16[3,128,128]{2,1,0:T(8,128)(2,1)S(1)}, bf16[3,128,128]{2,1,0:T(8,128)(2,1)S(1)}, u32[]{:S(2)}, u32[]{:S(2)}) %collective-permute-start.14) | collective-permute-done | bytes 98336 | tf_op jit(solution)/shard_map/ppermute | solution.py:121
  83.3 2.1 %gather.1 = (bf16[768,768]{1,0:T(8,128)(2,1)S(1)}, bf16[768,3072]{1,0:T(8,128)(2,1)S(1)}, bf16[3072,768]{1,0:T(8,128)(2,1)S(1)}) custom-call(bf16[192,768]{1,0:T(8,128)(2,1)S(1)} %copy-done.2, bf16[192,3072]{1,0:T(8,128)(2,1)S(1)} %copy-done, bf16[768,768]{1,0:T(8,128)(2,1)S(1)} %copy-done.1, ...), custom_call_target="tpu_custom_call" | custom-call | bytes 12582912 | tf_op jit(solution)/shard_map/gather/pallas_call | solution.py:402
  85.8 5.0 %feed.1 = (bf16[256,768]{1,0:T(8,128)(2,1)}, bf16[768,768]{1,0:T(8,128)(2,1)S(1)}, bf16[768,3072]{1,0:T(8,128)(2,1)S(1)}, bf16[3072,768]{1,0:T(8,128)(2,1)S(1)}) custom-call(f32[1,768]{1,0:T(1,128)S(1)} %broadcast_in_dim.3.gain, bf16[256,768]{1,0:T(8,128)(2,1)S(1)} %copy-done.3, ...), custom_call_target="tpu_custom_call", output_to_operand_aliasing={{1}: (6, {}), {2}: (7, {}), {3}: (8, {})} | custom-call | flops 3000000000 | bytes 12582912 | tf_op jit(solution)/shard_map/feed/pallas_call | solution.py:461
  (55 shorter events, 2.7 us)
Async XLA Ops:
  3.5 20.1 %collective-permute-start.1 = (bf16[1,432,384]{2,1,0:T(8,128)(2,1)}, bf16[1,432,384]{2,1,0:T(8,128)(2,1)S(1)}, u32[]{:S(2)}, u32[]{:S(2)}) collective-permute-start(bf16[1,432,384]{2,1,0:T(8,128)(2,1)} %get-tuple-element.40), channel_id=1, source_target_pairs={{0,8},{1,9},{2,10},{3,11},{4,12},{5,13},{6,14},{7,15},{8,0},{9,1},... | collective-permute-start | bytes 995336 | tf_op jit(solution)/shard_map/ppermute | solution.py:121
  7.6 16.9 %collective-permute-start = (bf16[1,432,384]{2,1,0:T(8,128)(2,1)}, bf16[1,432,384]{2,1,0:T(8,128)(2,1)S(1)}, u32[]{:S(2)}, u32[]{:S(2)}) collective-permute-start(bf16[1,432,384]{2,1,0:T(8,128)(2,1)} %get-tuple-element.40), channel_id=1, source_target_pairs={{0,4},{1,5},{2,6},{3,7},{4,0},{5,1},{6,2},{7,3},{8,12},{9,13},{10,... | collective-permute-start | bytes 995336 | tf_op jit(solution)/shard_map/ppermute | solution.py:121
  9.2 18.3 %collective-permute-start.2 = (bf16[3,256,128]{2,1,0:T(8,128)(2,1)}, bf16[3,256,128]{2,1,0:T(8,128)(2,1)S(1)}, u32[]{:S(2)}, u32[]{:S(2)}) collective-permute-start(bf16[3,256,128]{2,1,0:T(8,128)(2,1)} %get-tuple-element.41), channel_id=1, source_target_pairs={{0,4},{1,5},{2,6},{3,7},{4,0},{5,1},{6,2},{7,3},{8,12},{9,13},{10,... | collective-permute-start | bytes 589832 | tf_op jit(solution)/shard_map/ppermute | solution.py:121
  9.6 22.6 %collective-permute-start.3 = (bf16[3,256,128]{2,1,0:T(8,128)(2,1)}, bf16[3,256,128]{2,1,0:T(8,128)(2,1)S(1)}, u32[]{:S(2)}, u32[]{:S(2)}) collective-permute-start(bf16[3,256,128]{2,1,0:T(8,128)(2,1)} %get-tuple-element.42), channel_id=1, source_target_pairs={{0,12},{1,13},{2,14},{3,15},{4,8},{5,9},{6,10},{7,11},{8,4},{9,5},... | collective-permute-start | bytes 589832 | tf_op jit(solution)/shard_map/ppermute | solution.py:121
  11.0 21.3 %collective-permute-start.4 = (bf16[3,256,128]{2,1,0:T(8,128)(2,1)}, bf16[3,256,128]{2,1,0:T(8,128)(2,1)S(1)}, u32[]{:S(2)}, u32[]{:S(2)}) collective-permute-start(bf16[3,256,128]{2,1,0:T(8,128)(2,1)} %get-tuple-element.39), channel_id=1, source_target_pairs={{0,16},{1,17},{2,18},{3,19},{4,20},{5,21},{6,22},{7,23},{8,24},{9,... | collective-permute-start | bytes 589832 | tf_op jit(solution)/shard_map/ppermute | solution.py:121
  13.4 21.1 %copy-start.6 = (bf16[3,256,128]{2,1,0:T(8,128)(2,1)S(1)}, bf16[3,256,128]{2,1,0:T(8,128)(2,1)}, u32[]{:S(2)}) copy-start(bf16[3,256,128]{2,1,0:T(8,128)(2,1)} %get-tuple-element.47) | copy-start | bytes 589828
  32.3 21.6 %collective-permute-start.5 = (bf16[2,432,384]{2,1,0:T(8,128)(2,1)S(1)}, bf16[2,432,384]{2,1,0:T(8,128)(2,1)S(1)}, u32[]{:S(2)}, u32[]{:S(2)}) collective-permute-start(bf16[2,432,384]{2,1,0:T(8,128)(2,1)S(1)} %pad_maximum_fusion.2), channel_id=1, source_target_pairs={{0,16},{1,3},{2,18},{3,1},{4,20},{5,7},{6,22},{7,5},{8,24},{9,11},... | collective-permute-start | bytes 1990664 | tf_op jit(solution)/shard_map/ppermute | solution.py:121
  33.8 15.1 %copy-start.9 = (bf16[400,128]{1,0:T(8,128)(2,1)S(1)}, bf16[400,128]{1,0:T(8,128)(2,1)}, u32[]{:S(2)}) copy-start(bf16[400,128]{1,0:T(8,128)(2,1)} %get-tuple-element.57) | copy-start | bytes 307204
  33.8 15.4 %copy-start.8 = (bf16[400,128]{1,0:T(8,128)(2,1)S(1)}, bf16[400,128]{1,0:T(8,128)(2,1)}, u32[]{:S(2)}) copy-start(bf16[400,128]{1,0:T(8,128)(2,1)} %get-tuple-element.58) | copy-start | bytes 307204
  33.8 17.2 %copy-start.7 = (bf16[400,128]{1,0:T(8,128)(2,1)S(1)}, bf16[400,128]{1,0:T(8,128)(2,1)}, u32[]{:S(2)}) copy-start(bf16[400,128]{1,0:T(8,128)(2,1)} %get-tuple-element.59) | copy-start | bytes 307204
  33.8 19.4 %collective-permute-start.6 = (bf16[2,3,256,128]{3,2,1,0:T(8,128)(2,1)S(1)}, bf16[2,3,256,128]{3,2,1,0:T(8,128)(2,1)S(1)}, u32[]{:S(2)}, u32[]{:S(2)}) collective-permute-start(bf16[2,3,256,128]{3,2,1,0:T(8,128)(2,1)S(1)} %pad_maximum_fusion.3), channel_id=1, source_target_pairs={{0,16},{1,17},{2,18},{3,19},{4,20},{5,21},{6,22},{7,23},{8,24},{9,... | collective-permute-start | bytes 1179656 | tf_op jit(solution)/shard_map/ppermute | solution.py:121
  34.5 11.3 %collective-permute-start.7 = (bf16[3,256,128]{2,1,0:T(8,128)(2,1)S(1)}, bf16[3,256,128]{2,1,0:T(8,128)(2,1)S(1)}, u32[]{:S(2)}, u32[]{:S(2)}) collective-permute-start(bf16[3,256,128]{2,1,0:T(8,128)(2,1)S(1)} %copy-done.6), channel_id=1, source_target_pairs={{0,8},{1,9},{2,10},{3,11},{4,12},{5,13},{6,14},{7,15},{8,0},{9,1},... | collective-permute-start | bytes 589832 | tf_op jit(solution)/shard_map/ppermute | solution.py:121
  34.6 14.3 %collective-permute-start.8 = (bf16[1,432,384]{2,1,0:T(8,128)(2,1)S(1)}, bf16[1,432,384]{2,1,0:T(8,128)(2,1)S(1)}, u32[]{:S(2)}, u32[]{:S(2)}) collective-permute-start(bf16[1,432,384]{2,1,0:T(8,128)(2,1)S(1)} %get-tuple-element.74), channel_id=1, source_target_pairs={{0,4},{1,5},{2,6},{3,7},{4,0},{5,1},{6,2},{7,3},{8,12},{9,13},{10,... | collective-permute-start | bytes 995336 | tf_op jit(solution)/shard_map/ppermute | solution.py:121
  48.9 13.8 %collective-permute-start.10 = (bf16[400,128]{1,0:T(8,128)(2,1)S(1)}, bf16[400,128]{1,0:T(8,128)(2,1)S(1)}, u32[]{:S(2)}, u32[]{:S(2)}) collective-permute-start(bf16[400,128]{1,0:T(8,128)(2,1)S(1)} %copy-done.9), channel_id=1, source_target_pairs={{0,8},{1,9},{2,10},{3,11},{4,12},{5,13},{6,14},{7,15},{8,0},{9,1},... | collective-permute-start | bytes 307208 | tf_op jit(solution)/shard_map/ppermute | solution.py:121
  49.2 13.5 %collective-permute-start.11 = (bf16[400,128]{1,0:T(8,128)(2,1)S(1)}, bf16[400,128]{1,0:T(8,128)(2,1)S(1)}, u32[]{:S(2)}, u32[]{:S(2)}) collective-permute-start(bf16[400,128]{1,0:T(8,128)(2,1)S(1)} %copy-done.8), channel_id=1, source_target_pairs={{0,4},{1,5},{2,6},{3,7},{4,0},{5,1},{6,2},{7,3},{8,12},{9,13},{10,... | collective-permute-start | bytes 307208 | tf_op jit(solution)/shard_map/ppermute | solution.py:121
  51.0 11.7 %collective-permute-start.12 = (bf16[400,128]{1,0:T(8,128)(2,1)S(1)}, bf16[400,128]{1,0:T(8,128)(2,1)S(1)}, u32[]{:S(2)}, u32[]{:S(2)}) collective-permute-start(bf16[400,128]{1,0:T(8,128)(2,1)S(1)} %copy-done.7), channel_id=1, source_target_pairs={{0,12},{1,13},{2,14},{3,15},{4,8},{5,9},{6,10},{7,11},{8,4},{9,5},... | collective-permute-start | bytes 307208 | tf_op jit(solution)/shard_map/ppermute | solution.py:121
  53.3 7.8 %collective-permute-start.9 = (bf16[3,256,128]{2,1,0:T(8,128)(2,1)S(1)}, bf16[3,256,128]{2,1,0:T(8,128)(2,1)S(1)}, u32[]{:S(2)}, u32[]{:S(2)}) collective-permute-start(bf16[3,256,128]{2,1,0:T(8,128)(2,1)S(1)} %collective-permute-done.7), channel_id=1, source_target_pairs={{0,16},{1,17},{2,18},{3,19},{4,20},{5,21},{6,22},{7,23},{8,24},{9,... | collective-permute-start | bytes 589832 | tf_op jit(solution)/shard_map/ppermute | solution.py:121
  53.9 7.3 %copy-start.4 = (bf16[400,128]{1,0:T(8,128)(2,1)S(1)}, bf16[400,128]{1,0:T(8,128)(2,1)}, u32[]{:S(2)}) copy-start(bf16[400,128]{1,0:T(8,128)(2,1)} %get-tuple-element.56.refs_0_) | copy-start | bytes 307204
  54.0 14.3 %collective-permute-start.16 = (bf16[3,432,384]{2,1,0:T(8,128)(2,1)S(1)}, bf16[3,432,384]{2,1,0:T(8,128)(2,1)S(1)}, u32[]{:S(2)}, u32[]{:S(2)}) collective-permute-start(bf16[3,432,384]{2,1,0:T(8,128)(2,1)S(1)} %pad_maximum_fusion), channel_id=1, source_target_pairs={{0,2},{1,17},{2,0},{3,19},{4,6},{5,21},{6,4},{7,23},{8,10},{9,25},... | collective-permute-start | bytes 2985992 | tf_op jit(solution)/shard_map/ppermute | solution.py:121
  61.1 7.1 %collective-permute-start.17 = (bf16[1,432,384]{2,1,0:T(8,128)(2,1)S(1)}, bf16[1,432,384]{2,1,0:T(8,128)(2,1)S(1)}, u32[]{:S(2)}, u32[]{:S(2)}) collective-permute-start(bf16[1,432,384]{2,1,0:T(8,128)(2,1)S(1)} %slice.20), channel_id=1, source_target_pairs={{0,4},{1,5},{2,6},{3,7},{4,0},{5,1},{6,2},{7,3},{8,12},{9,13},{10,... | collective-permute-start | bytes 995336 | tf_op jit(solution)/shard_map/ppermute | solution.py:121
  68.4 14.8 %copy-start.5 = (f32[768]{0:T(1024)S(1)}, f32[768]{0:T(1024)}, u32[]{:S(2)}) copy-start(f32[768]{0:T(1024)} %param.15) | copy-start | bytes 9220
  68.5 14.8 %copy-start = (bf16[192,3072]{1,0:T(8,128)(2,1)S(1)}, bf16[192,3072]{1,0:T(8,128)(2,1)}, u32[]{:S(2)}) copy-start(bf16[192,3072]{1,0:T(8,128)(2,1)} %up_w.3) | copy-start | bytes 3538948
  68.5 14.8 %copy-start.1 = (bf16[768,768]{1,0:T(8,128)(2,1)S(1)}, bf16[768,768]{1,0:T(8,128)(2,1)}, u32[]{:S(2)}) copy-start(bf16[768,768]{1,0:T(8,128)(2,1)} %down_w.3) | copy-start | bytes 3538948
  68.5 14.8 %copy-start.2 = (bf16[192,768]{1,0:T(8,128)(2,1)S(1)}, bf16[192,768]{1,0:T(8,128)(2,1)}, u32[]{:S(2)}) copy-start(bf16[192,768]{1,0:T(8,128)(2,1)} %out_w.3) | copy-start | bytes 884740
  68.6 14.6 %collective-permute-start.18 = (bf16[9,432,384]{2,1,0:T(8,128)(2,1)S(1)}, bf16[9,432,384]{2,1,0:T(8,128)(2,1)S(1)}, u32[]{:S(2)}, u32[]{:S(2)}) collective-permute-start(bf16[9,432,384]{2,1,0:T(8,128)(2,1)S(1)} %constant_dynamic-update-slice_fusion.2.early), channel_id=1, source_target_pairs={{0,1},{1,0},{2,3},{3,2},{4,5},{5,4},{6,7},{7,6},{8,9},{9,8},{10,11... | collective-permute-start | bytes 8957960 | tf_op jit(solution)/shard_map/ppermute | solution.py:121
  68.9 14.3 %collective-permute-start.19 = (bf16[3,432,384]{2,1,0:T(8,128)(2,1)S(1)}, bf16[3,432,384]{2,1,0:T(8,128)(2,1)S(1)}, u32[]{:S(2)}, u32[]{:S(2)}) collective-permute-start(bf16[3,432,384]{2,1,0:T(8,128)(2,1)S(1)} %pad_maximum_fusion.1), channel_id=1, source_target_pairs={{0,2},{1,17},{2,0},{3,19},{4,6},{5,21},{6,4},{7,23},{8,10},{9,25},... | collective-permute-start | bytes 2985992 | tf_op jit(solution)/shard_map/ppermute | solution.py:121
  69.4 5.5 %collective-permute-start.13 = (bf16[3,128,128]{2,1,0:T(8,128)(2,1)S(1)}, bf16[3,128,128]{2,1,0:T(8,128)(2,1)S(1)}, u32[]{:S(2)}, u32[]{:S(2)}) collective-permute-start(bf16[3,128,128]{2,1,0:T(8,128)(2,1)S(1)} %get-tuple-element.60), channel_id=1, source_target_pairs={{0,4},{1,5},{2,6},{3,7},{4,0},{5,1},{6,2},{7,3},{8,12},{9,13},{10,... | collective-permute-start | bytes 294920 | tf_op jit(solution)/shard_map/ppermute | solution.py:121
  69.4 7.4 %collective-permute-start.15 = (bf16[3,128,128]{2,1,0:T(8,128)(2,1)S(1)}, bf16[3,128,128]{2,1,0:T(8,128)(2,1)S(1)}, u32[]{:S(2)}, u32[]{:S(2)}) collective-permute-start(bf16[3,128,128]{2,1,0:T(8,128)(2,1)S(1)} %get-tuple-element.62), channel_id=1, source_target_pairs={{0,12},{1,13},{2,14},{3,15},{4,8},{5,9},{6,10},{7,11},{8,4},{9,5},... | collective-permute-start | bytes 294920 | tf_op jit(solution)/shard_map/ppermute | solution.py:121
  71.0 11.8 %collective-permute-start.14 = (bf16[3,128,128]{2,1,0:T(8,128)(2,1)S(1)}, bf16[3,128,128]{2,1,0:T(8,128)(2,1)S(1)}, u32[]{:S(2)}, u32[]{:S(2)}) collective-permute-start(bf16[3,128,128]{2,1,0:T(8,128)(2,1)S(1)} %get-tuple-element.61), channel_id=1, source_target_pairs={{0,8},{1,9},{2,10},{3,11},{4,12},{5,13},{6,14},{7,15},{8,0},{9,1},... | collective-permute-start | bytes 294920 | tf_op jit(solution)/shard_map/ppermute | solution.py:121
  83.2 2.6 %collective-permute-start.20 = (bf16[3,432,384]{2,1,0:T(8,128)(2,1)S(1)}, bf16[3,432,384]{2,1,0:T(8,128)(2,1)S(1)}, u32[]{:S(2)}, u32[]{:S(2)}) collective-permute-start(bf16[3,432,384]{2,1,0:T(8,128)(2,1)S(1)} %collective-permute-done.19.late), channel_id=1, source_target_pairs={{0,1},{1,0},{2,3},{3,2},{4,5},{5,4},{6,7},{7,6},{8,9},{9,8},{10,11... | collective-permute-start | bytes 2985992 | tf_op jit(solution)/shard_map/ppermute | solution.py:121
  83.2 2.6 %copy-start.3 = (bf16[256,768]{1,0:T(8,128)(2,1)S(1)}, bf16[256,768]{1,0:T(8,128)(2,1)}, u32[]{:S(2)}) copy-start(bf16[256,768]{1,0:T(8,128)(2,1)} %surface.1) | copy-start | bytes 1179652

commit v5 on v4

--- a/solution.py
+++ b/solution.py
@@ -493,9 +493,6 @@
     w12 = jnp.concatenate([sent(piece, across_head(k)) for k in (1, 2)])
     far[0] = sent(kv_slots[0], over_blk)
     near[1], near[3] = (sent(kv_slots[s], across_head(s)) for s in (1, 3))
-    w12, near[1], near[3], far[0], kv_slots[2] = lax.optimization_barrier(
-        (w12, near[1], near[3], far[0], kv_slots[2])
-    )
     first12 = sent(w12, plane_first)
     far13 = sent(jnp.stack([near[1], near[3]]), over_blk)
     near[2] = sent(kv_slots[2], across_head(2))

time: 91.1 us -> 88.1 us (0.967)
  waiting for transfers between devices: 49.4 us -> 42.1 us
  starting transfers between devices: 23.8 us -> 28.5 us
    ppermute x21, waiting for transfers between devices: 49.4 us -> 42.1 us  [sent(): lax.ppermute(value, AXES, [(flat(*d), flat(*route(*d))) for d in DEVICES])]
    ppermute x21, starting transfers between devices: 23.8 us -> 28.5 us  [sent(): lax.ppermute(value, AXES, [(flat(*d), flat(*route(*d))) for d in DEVICES])]
  transfers between devices with their start and end apart: 21 -> 21, of which waited for: 13 -> 12; matrix products, arithmetic and copies ran while one was open for 2% -> 2% of each run, Pallas kernels for 7% -> 7%
where the time goes in v5:
time: 88.1 us; the launch traced here: 87.9 us
  waiting for transfers between devices  42.1 us (48%)
  starting transfers between devices  28.5 us (32%)
  Pallas kernels  14.1 us (16%)
  local copies, waits for them, and re-layouts  1.73 us (2%)
  between operations  1.12 us (1%)
    ppermute x21, waiting for transfers between devices, sent(): lax.ppermute(value, AXES, [(flat(*d), flat(*route(*d))) for d in DEVICES])  42.1 us
    ppermute x21, starting transfers between devices, sent(): lax.ppermute(value, AXES, [(flat(*d), flat(*route(*d))) for d in DEVICES])  28.5 us
    pallas_call x1, Pallas kernels, fed(): pl.pallas_call(feed_kernel, out_shape=[jax.ShapeDtypeStruct(v.shape, jnp....  4.95 us
    pallas_call x2, Pallas kernels, attended(): pl.pallas_call(attend_kernel, out_shape=[made] * len(queries), in_specs=[...  4.28 us
    pallas_call x1, Pallas kernels, packed(): pl.pallas_call(pack_kernel, out_shape=[made(kv_shape)] * ZS + [made((q_ro...  2.84 us
    pallas_call x1, Pallas kernels, gathered(): pl.pallas_call(gather_kernel, out_shape=[made(width, width), made(width,...  2.06 us
  transfers between devices with their start and end apart: 21, of which 12 were waited for; matrix products, arithmetic and copies ran while one was open for 2% of the time, Pallas kernels for 7%

profile of v5, /device:TPU:0, one launch (start us, length us, event | category | flops | bytes accessed | tf_op | source)
XLA Modules:
  0.0 87.9 jit_solution(11108415301331861189)
XLA Ops:
  0.7 2.8 %pack_heads.1 = (bf16[3,256,128]{2,1,0:T(8,128)(2,1)}, bf16[3,256,128]{2,1,0:T(8,128)(2,1)}, bf16[3,256,128]{2,1,0:T(8,128)(2,1)}, bf16[3,256,128]{2,1,0:T(8,128...) custom-call(s32[1,4]{1,0:T(1,128)} %listed_hbm.1, ...), custom_call_target="tpu_custom_call" | custom-call | bytes 4194304 | tf_op jit(solution)/shard_map/pack_heads/pallas_call | solution.py:228
  3.5 4.1 %collective-permute-start.2 = (bf16[1,432,384]{2,1,0:T(8,128)(2,1)}, bf16[1,432,384]{2,1,0:T(8,128)(2,1)S(1)}, u32[]{:S(2)}, u32[]{:S(2)}) collective-permute-start(bf16[1,432,384]{2,1,0:T(8,128)(2,1)} %get-tuple-element.36), channel_id=1, source_target_pairs={{0,8},{1,9},{2,10},{3,11},{4,12},{5,13},{6,14},{7,15},{8,0},{9,1},... | collective-permute-start | bytes 995336 | tf_op jit(solution)/shard_map/ppermute | solution.py:121
  7.6 1.6 %collective-permute-start.1 = (bf16[1,432,384]{2,1,0:T(8,128)(2,1)}, bf16[1,432,384]{2,1,0:T(8,128)(2,1)S(1)}, u32[]{:S(2)}, u32[]{:S(2)}) collective-permute-start(bf16[1,432,384]{2,1,0:T(8,128)(2,1)} %get-tuple-element.36), channel_id=1, source_target_pairs={{0,4},{1,5},{2,6},{3,7},{4,0},{5,1},{6,2},{7,3},{8,12},{9,13},{10,... | collective-permute-start | bytes 995336 | tf_op jit(solution)/shard_map/ppermute | solution.py:121
  9.2 0.4 collective-permute-start
  9.6 1.3 %collective-permute-start.4 = (bf16[3,256,128]{2,1,0:T(8,128)(2,1)}, bf16[3,256,128]{2,1,0:T(8,128)(2,1)S(1)}, u32[]{:S(2)}, u32[]{:S(2)}) collective-permute-start(bf16[3,256,128]{2,1,0:T(8,128)(2,1)} %get-tuple-element.37), channel_id=1, source_target_pairs={{0,12},{1,13},{2,14},{3,15},{4,8},{5,9},{6,10},{7,11},{8,4},{9,5},... | collective-permute-start | bytes 589832 | tf_op jit(solution)/shard_map/ppermute | solution.py:121
  11.0 1.7 %collective-permute-start.6 = (bf16[3,256,128]{2,1,0:T(8,128)(2,1)}, bf16[3,256,128]{2,1,0:T(8,128)(2,1)S(1)}, u32[]{:S(2)}, u32[]{:S(2)}) collective-permute-start(bf16[3,256,128]{2,1,0:T(8,128)(2,1)} %get-tuple-element.38), channel_id=1, source_target_pairs={{0,8},{1,9},{2,10},{3,11},{4,12},{5,13},{6,14},{7,15},{8,0},{9,1},... | collective-permute-start | bytes 589832 | tf_op jit(solution)/shard_map/ppermute | solution.py:121
  12.7 10.9 %collective-permute-done.2 = bf16[1,432,384]{2,1,0:T(8,128)(2,1)S(1)} collective-permute-done((bf16[1,432,384]{2,1,0:T(8,128)(2,1)}, bf16[1,432,384]{2,1,0:T(8,128)(2,1)S(1)}, u32[]{:S(2)}, u32[]{:S(2)}) %collective-permute-start.2) | collective-permute-done | bytes 331808 | tf_op jit(solution)/shard_map/ppermute | solution.py:121
  23.6 1.8 %collective-permute-start.8 = (bf16[3,256,128]{2,1,0:T(8,128)(2,1)}, bf16[3,256,128]{2,1,0:T(8,128)(2,1)S(1)}, u32[]{:S(2)}, u32[]{:S(2)}) collective-permute-start(bf16[3,256,128]{2,1,0:T(8,128)(2,1)} %get-tuple-element.34), channel_id=1, source_target_pairs={{0,16},{1,17},{2,18},{3,19},{4,20},{5,21},{6,22},{7,23},{8,24},{9,... | collective-permute-start | bytes 589832 | tf_op jit(solution)/shard_map/ppermute | solution.py:121
  25.5 0.7 collective-permute-start.3
  26.2 0.9 %bitcast_dynamic-update-slice_fusion.3 = bf16[8,3,256,128]{3,2,1,0:T(8,128)(2,1)S(1)} fusion(bf16[3,256,128]{2,1,0:T(8,128)(2,1)} %get-tuple-element.34), kind=kLoop, calls=%fused_computation.7 | loop fusion | bytes 393216
  27.1 4.6 %collective-permute-done = bf16[3,256,128]{2,1,0:T(8,128)(2,1)S(1)} collective-permute-done((bf16[3,256,128]{2,1,0:T(8,128)(2,1)}, bf16[3,256,128]{2,1,0:T(8,128)(2,1)S(1)}, u32[]{:S(2)}, u32[]{:S(2)}) %collective-permute-start) | collective-permute-done | bytes 196640 | tf_op jit(solution)/shard_map/ppermute | solution.py:121
  31.8 1.7 %collective-permute-done.4 = bf16[3,256,128]{2,1,0:T(8,128)(2,1)S(1)} collective-permute-done((bf16[3,256,128]{2,1,0:T(8,128)(2,1)}, bf16[3,256,128]{2,1,0:T(8,128)(2,1)S(1)}, u32[]{:S(2)}, u32[]{:S(2)}) %collective-permute-start.4) | collective-permute-done | bytes 196640 | tf_op jit(solution)/shard_map/ppermute | solution.py:121
  33.5 1.6 %collective-permute-start.5 = (bf16[2,3,256,128]{3,2,1,0:T(8,128)(2,1)S(1)}, bf16[2,3,256,128]{3,2,1,0:T(8,128)(2,1)S(1)}, u32[]{:S(2)}, u32[]{:S(2)}) collective-permute-start(bf16[2,3,256,128]{3,2,1,0:T(8,128)(2,1)S(1)} %pad_maximum_fusion.3), channel_id=1, source_target_pairs={{0,16},{1,17},{2,18},{3,19},{4,20},{5,21},{6,22},{7,23},{8,24},{9,... | collective-permute-start | bytes 1179656 | tf_op jit(solution)/shard_map/ppermute | solution.py:121
  35.1 2.6 %collective-permute-start.7 = (bf16[1,432,384]{2,1,0:T(8,128)(2,1)S(1)}, bf16[1,432,384]{2,1,0:T(8,128)(2,1)S(1)}, u32[]{:S(2)}, u32[]{:S(2)}) collective-permute-start(bf16[1,432,384]{2,1,0:T(8,128)(2,1)S(1)} %collective-permute-done.2), channel_id=1, source_target_pairs={{0,4},{1,5},{2,6},{3,7},{4,0},{5,1},{6,2},{7,3},{8,12},{9,13},{10,... | collective-permute-start | bytes 995336 | tf_op jit(solution)/shard_map/ppermute | solution.py:121
  37.8 1.9 %collective-permute-done.6 = bf16[3,256,128]{2,1,0:T(8,128)(2,1)S(1)} collective-permute-done((bf16[3,256,128]{2,1,0:T(8,128)(2,1)}, bf16[3,256,128]{2,1,0:T(8,128)(2,1)S(1)}, u32[]{:S(2)}, u32[]{:S(2)}) %collective-permute-start.6) | collective-permute-done | bytes 196640 | tf_op jit(solution)/shard_map/ppermute | solution.py:121
  39.7 5.7 %collective-permute-done.7 = bf16[1,432,384]{2,1,0:T(8,128)(2,1)S(1)} collective-permute-done((bf16[1,432,384]{2,1,0:T(8,128)(2,1)S(1)}, bf16[1,432,384]{2,1,0:T(8,128)(2,1)S(1)}, u32[]{:S(2)}, u32[]{:S(2)}) %collective-permute-start.7) | collective-permute-done | bytes 331808 | tf_op jit(solution)/shard_map/ppermute | solution.py:121
  45.4 1.6 %collective-permute-start.10 = (bf16[400,128]{1,0:T(8,128)(2,1)S(1)}, bf16[400,128]{1,0:T(8,128)(2,1)S(1)}, u32[]{:S(2)}, u32[]{:S(2)}) collective-permute-start(bf16[400,128]{1,0:T(8,128)(2,1)S(1)} %copy-done.8), channel_id=1, source_target_pairs={{0,8},{1,9},{2,10},{3,11},{4,12},{5,13},{6,14},{7,15},{8,0},{9,1},... | collective-permute-start | bytes 307208 | tf_op jit(solution)/shard_map/ppermute | solution.py:121
  47.0 2.5 %collective-permute-start.11 = (bf16[400,128]{1,0:T(8,128)(2,1)S(1)}, bf16[400,128]{1,0:T(8,128)(2,1)S(1)}, u32[]{:S(2)}, u32[]{:S(2)}) collective-permute-start(bf16[400,128]{1,0:T(8,128)(2,1)S(1)} %copy-done.7), channel_id=1, source_target_pairs={{0,4},{1,5},{2,6},{3,7},{4,0},{5,1},{6,2},{7,3},{8,12},{9,13},{10,... | collective-permute-start | bytes 307208 | tf_op jit(solution)/shard_map/ppermute | solution.py:121
  49.8 0.6 collective-permute-start.9
  50.6 1.6 %collective-permute-start.16 = (bf16[3,432,384]{2,1,0:T(8,128)(2,1)S(1)}, bf16[3,432,384]{2,1,0:T(8,128)(2,1)S(1)}, u32[]{:S(2)}, u32[]{:S(2)}) collective-permute-start(bf16[3,432,384]{2,1,0:T(8,128)(2,1)S(1)} %pad_maximum_fusion), channel_id=1, source_target_pairs={{0,2},{1,17},{2,0},{3,19},{4,6},{5,21},{6,4},{7,23},{8,10},{9,25},... | collective-permute-start | bytes 2985992 | tf_op jit(solution)/shard_map/ppermute | solution.py:121
  52.3 5.3 %collective-permute-done.9 = bf16[3,256,128]{2,1,0:T(8,128)(2,1)S(1)} collective-permute-done((bf16[3,256,128]{2,1,0:T(8,128)(2,1)S(1)}, bf16[3,256,128]{2,1,0:T(8,128)(2,1)S(1)}, u32[]{:S(2)}, u32[]{:S(2)}) %collective-permute-start.9) | collective-permute-done | bytes 196640 | tf_op jit(solution)/shard_map/ppermute | solution.py:121
  58.0 1.5 %attend.2.refs_0_ = bf16[3,128,128]{2,1,0:T(8,128)(2,1)S(1)} custom-call(bf16[8,3,256,128]{3,2,1,0:T(8,128)(2,1)S(1)} %slice_dynamic-update-slice_fusion.blocks, bf16[400,128]{1,0:T(8,128)(2,1)S(1)} %copy-done.4), custom_call_target="tpu_custom_call" | custom-call | flops 500000000 | bytes 1048576 | tf_op jit(solution)/shard_map/attend/pallas_call | solution.py:308
  59.5 2.8 %attend.3 = (bf16[3,128,128]{2,1,0:T(8,128)(2,1)S(1)}, bf16[3,128,128]{2,1,0:T(8,128)(2,1)S(1)}, bf16[3,128,128]{2,1,0:T(8,128)(2,1)S(1)}) custom-call(bf16[8,3,256,128]{3,2,1,0:T(8,128)(2,1)S(1)} %slice_dynamic-update-slice_fusion.blocks, bf16[400,128]{1,0:T(8,128)(2,1)S(1)} %collective-permute-done.10.refs_0_, ...), custom_call_target="tpu_custom_call" | custom-call | flops 500000000 | bytes 1048576 | tf_op jit(solution)/shard_map/attend/pallas_call | solution.py:308
  62.5 2.3 %collective-permute-done.17 = bf16[1,432,384]{2,1,0:T(8,128)(2,1)S(1)} collective-permute-done((bf16[1,432,384]{2,1,0:T(8,128)(2,1)S(1)}, bf16[1,432,384]{2,1,0:T(8,128)(2,1)S(1)}, u32[]{:S(2)}, u32[]{:S(2)}) %collective-permute-start.17) | collective-permute-done | bytes 331808 | tf_op jit(solution)/shard_map/ppermute | solution.py:121
  65.6 1.6 %collective-permute-start.19 = (bf16[3,432,384]{2,1,0:T(8,128)(2,1)S(1)}, bf16[3,432,384]{2,1,0:T(8,128)(2,1)S(1)}, u32[]{:S(2)}, u32[]{:S(2)}) collective-permute-start(bf16[3,432,384]{2,1,0:T(8,128)(2,1)S(1)} %pad_maximum_fusion.1), channel_id=1, source_target_pairs={{0,2},{1,17},{2,0},{3,19},{4,6},{5,21},{6,4},{7,23},{8,10},{9,25},... | collective-permute-start | bytes 2985992 | tf_op jit(solution)/shard_map/ppermute | solution.py:121
  67.5 3.1 %collective-permute-start.15 = (bf16[3,128,128]{2,1,0:T(8,128)(2,1)S(1)}, bf16[3,128,128]{2,1,0:T(8,128)(2,1)S(1)}, u32[]{:S(2)}, u32[]{:S(2)}) collective-permute-start(bf16[3,128,128]{2,1,0:T(8,128)(2,1)S(1)} %get-tuple-element.52), channel_id=1, source_target_pairs={{0,12},{1,13},{2,14},{3,15},{4,8},{5,9},{6,10},{7,11},{8,4},{9,5},... | collective-permute-start | bytes 294920 | tf_op jit(solution)/shard_map/ppermute | solution.py:121
  70.6 0.6 collective-permute-start.14
  71.2 0.7 collective-permute-done.13.refs_1_
  71.9 4.5 %collective-permute-done.15.refs_3_ = bf16[3,128,128]{2,1,0:T(8,128)(2,1)S(1)} collective-permute-done((bf16[3,128,128]{2,1,0:T(8,128)(2,1)S(1)}, bf16[3,128,128]{2,1,0:T(8,128)(2,1)S(1)}, u32[]{:S(2)}, u32[]{:S(2)}) %collective-permute-start.15) | collective-permute-done | bytes 98336 | tf_op jit(solution)/shard_map/ppermute | solution.py:121
  76.4 3.9 %collective-permute-done.14.refs_2_ = bf16[3,128,128]{2,1,0:T(8,128)(2,1)S(1)} collective-permute-done((bf16[3,128,128]{2,1,0:T(8,128)(2,1)S(1)}, bf16[3,128,128]{2,1,0:T(8,128)(2,1)S(1)}, u32[]{:S(2)}, u32[]{:S(2)}) %collective-permute-start.14) | collective-permute-done | bytes 98336 | tf_op jit(solution)/shard_map/ppermute | solution.py:121
  80.3 2.1 %gather.1 = (bf16[768,768]{1,0:T(8,128)(2,1)S(1)}, bf16[768,3072]{1,0:T(8,128)(2,1)S(1)}, bf16[3072,768]{1,0:T(8,128)(2,1)S(1)}) custom-call(bf16[192,768]{1,0:T(8,128)(2,1)S(1)} %copy-done.2, bf16[192,3072]{1,0:T(8,128)(2,1)S(1)} %copy-done, bf16[768,768]{1,0:T(8,128)(2,1)S(1)} %copy-done.1, ...), custom_call_target="tpu_custom_call" | custom-call | bytes 12582912 | tf_op jit(solution)/shard_map/gather/pallas_call | solution.py:402
  82.8 5.0 %feed.1 = (bf16[256,768]{1,0:T(8,128)(2,1)}, bf16[768,768]{1,0:T(8,128)(2,1)S(1)}, bf16[768,3072]{1,0:T(8,128)(2,1)S(1)}, bf16[3072,768]{1,0:T(8,128)(2,1)S(1)}) custom-call(f32[1,768]{1,0:T(1,128)S(1)} %broadcast_in_dim.3.gain, bf16[256,768]{1,0:T(8,128)(2,1)S(1)} %copy-done.3, ...), custom_call_target="tpu_custom_call", output_to_operand_aliasing={{1}: (6, {}), {2}: (7, {}), {3}: (8, {})} | custom-call | flops 3000000000 | bytes 12582912 | tf_op jit(solution)/shard_map/feed/pallas_call | solution.py:461
  (53 shorter events, 3.0 us)
Async XLA Ops:
  3.5 20.1 %collective-permute-start.2 = (bf16[1,432,384]{2,1,0:T(8,128)(2,1)}, bf16[1,432,384]{2,1,0:T(8,128)(2,1)S(1)}, u32[]{:S(2)}, u32[]{:S(2)}) collective-permute-start(bf16[1,432,384]{2,1,0:T(8,128)(2,1)} %get-tuple-element.36), channel_id=1, source_target_pairs={{0,8},{1,9},{2,10},{3,11},{4,12},{5,13},{6,14},{7,15},{8,0},{9,1},... | collective-permute-start | bytes 995336 | tf_op jit(solution)/shard_map/ppermute | solution.py:121
  7.6 17.8 %collective-permute-start.1 = (bf16[1,432,384]{2,1,0:T(8,128)(2,1)}, bf16[1,432,384]{2,1,0:T(8,128)(2,1)S(1)}, u32[]{:S(2)}, u32[]{:S(2)}) collective-permute-start(bf16[1,432,384]{2,1,0:T(8,128)(2,1)} %get-tuple-element.36), channel_id=1, source_target_pairs={{0,4},{1,5},{2,6},{3,7},{4,0},{5,1},{6,2},{7,3},{8,12},{9,13},{10,... | collective-permute-start | bytes 995336 | tf_op jit(solution)/shard_map/ppermute | solution.py:121
  9.2 22.6 %collective-permute-start = (bf16[3,256,128]{2,1,0:T(8,128)(2,1)}, bf16[3,256,128]{2,1,0:T(8,128)(2,1)S(1)}, u32[]{:S(2)}, u32[]{:S(2)}) collective-permute-start(bf16[3,256,128]{2,1,0:T(8,128)(2,1)} %get-tuple-element.35), channel_id=1, source_target_pairs={{0,4},{1,5},{2,6},{3,7},{4,0},{5,1},{6,2},{7,3},{8,12},{9,13},{10,... | collective-permute-start | bytes 589832 | tf_op jit(solution)/shard_map/ppermute | solution.py:121
  9.6 23.8 %collective-permute-start.4 = (bf16[3,256,128]{2,1,0:T(8,128)(2,1)}, bf16[3,256,128]{2,1,0:T(8,128)(2,1)S(1)}, u32[]{:S(2)}, u32[]{:S(2)}) collective-permute-start(bf16[3,256,128]{2,1,0:T(8,128)(2,1)} %get-tuple-element.37), channel_id=1, source_target_pairs={{0,12},{1,13},{2,14},{3,15},{4,8},{5,9},{6,10},{7,11},{8,4},{9,5},... | collective-permute-start | bytes 589832 | tf_op jit(solution)/shard_map/ppermute | solution.py:121
  11.0 28.7 %collective-permute-start.6 = (bf16[3,256,128]{2,1,0:T(8,128)(2,1)}, bf16[3,256,128]{2,1,0:T(8,128)(2,1)S(1)}, u32[]{:S(2)}, u32[]{:S(2)}) collective-permute-start(bf16[3,256,128]{2,1,0:T(8,128)(2,1)} %get-tuple-element.38), channel_id=1, source_target_pairs={{0,8},{1,9},{2,10},{3,11},{4,12},{5,13},{6,14},{7,15},{8,0},{9,1},... | collective-permute-start | bytes 589832 | tf_op jit(solution)/shard_map/ppermute | solution.py:121
  23.6 27.0 %collective-permute-start.8 = (bf16[3,256,128]{2,1,0:T(8,128)(2,1)}, bf16[3,256,128]{2,1,0:T(8,128)(2,1)S(1)}, u32[]{:S(2)}, u32[]{:S(2)}) collective-permute-start(bf16[3,256,128]{2,1,0:T(8,128)(2,1)} %get-tuple-element.34), channel_id=1, source_target_pairs={{0,16},{1,17},{2,18},{3,19},{4,20},{5,21},{6,22},{7,23},{8,24},{9,... | collective-permute-start | bytes 589832 | tf_op jit(solution)/shard_map/ppermute | solution.py:121
  25.5 19.9 %copy-start.8 = (bf16[400,128]{1,0:T(8,128)(2,1)S(1)}, bf16[400,128]{1,0:T(8,128)(2,1)}, u32[]{:S(2)}) copy-start(bf16[400,128]{1,0:T(8,128)(2,1)} %get-tuple-element.47) | copy-start | bytes 307204
  25.5 21.4 %copy-start.7 = (bf16[400,128]{1,0:T(8,128)(2,1)S(1)}, bf16[400,128]{1,0:T(8,128)(2,1)}, u32[]{:S(2)}) copy-start(bf16[400,128]{1,0:T(8,128)(2,1)} %get-tuple-element.48) | copy-start | bytes 307204
  25.5 23.9 %copy-start.6 = (bf16[400,128]{1,0:T(8,128)(2,1)S(1)}, bf16[400,128]{1,0:T(8,128)(2,1)}, u32[]{:S(2)}) copy-start(bf16[400,128]{1,0:T(8,128)(2,1)} %get-tuple-element.49) | copy-start | bytes 307204
  25.5 24.2 %collective-permute-start.3 = (bf16[2,432,384]{2,1,0:T(8,128)(2,1)S(1)}, bf16[2,432,384]{2,1,0:T(8,128)(2,1)S(1)}, u32[]{:S(2)}, u32[]{:S(2)}) collective-permute-start(bf16[2,432,384]{2,1,0:T(8,128)(2,1)S(1)} %pad_maximum_fusion.2), channel_id=1, source_target_pairs={{0,16},{1,3},{2,18},{3,1},{4,20},{5,7},{6,22},{7,5},{8,24},{9,11},... | collective-permute-start | bytes 1990664 | tf_op jit(solution)/shard_map/ppermute | solution.py:121
  33.5 15.9 %collective-permute-start.5 = (bf16[2,3,256,128]{3,2,1,0:T(8,128)(2,1)S(1)}, bf16[2,3,256,128]{3,2,1,0:T(8,128)(2,1)S(1)}, u32[]{:S(2)}, u32[]{:S(2)}) collective-permute-start(bf16[2,3,256,128]{3,2,1,0:T(8,128)(2,1)S(1)} %pad_maximum_fusion.3), channel_id=1, source_target_pairs={{0,16},{1,17},{2,18},{3,19},{4,20},{5,21},{6,22},{7,23},{8,24},{9,... | collective-permute-start | bytes 1179656 | tf_op jit(solution)/shard_map/ppermute | solution.py:121
  35.1 10.3 %collective-permute-start.7 = (bf16[1,432,384]{2,1,0:T(8,128)(2,1)S(1)}, bf16[1,432,384]{2,1,0:T(8,128)(2,1)S(1)}, u32[]{:S(2)}, u32[]{:S(2)}) collective-permute-start(bf16[1,432,384]{2,1,0:T(8,128)(2,1)S(1)} %collective-permute-done.2), channel_id=1, source_target_pairs={{0,4},{1,5},{2,6},{3,7},{4,0},{5,1},{6,2},{7,3},{8,12},{9,13},{10,... | collective-permute-start | bytes 995336 | tf_op jit(solution)/shard_map/ppermute | solution.py:121
  45.4 14.1 %collective-permute-start.10 = (bf16[400,128]{1,0:T(8,128)(2,1)S(1)}, bf16[400,128]{1,0:T(8,128)(2,1)S(1)}, u32[]{:S(2)}, u32[]{:S(2)}) collective-permute-start(bf16[400,128]{1,0:T(8,128)(2,1)S(1)} %copy-done.8), channel_id=1, source_target_pairs={{0,8},{1,9},{2,10},{3,11},{4,12},{5,13},{6,14},{7,15},{8,0},{9,1},... | collective-permute-start | bytes 307208 | tf_op jit(solution)/shard_map/ppermute | solution.py:121
  47.0 12.5 %collective-permute-start.11 = (bf16[400,128]{1,0:T(8,128)(2,1)S(1)}, bf16[400,128]{1,0:T(8,128)(2,1)S(1)}, u32[]{:S(2)}, u32[]{:S(2)}) collective-permute-start(bf16[400,128]{1,0:T(8,128)(2,1)S(1)} %copy-done.7), channel_id=1, source_target_pairs={{0,4},{1,5},{2,6},{3,7},{4,0},{5,1},{6,2},{7,3},{8,12},{9,13},{10,... | collective-permute-start | bytes 307208 | tf_op jit(solution)/shard_map/ppermute | solution.py:121
  49.5 10.0 %collective-permute-start.12 = (bf16[400,128]{1,0:T(8,128)(2,1)S(1)}, bf16[400,128]{1,0:T(8,128)(2,1)S(1)}, u32[]{:S(2)}, u32[]{:S(2)}) collective-permute-start(bf16[400,128]{1,0:T(8,128)(2,1)S(1)} %copy-done.6), channel_id=1, source_target_pairs={{0,12},{1,13},{2,14},{3,15},{4,8},{5,9},{6,10},{7,11},{8,4},{9,5},... | collective-permute-start | bytes 307208 | tf_op jit(solution)/shard_map/ppermute | solution.py:121
  49.8 7.8 %collective-permute-start.9 = (bf16[3,256,128]{2,1,0:T(8,128)(2,1)S(1)}, bf16[3,256,128]{2,1,0:T(8,128)(2,1)S(1)}, u32[]{:S(2)}, u32[]{:S(2)}) collective-permute-start(bf16[3,256,128]{2,1,0:T(8,128)(2,1)S(1)} %collective-permute-done.6), channel_id=1, source_target_pairs={{0,16},{1,17},{2,18},{3,19},{4,20},{5,21},{6,22},{7,23},{8,24},{9,... | collective-permute-start | bytes 589832 | tf_op jit(solution)/shard_map/ppermute | solution.py:121
  50.5 7.5 %copy-start.4 = (bf16[400,128]{1,0:T(8,128)(2,1)S(1)}, bf16[400,128]{1,0:T(8,128)(2,1)}, u32[]{:S(2)}) copy-start(bf16[400,128]{1,0:T(8,128)(2,1)} %get-tuple-element.46.refs_0_) | copy-start | bytes 307204
  50.6 14.3 %collective-permute-start.16 = (bf16[3,432,384]{2,1,0:T(8,128)(2,1)S(1)}, bf16[3,432,384]{2,1,0:T(8,128)(2,1)S(1)}, u32[]{:S(2)}, u32[]{:S(2)}) collective-permute-start(bf16[3,432,384]{2,1,0:T(8,128)(2,1)S(1)} %pad_maximum_fusion), channel_id=1, source_target_pairs={{0,2},{1,17},{2,0},{3,19},{4,6},{5,21},{6,4},{7,23},{8,10},{9,25},... | collective-permute-start | bytes 2985992 | tf_op jit(solution)/shard_map/ppermute | solution.py:121
  57.6 7.1 %collective-permute-start.17 = (bf16[1,432,384]{2,1,0:T(8,128)(2,1)S(1)}, bf16[1,432,384]{2,1,0:T(8,128)(2,1)S(1)}, u32[]{:S(2)}, u32[]{:S(2)}) collective-permute-start(bf16[1,432,384]{2,1,0:T(8,128)(2,1)S(1)} %slice.11), channel_id=1, source_target_pairs={{0,4},{1,5},{2,6},{3,7},{4,0},{5,1},{6,2},{7,3},{8,12},{9,13},{10,... | collective-permute-start | bytes 995336 | tf_op jit(solution)/shard_map/ppermute | solution.py:121
  65.1 15.2 %copy-start.5 = (f32[768]{0:T(1024)S(1)}, f32[768]{0:T(1024)}, u32[]{:S(2)}) copy-start(f32[768]{0:T(1024)} %param.15) | copy-start | bytes 9220
  65.1 15.2 %copy-start = (bf16[192,3072]{1,0:T(8,128)(2,1)S(1)}, bf16[192,3072]{1,0:T(8,128)(2,1)}, u32[]{:S(2)}) copy-start(bf16[192,3072]{1,0:T(8,128)(2,1)} %up_w.3) | copy-start | bytes 3538948
  65.1 15.2 %copy-start.1 = (bf16[768,768]{1,0:T(8,128)(2,1)S(1)}, bf16[768,768]{1,0:T(8,128)(2,1)}, u32[]{:S(2)}) copy-start(bf16[768,768]{1,0:T(8,128)(2,1)} %down_w.3) | copy-start | bytes 3538948
  65.1 15.2 %copy-start.2 = (bf16[192,768]{1,0:T(8,128)(2,1)S(1)}, bf16[192,768]{1,0:T(8,128)(2,1)}, u32[]{:S(2)}) copy-start(bf16[192,768]{1,0:T(8,128)(2,1)} %out_w.3) | copy-start | bytes 884740
  65.3 15.0 %collective-permute-start.18 = (bf16[9,432,384]{2,1,0:T(8,128)(2,1)S(1)}, bf16[9,432,384]{2,1,0:T(8,128)(2,1)S(1)}, u32[]{:S(2)}, u32[]{:S(2)}) collective-permute-start(bf16[9,432,384]{2,1,0:T(8,128)(2,1)S(1)} %constant_dynamic-update-slice_fusion.2.early), channel_id=1, source_target_pairs={{0,1},{1,0},{2,3},{3,2},{4,5},{5,4},{6,7},{7,6},{8,9},{9,8},{10,11... | collective-permute-start | bytes 8957960 | tf_op jit(solution)/shard_map/ppermute | solution.py:121
  65.6 14.7 %collective-permute-start.19 = (bf16[3,432,384]{2,1,0:T(8,128)(2,1)S(1)}, bf16[3,432,384]{2,1,0:T(8,128)(2,1)S(1)}, u32[]{:S(2)}, u32[]{:S(2)}) collective-permute-start(bf16[3,432,384]{2,1,0:T(8,128)(2,1)S(1)} %pad_maximum_fusion.1), channel_id=1, source_target_pairs={{0,2},{1,17},{2,0},{3,19},{4,6},{5,21},{6,4},{7,23},{8,10},{9,25},... | collective-permute-start | bytes 2985992 | tf_op jit(solution)/shard_map/ppermute | solution.py:121
  67.2 4.7 %collective-permute-start.13 = (bf16[3,128,128]{2,1,0:T(8,128)(2,1)S(1)}, bf16[3,128,128]{2,1,0:T(8,128)(2,1)S(1)}, u32[]{:S(2)}, u32[]{:S(2)}) collective-permute-start(bf16[3,128,128]{2,1,0:T(8,128)(2,1)S(1)} %get-tuple-element.50), channel_id=1, source_target_pairs={{0,4},{1,5},{2,6},{3,7},{4,0},{5,1},{6,2},{7,3},{8,12},{9,13},{10,... | collective-permute-start | bytes 294920 | tf_op jit(solution)/shard_map/ppermute | solution.py:121
  67.5 8.8 %collective-permute-start.15 = (bf16[3,128,128]{2,1,0:T(8,128)(2,1)S(1)}, bf16[3,128,128]{2,1,0:T(8,128)(2,1)S(1)}, u32[]{:S(2)}, u32[]{:S(2)}) collective-permute-start(bf16[3,128,128]{2,1,0:T(8,128)(2,1)S(1)} %get-tuple-element.52), channel_id=1, source_target_pairs={{0,12},{1,13},{2,14},{3,15},{4,8},{5,9},{6,10},{7,11},{8,4},{9,5},... | collective-permute-start | bytes 294920 | tf_op jit(solution)/shard_map/ppermute | solution.py:121
  70.6 9.6 %collective-permute-start.14 = (bf16[3,128,128]{2,1,0:T(8,128)(2,1)S(1)}, bf16[3,128,128]{2,1,0:T(8,128)(2,1)S(1)}, u32[]{:S(2)}, u32[]{:S(2)}) collective-permute-start(bf16[3,128,128]{2,1,0:T(8,128)(2,1)S(1)} %get-tuple-element.51), channel_id=1, source_target_pairs={{0,8},{1,9},{2,10},{3,11},{4,12},{5,13},{6,14},{7,15},{8,0},{9,1},... | collective-permute-start | bytes 294920 | tf_op jit(solution)/shard_map/ppermute | solution.py:121
  80.2 2.6 %collective-permute-start.20 = (bf16[3,432,384]{2,1,0:T(8,128)(2,1)S(1)}, bf16[3,432,384]{2,1,0:T(8,128)(2,1)S(1)}, u32[]{:S(2)}, u32[]{:S(2)}) collective-permute-start(bf16[3,432,384]{2,1,0:T(8,128)(2,1)S(1)} %collective-permute-done.19.late), channel_id=1, source_target_pairs={{0,1},{1,0},{2,3},{3,2},{4,5},{5,4},{6,7},{7,6},{8,9},{9,8},{10,11... | collective-permute-start | bytes 2985992 | tf_op jit(solution)/shard_map/ppermute | solution.py:121
  80.3 2.6 %copy-start.3 = (bf16[256,768]{1,0:T(8,128)(2,1)S(1)}, bf16[256,768]{1,0:T(8,128)(2,1)}, u32[]{:S(2)}) copy-start(bf16[256,768]{1,0:T(8,128)(2,1)} %surface.1) | copy-start | bytes 1179652

commit v6 on v5

--- a/solution.py
+++ b/solution.py
@@ -504,7 +504,7 @@
     more12 = sent(jnp.concatenate([first12, w12[:1]]), plane_second)
     first12, far13, near[2], w3 = lax.optimization_barrier((first12, far13, near[2], w3))
     far[1], far[3] = far13[0], far13[1]
-    away = (2, 1, 3)
+    away = (1, 3, 2)
     for s in away:
         q[s] = sent(q_slots[s], across_head(s))
     more3 = sent(first12[1:], across_head(1))

time: 88.1 us -> 87.6 us (level)
  transfers between devices with their start and end apart: 21 -> 21, of which waited for: 12 -> 13; matrix products, arithmetic and copies ran while one was open for 2% -> 2% of each run, Pallas kernels for 7% -> 8%
where the time goes in v6:
time: 87.6 us; the launch traced here: 87.4 us
  waiting for transfers between devices  41.4 us (47%)
  starting transfers between devices  28.4 us (32%)
  Pallas kernels  14.4 us (16%)
  local copies, waits for them, and re-layouts  1.73 us (2%)
  between operations  1.12 us (1%)
    ppermute x21, waiting for transfers between devices, sent(): lax.ppermute(value, AXES, [(flat(*d), flat(*route(*d))) for d in DEVICES])  41.4 us
    ppermute x21, starting transfers between devices, sent(): lax.ppermute(value, AXES, [(flat(*d), flat(*route(*d))) for d in DEVICES])  28.4 us
    pallas_call x1, Pallas kernels, fed(): pl.pallas_call(feed_kernel, out_shape=[jax.ShapeDtypeStruct(v.shape, jnp....  4.96 us
    pallas_call x2, Pallas kernels, attended(): pl.pallas_call(attend_kernel, out_shape=[made] * len(queries), in_specs=[...  4.52 us
    pallas_call x1, Pallas kernels, packed(): pl.pallas_call(pack_kernel, out_shape=[made(kv_shape)] * ZS + [made((q_ro...  2.84 us
    pallas_call x1, Pallas kernels, gathered(): pl.pallas_call(gather_kernel, out_shape=[made(width, width), made(width,...  2.06 us
  transfers between devices with their start and end apart: 21, of which 13 were waited for; matrix products, arithmetic and copies ran while one was open for 2% of the time, Pallas kernels for 8%

profile of v6, /device:TPU:0, one launch (start us, length us, event | category | flops | bytes accessed | tf_op | source)
XLA Modules:
  0.0 87.4 jit_solution(17519344736244646568)
XLA Ops:
  0.7 2.8 %pack_heads.1 = (bf16[3,256,128]{2,1,0:T(8,128)(2,1)}, bf16[3,256,128]{2,1,0:T(8,128)(2,1)}, bf16[3,256,128]{2,1,0:T(8,128)(2,1)}, bf16[3,256,128]{2,1,0:T(8,128...) custom-call(s32[1,4]{1,0:T(1,128)} %listed_hbm.1, ...), custom_call_target="tpu_custom_call" | custom-call | bytes 4194304 | tf_op jit(solution)/shard_map/pack_heads/pallas_call | solution.py:228
  3.5 4.1 %collective-permute-start.2 = (bf16[1,432,384]{2,1,0:T(8,128)(2,1)}, bf16[1,432,384]{2,1,0:T(8,128)(2,1)S(1)}, u32[]{:S(2)}, u32[]{:S(2)}) collective-permute-start(bf16[1,432,384]{2,1,0:T(8,128)(2,1)} %get-tuple-element.36), channel_id=1, source_target_pairs={{0,8},{1,9},{2,10},{3,11},{4,12},{5,13},{6,14},{7,15},{8,0},{9,1},... | collective-permute-start | bytes 995336 | tf_op jit(solution)/shard_map/ppermute | solution.py:121
  7.6 1.6 %collective-permute-start.1 = (bf16[1,432,384]{2,1,0:T(8,128)(2,1)}, bf16[1,432,384]{2,1,0:T(8,128)(2,1)S(1)}, u32[]{:S(2)}, u32[]{:S(2)}) collective-permute-start(bf16[1,432,384]{2,1,0:T(8,128)(2,1)} %get-tuple-element.36), channel_id=1, source_target_pairs={{0,4},{1,5},{2,6},{3,7},{4,0},{5,1},{6,2},{7,3},{8,12},{9,13},{10,... | collective-permute-start | bytes 995336 | tf_op jit(solution)/shard_map/ppermute | solution.py:121
  9.6 1.3 %collective-permute-start.4 = (bf16[3,256,128]{2,1,0:T(8,128)(2,1)}, bf16[3,256,128]{2,1,0:T(8,128)(2,1)S(1)}, u32[]{:S(2)}, u32[]{:S(2)}) collective-permute-start(bf16[3,256,128]{2,1,0:T(8,128)(2,1)} %get-tuple-element.37), channel_id=1, source_target_pairs={{0,12},{1,13},{2,14},{3,15},{4,8},{5,9},{6,10},{7,11},{8,4},{9,5},... | collective-permute-start | bytes 589832 | tf_op jit(solution)/shard_map/ppermute | solution.py:121
  11.0 1.7 %collective-permute-start.6 = (bf16[3,256,128]{2,1,0:T(8,128)(2,1)}, bf16[3,256,128]{2,1,0:T(8,128)(2,1)S(1)}, u32[]{:S(2)}, u32[]{:S(2)}) collective-permute-start(bf16[3,256,128]{2,1,0:T(8,128)(2,1)} %get-tuple-element.38), channel_id=1, source_target_pairs={{0,8},{1,9},{2,10},{3,11},{4,12},{5,13},{6,14},{7,15},{8,0},{9,1},... | collective-permute-start | bytes 589832 | tf_op jit(solution)/shard_map/ppermute | solution.py:121
  12.7 10.9 %collective-permute-done.2 = bf16[1,432,384]{2,1,0:T(8,128)(2,1)S(1)} collective-permute-done((bf16[1,432,384]{2,1,0:T(8,128)(2,1)}, bf16[1,432,384]{2,1,0:T(8,128)(2,1)S(1)}, u32[]{:S(2)}, u32[]{:S(2)}) %collective-permute-start.2) | collective-permute-done | bytes 331808 | tf_op jit(solution)/shard_map/ppermute | solution.py:121
  23.6 1.8 %collective-permute-start.8 = (bf16[3,256,128]{2,1,0:T(8,128)(2,1)}, bf16[3,256,128]{2,1,0:T(8,128)(2,1)S(1)}, u32[]{:S(2)}, u32[]{:S(2)}) collective-permute-start(bf16[3,256,128]{2,1,0:T(8,128)(2,1)} %get-tuple-element.34), channel_id=1, source_target_pairs={{0,16},{1,17},{2,18},{3,19},{4,20},{5,21},{6,22},{7,23},{8,24},{9,... | collective-permute-start | bytes 589832 | tf_op jit(solution)/shard_map/ppermute | solution.py:121
  25.5 0.7 collective-permute-start.3
  26.2 0.9 %bitcast_dynamic-update-slice_fusion.3 = bf16[8,3,256,128]{3,2,1,0:T(8,128)(2,1)S(1)} fusion(bf16[3,256,128]{2,1,0:T(8,128)(2,1)} %get-tuple-element.34), kind=kLoop, calls=%fused_computation.7 | loop fusion | bytes 393216
  27.1 4.6 %collective-permute-done = bf16[3,256,128]{2,1,0:T(8,128)(2,1)S(1)} collective-permute-done((bf16[3,256,128]{2,1,0:T(8,128)(2,1)}, bf16[3,256,128]{2,1,0:T(8,128)(2,1)S(1)}, u32[]{:S(2)}, u32[]{:S(2)}) %collective-permute-start) | collective-permute-done | bytes 196640 | tf_op jit(solution)/shard_map/ppermute | solution.py:121
  31.8 1.7 %collective-permute-done.4 = bf16[3,256,128]{2,1,0:T(8,128)(2,1)S(1)} collective-permute-done((bf16[3,256,128]{2,1,0:T(8,128)(2,1)}, bf16[3,256,128]{2,1,0:T(8,128)(2,1)S(1)}, u32[]{:S(2)}, u32[]{:S(2)}) %collective-permute-start.4) | collective-permute-done | bytes 196640 | tf_op jit(solution)/shard_map/ppermute | solution.py:121
  33.5 1.6 %collective-permute-start.5 = (bf16[2,3,256,128]{3,2,1,0:T(8,128)(2,1)S(1)}, bf16[2,3,256,128]{3,2,1,0:T(8,128)(2,1)S(1)}, u32[]{:S(2)}, u32[]{:S(2)}) collective-permute-start(bf16[2,3,256,128]{3,2,1,0:T(8,128)(2,1)S(1)} %pad_maximum_fusion.3), channel_id=1, source_target_pairs={{0,16},{1,17},{2,18},{3,19},{4,20},{5,21},{6,22},{7,23},{8,24},{9,... | collective-permute-start | bytes 1179656 | tf_op jit(solution)/shard_map/ppermute | solution.py:121
  35.1 2.6 %collective-permute-start.7 = (bf16[1,432,384]{2,1,0:T(8,128)(2,1)S(1)}, bf16[1,432,384]{2,1,0:T(8,128)(2,1)S(1)}, u32[]{:S(2)}, u32[]{:S(2)}) collective-permute-start(bf16[1,432,384]{2,1,0:T(8,128)(2,1)S(1)} %collective-permute-done.2), channel_id=1, source_target_pairs={{0,4},{1,5},{2,6},{3,7},{4,0},{5,1},{6,2},{7,3},{8,12},{9,13},{10,... | collective-permute-start | bytes 995336 | tf_op jit(solution)/shard_map/ppermute | solution.py:121
  37.8 1.9 %collective-permute-done.6 = bf16[3,256,128]{2,1,0:T(8,128)(2,1)S(1)} collective-permute-done((bf16[3,256,128]{2,1,0:T(8,128)(2,1)}, bf16[3,256,128]{2,1,0:T(8,128)(2,1)S(1)}, u32[]{:S(2)}, u32[]{:S(2)}) %collective-permute-start.6) | collective-permute-done | bytes 196640 | tf_op jit(solution)/shard_map/ppermute | solution.py:121
  39.7 5.7 %collective-permute-done.7 = bf16[1,432,384]{2,1,0:T(8,128)(2,1)S(1)} collective-permute-done((bf16[1,432,384]{2,1,0:T(8,128)(2,1)S(1)}, bf16[1,432,384]{2,1,0:T(8,128)(2,1)S(1)}, u32[]{:S(2)}, u32[]{:S(2)}) %collective-permute-start.7) | collective-permute-done | bytes 331808 | tf_op jit(solution)/shard_map/ppermute | solution.py:121
  45.4 3.6 %collective-permute-start.11 = (bf16[400,128]{1,0:T(8,128)(2,1)S(1)}, bf16[400,128]{1,0:T(8,128)(2,1)S(1)}, u32[]{:S(2)}, u32[]{:S(2)}) collective-permute-start(bf16[400,128]{1,0:T(8,128)(2,1)S(1)} %copy-done.7), channel_id=1, source_target_pairs={{0,12},{1,13},{2,14},{3,15},{4,8},{5,9},{6,10},{7,11},{8,4},{9,5},... | collective-permute-start | bytes 307208 | tf_op jit(solution)/shard_map/ppermute | solution.py:121
  49.0 0.6 collective-permute-start.12
  49.5 0.5 collective-permute-start.9
  50.3 1.6 %collective-permute-start.16 = (bf16[3,432,384]{2,1,0:T(8,128)(2,1)S(1)}, bf16[3,432,384]{2,1,0:T(8,128)(2,1)S(1)}, u32[]{:S(2)}, u32[]{:S(2)}) collective-permute-start(bf16[3,432,384]{2,1,0:T(8,128)(2,1)S(1)} %pad_maximum_fusion), channel_id=1, source_target_pairs={{0,2},{1,17},{2,0},{3,19},{4,6},{5,21},{6,4},{7,23},{8,10},{9,25},... | collective-permute-start | bytes 2985992 | tf_op jit(solution)/shard_map/ppermute | solution.py:121
  52.0 5.4 %collective-permute-done.9 = bf16[3,256,128]{2,1,0:T(8,128)(2,1)S(1)} collective-permute-done((bf16[3,256,128]{2,1,0:T(8,128)(2,1)S(1)}, bf16[3,256,128]{2,1,0:T(8,128)(2,1)S(1)}, u32[]{:S(2)}, u32[]{:S(2)}) %collective-permute-start.9) | collective-permute-done | bytes 196640 | tf_op jit(solution)/shard_map/ppermute | solution.py:121
  57.4 0.6 collective-permute-start.17
  58.0 1.5 %attend.2.refs_0_ = bf16[3,128,128]{2,1,0:T(8,128)(2,1)S(1)} custom-call(bf16[8,3,256,128]{3,2,1,0:T(8,128)(2,1)S(1)} %slice_dynamic-update-slice_fusion.blocks, bf16[400,128]{1,0:T(8,128)(2,1)S(1)} %copy-done.4), custom_call_target="tpu_custom_call" | custom-call | flops 500000000 | bytes 1048576 | tf_op jit(solution)/shard_map/attend/pallas_call | solution.py:308
  59.5 3.1 %attend.3 = (bf16[3,128,128]{2,1,0:T(8,128)(2,1)S(1)}, bf16[3,128,128]{2,1,0:T(8,128)(2,1)S(1)}, bf16[3,128,128]{2,1,0:T(8,128)(2,1)S(1)}) custom-call(bf16[8,3,256,128]{3,2,1,0:T(8,128)(2,1)S(1)} %slice_dynamic-update-slice_fusion.blocks, bf16[400,128]{1,0:T(8,128)(2,1)S(1)} %collective-permute-done.10.refs_0_, ...), custom_call_target="tpu_custom_call" | custom-call | flops 500000000 | bytes 1048576 | tf_op jit(solution)/shard_map/attend/pallas_call | solution.py:308
  62.7 1.8 %collective-permute-done.17 = bf16[1,432,384]{2,1,0:T(8,128)(2,1)S(1)} collective-permute-done((bf16[1,432,384]{2,1,0:T(8,128)(2,1)S(1)}, bf16[1,432,384]{2,1,0:T(8,128)(2,1)S(1)}, u32[]{:S(2)}, u32[]{:S(2)}) %collective-permute-start.17) | collective-permute-done | bytes 331808 | tf_op jit(solution)/shard_map/ppermute | solution.py:121
  65.4 1.6 %collective-permute-start.19 = (bf16[3,432,384]{2,1,0:T(8,128)(2,1)S(1)}, bf16[3,432,384]{2,1,0:T(8,128)(2,1)S(1)}, u32[]{:S(2)}, u32[]{:S(2)}) collective-permute-start(bf16[3,432,384]{2,1,0:T(8,128)(2,1)S(1)} %pad_maximum_fusion.1), channel_id=1, source_target_pairs={{0,2},{1,17},{2,0},{3,19},{4,6},{5,21},{6,4},{7,23},{8,10},{9,25},... | collective-permute-start | bytes 2985992 | tf_op jit(solution)/shard_map/ppermute | solution.py:121
  67.0 0.7 collective-permute-start.13
  67.7 3.1 %collective-permute-start.15 = (bf16[3,128,128]{2,1,0:T(8,128)(2,1)S(1)}, bf16[3,128,128]{2,1,0:T(8,128)(2,1)S(1)}, u32[]{:S(2)}, u32[]{:S(2)}) collective-permute-start(bf16[3,128,128]{2,1,0:T(8,128)(2,1)S(1)} %get-tuple-element.52), channel_id=1, source_target_pairs={{0,12},{1,13},{2,14},{3,15},{4,8},{5,9},{6,10},{7,11},{8,4},{9,5},... | collective-permute-start | bytes 294920 | tf_op jit(solution)/shard_map/ppermute | solution.py:121
  70.8 0.8 collective-permute-done.13.refs_1_
  71.6 5.0 %collective-permute-done.15.refs_3_ = bf16[3,128,128]{2,1,0:T(8,128)(2,1)S(1)} collective-permute-done((bf16[3,128,128]{2,1,0:T(8,128)(2,1)S(1)}, bf16[3,128,128]{2,1,0:T(8,128)(2,1)S(1)}, u32[]{:S(2)}, u32[]{:S(2)}) %collective-permute-start.15) | collective-permute-done | bytes 98336 | tf_op jit(solution)/shard_map/ppermute | solution.py:121
  76.7 2.7 %collective-permute-done.14.refs_2_ = bf16[3,128,128]{2,1,0:T(8,128)(2,1)S(1)} collective-permute-done((bf16[3,128,128]{2,1,0:T(8,128)(2,1)S(1)}, bf16[3,128,128]{2,1,0:T(8,128)(2,1)S(1)}, u32[]{:S(2)}, u32[]{:S(2)}) %collective-permute-start.14) | collective-permute-done | bytes 98336 | tf_op jit(solution)/shard_map/ppermute | solution.py:121
  79.8 2.1 %gather.1 = (bf16[768,768]{1,0:T(8,128)(2,1)S(1)}, bf16[768,3072]{1,0:T(8,128)(2,1)S(1)}, bf16[3072,768]{1,0:T(8,128)(2,1)S(1)}) custom-call(bf16[192,768]{1,0:T(8,128)(2,1)S(1)} %copy-done.2, bf16[192,3072]{1,0:T(8,128)(2,1)S(1)} %copy-done, bf16[768,768]{1,0:T(8,128)(2,1)S(1)} %copy-done.1, ...), custom_call_target="tpu_custom_call" | custom-call | bytes 12582912 | tf_op jit(solution)/shard_map/gather/pallas_call | solution.py:402
  82.3 5.0 %feed.1 = (bf16[256,768]{1,0:T(8,128)(2,1)}, bf16[768,768]{1,0:T(8,128)(2,1)S(1)}, bf16[768,3072]{1,0:T(8,128)(2,1)S(1)}, bf16[3072,768]{1,0:T(8,128)(2,1)S(1)}) custom-call(f32[1,768]{1,0:T(1,128)S(1)} %broadcast_in_dim.3.gain, bf16[256,768]{1,0:T(8,128)(2,1)S(1)} %copy-done.3, ...), custom_call_target="tpu_custom_call", output_to_operand_aliasing={{1}: (6, {}), {2}: (7, {}), {3}: (8, {})} | custom-call | flops 3000000000 | bytes 12582912 | tf_op jit(solution)/shard_map/feed/pallas_call | solution.py:461
  (53 shorter events, 2.8 us)
Async XLA Ops:
  3.5 20.1 %collective-permute-start.2 = (bf16[1,432,384]{2,1,0:T(8,128)(2,1)}, bf16[1,432,384]{2,1,0:T(8,128)(2,1)S(1)}, u32[]{:S(2)}, u32[]{:S(2)}) collective-permute-start(bf16[1,432,384]{2,1,0:T(8,128)(2,1)} %get-tuple-element.36), channel_id=1, source_target_pairs={{0,8},{1,9},{2,10},{3,11},{4,12},{5,13},{6,14},{7,15},{8,0},{9,1},... | collective-permute-start | bytes 995336 | tf_op jit(solution)/shard_map/ppermute | solution.py:121
  7.6 17.8 %collective-permute-start.1 = (bf16[1,432,384]{2,1,0:T(8,128)(2,1)}, bf16[1,432,384]{2,1,0:T(8,128)(2,1)S(1)}, u32[]{:S(2)}, u32[]{:S(2)}) collective-permute-start(bf16[1,432,384]{2,1,0:T(8,128)(2,1)} %get-tuple-element.36), channel_id=1, source_target_pairs={{0,4},{1,5},{2,6},{3,7},{4,0},{5,1},{6,2},{7,3},{8,12},{9,13},{10,... | collective-permute-start | bytes 995336 | tf_op jit(solution)/shard_map/ppermute | solution.py:121
  9.2 22.6 %collective-permute-start = (bf16[3,256,128]{2,1,0:T(8,128)(2,1)}, bf16[3,256,128]{2,1,0:T(8,128)(2,1)S(1)}, u32[]{:S(2)}, u32[]{:S(2)}) collective-permute-start(bf16[3,256,128]{2,1,0:T(8,128)(2,1)} %get-tuple-element.35), channel_id=1, source_target_pairs={{0,4},{1,5},{2,6},{3,7},{4,0},{5,1},{6,2},{7,3},{8,12},{9,13},{10,... | collective-permute-start | bytes 589832 | tf_op jit(solution)/shard_map/ppermute | solution.py:121
  9.6 23.8 %collective-permute-start.4 = (bf16[3,256,128]{2,1,0:T(8,128)(2,1)}, bf16[3,256,128]{2,1,0:T(8,128)(2,1)S(1)}, u32[]{:S(2)}, u32[]{:S(2)}) collective-permute-start(bf16[3,256,128]{2,1,0:T(8,128)(2,1)} %get-tuple-element.37), channel_id=1, source_target_pairs={{0,12},{1,13},{2,14},{3,15},{4,8},{5,9},{6,10},{7,11},{8,4},{9,5},... | collective-permute-start | bytes 589832 | tf_op jit(solution)/shard_map/ppermute | solution.py:121
  11.0 28.7 %collective-permute-start.6 = (bf16[3,256,128]{2,1,0:T(8,128)(2,1)}, bf16[3,256,128]{2,1,0:T(8,128)(2,1)S(1)}, u32[]{:S(2)}, u32[]{:S(2)}) collective-permute-start(bf16[3,256,128]{2,1,0:T(8,128)(2,1)} %get-tuple-element.38), channel_id=1, source_target_pairs={{0,8},{1,9},{2,10},{3,11},{4,12},{5,13},{6,14},{7,15},{8,0},{9,1},... | collective-permute-start | bytes 589832 | tf_op jit(solution)/shard_map/ppermute | solution.py:121
  23.6 26.7 %collective-permute-start.8 = (bf16[3,256,128]{2,1,0:T(8,128)(2,1)}, bf16[3,256,128]{2,1,0:T(8,128)(2,1)S(1)}, u32[]{:S(2)}, u32[]{:S(2)}) collective-permute-start(bf16[3,256,128]{2,1,0:T(8,128)(2,1)} %get-tuple-element.34), channel_id=1, source_target_pairs={{0,16},{1,17},{2,18},{3,19},{4,20},{5,21},{6,22},{7,23},{8,24},{9,... | collective-permute-start | bytes 589832 | tf_op jit(solution)/shard_map/ppermute | solution.py:121
  25.5 19.9 %copy-start.8 = (bf16[400,128]{1,0:T(8,128)(2,1)S(1)}, bf16[400,128]{1,0:T(8,128)(2,1)}, u32[]{:S(2)}) copy-start(bf16[400,128]{1,0:T(8,128)(2,1)} %get-tuple-element.47) | copy-start | bytes 307204
  25.5 19.9 %copy-start.7 = (bf16[400,128]{1,0:T(8,128)(2,1)S(1)}, bf16[400,128]{1,0:T(8,128)(2,1)}, u32[]{:S(2)}) copy-start(bf16[400,128]{1,0:T(8,128)(2,1)} %get-tuple-element.48) | copy-start | bytes 307204
  25.5 23.4 %copy-start.6 = (bf16[400,128]{1,0:T(8,128)(2,1)S(1)}, bf16[400,128]{1,0:T(8,128)(2,1)}, u32[]{:S(2)}) copy-start(bf16[400,128]{1,0:T(8,128)(2,1)} %get-tuple-element.49) | copy-start | bytes 307204
  25.5 24.0 %collective-permute-start.3 = (bf16[2,432,384]{2,1,0:T(8,128)(2,1)S(1)}, bf16[2,432,384]{2,1,0:T(8,128)(2,1)S(1)}, u32[]{:S(2)}, u32[]{:S(2)}) collective-permute-start(bf16[2,432,384]{2,1,0:T(8,128)(2,1)S(1)} %pad_maximum_fusion.2), channel_id=1, source_target_pairs={{0,16},{1,3},{2,18},{3,1},{4,20},{5,7},{6,22},{7,5},{8,24},{9,11},... | collective-permute-start | bytes 1990664 | tf_op jit(solution)/shard_map/ppermute | solution.py:121
  33.5 15.5 %collective-permute-start.5 = (bf16[2,3,256,128]{3,2,1,0:T(8,128)(2,1)S(1)}, bf16[2,3,256,128]{3,2,1,0:T(8,128)(2,1)S(1)}, u32[]{:S(2)}, u32[]{:S(2)}) collective-permute-start(bf16[2,3,256,128]{3,2,1,0:T(8,128)(2,1)S(1)} %pad_maximum_fusion.3), channel_id=1, source_target_pairs={{0,16},{1,17},{2,18},{3,19},{4,20},{5,21},{6,22},{7,23},{8,24},{9,... | collective-permute-start | bytes 1179656 | tf_op jit(solution)/shard_map/ppermute | solution.py:121
  35.1 10.3 %collective-permute-start.7 = (bf16[1,432,384]{2,1,0:T(8,128)(2,1)S(1)}, bf16[1,432,384]{2,1,0:T(8,128)(2,1)S(1)}, u32[]{:S(2)}, u32[]{:S(2)}) collective-permute-start(bf16[1,432,384]{2,1,0:T(8,128)(2,1)S(1)} %collective-permute-done.2), channel_id=1, source_target_pairs={{0,4},{1,5},{2,6},{3,7},{4,0},{5,1},{6,2},{7,3},{8,12},{9,13},{10,... | collective-permute-start | bytes 995336 | tf_op jit(solution)/shard_map/ppermute | solution.py:121
  45.4 14.1 %collective-permute-start.10 = (bf16[400,128]{1,0:T(8,128)(2,1)S(1)}, bf16[400,128]{1,0:T(8,128)(2,1)S(1)}, u32[]{:S(2)}, u32[]{:S(2)}) collective-permute-start(bf16[400,128]{1,0:T(8,128)(2,1)S(1)} %copy-done.8), channel_id=1, source_target_pairs={{0,4},{1,5},{2,6},{3,7},{4,0},{5,1},{6,2},{7,3},{8,12},{9,13},{10,... | collective-permute-start | bytes 307208 | tf_op jit(solution)/shard_map/ppermute | solution.py:121
  45.4 14.1 %collective-permute-start.11 = (bf16[400,128]{1,0:T(8,128)(2,1)S(1)}, bf16[400,128]{1,0:T(8,128)(2,1)S(1)}, u32[]{:S(2)}, u32[]{:S(2)}) collective-permute-start(bf16[400,128]{1,0:T(8,128)(2,1)S(1)} %copy-done.7), channel_id=1, source_target_pairs={{0,12},{1,13},{2,14},{3,15},{4,8},{5,9},{6,10},{7,11},{8,4},{9,5},... | collective-permute-start | bytes 307208 | tf_op jit(solution)/shard_map/ppermute | solution.py:121
  49.0 10.5 %collective-permute-start.12 = (bf16[400,128]{1,0:T(8,128)(2,1)S(1)}, bf16[400,128]{1,0:T(8,128)(2,1)S(1)}, u32[]{:S(2)}, u32[]{:S(2)}) collective-permute-start(bf16[400,128]{1,0:T(8,128)(2,1)S(1)} %copy-done.6), channel_id=1, source_target_pairs={{0,8},{1,9},{2,10},{3,11},{4,12},{5,13},{6,14},{7,15},{8,0},{9,1},... | collective-permute-start | bytes 307208 | tf_op jit(solution)/shard_map/ppermute | solution.py:121
  49.5 7.8 %collective-permute-start.9 = (bf16[3,256,128]{2,1,0:T(8,128)(2,1)S(1)}, bf16[3,256,128]{2,1,0:T(8,128)(2,1)S(1)}, u32[]{:S(2)}, u32[]{:S(2)}) collective-permute-start(bf16[3,256,128]{2,1,0:T(8,128)(2,1)S(1)} %collective-permute-done.6), channel_id=1, source_target_pairs={{0,16},{1,17},{2,18},{3,19},{4,20},{5,21},{6,22},{7,23},{8,24},{9,... | collective-permute-start | bytes 589832 | tf_op jit(solution)/shard_map/ppermute | solution.py:121
  50.2 7.8 %copy-start.4 = (bf16[400,128]{1,0:T(8,128)(2,1)S(1)}, bf16[400,128]{1,0:T(8,128)(2,1)}, u32[]{:S(2)}) copy-start(bf16[400,128]{1,0:T(8,128)(2,1)} %get-tuple-element.46.refs_0_) | copy-start | bytes 307204
  50.3 14.3 %collective-permute-start.16 = (bf16[3,432,384]{2,1,0:T(8,128)(2,1)S(1)}, bf16[3,432,384]{2,1,0:T(8,128)(2,1)S(1)}, u32[]{:S(2)}, u32[]{:S(2)}) collective-permute-start(bf16[3,432,384]{2,1,0:T(8,128)(2,1)S(1)} %pad_maximum_fusion), channel_id=1, source_target_pairs={{0,2},{1,17},{2,0},{3,19},{4,6},{5,21},{6,4},{7,23},{8,10},{9,25},... | collective-permute-start | bytes 2985992 | tf_op jit(solution)/shard_map/ppermute | solution.py:121
  57.4 7.1 %collective-permute-start.17 = (bf16[1,432,384]{2,1,0:T(8,128)(2,1)S(1)}, bf16[1,432,384]{2,1,0:T(8,128)(2,1)S(1)}, u32[]{:S(2)}, u32[]{:S(2)}) collective-permute-start(bf16[1,432,384]{2,1,0:T(8,128)(2,1)S(1)} %slice.11), channel_id=1, source_target_pairs={{0,4},{1,5},{2,6},{3,7},{4,0},{5,1},{6,2},{7,3},{8,12},{9,13},{10,... | collective-permute-start | bytes 995336 | tf_op jit(solution)/shard_map/ppermute | solution.py:121
  64.8 14.9 %copy-start.5 = (f32[768]{0:T(1024)S(1)}, f32[768]{0:T(1024)}, u32[]{:S(2)}) copy-start(f32[768]{0:T(1024)} %param.15) | copy-start | bytes 9220
  64.8 14.9 %copy-start = (bf16[192,3072]{1,0:T(8,128)(2,1)S(1)}, bf16[192,3072]{1,0:T(8,128)(2,1)}, u32[]{:S(2)}) copy-start(bf16[192,3072]{1,0:T(8,128)(2,1)} %up_w.3) | copy-start | bytes 3538948
  64.8 14.9 %copy-start.1 = (bf16[768,768]{1,0:T(8,128)(2,1)S(1)}, bf16[768,768]{1,0:T(8,128)(2,1)}, u32[]{:S(2)}) copy-start(bf16[768,768]{1,0:T(8,128)(2,1)} %down_w.3) | copy-start | bytes 3538948
  64.8 14.9 %copy-start.2 = (bf16[192,768]{1,0:T(8,128)(2,1)S(1)}, bf16[192,768]{1,0:T(8,128)(2,1)}, u32[]{:S(2)}) copy-start(bf16[192,768]{1,0:T(8,128)(2,1)} %out_w.3) | copy-start | bytes 884740
  64.9 14.8 %collective-permute-start.18 = (bf16[9,432,384]{2,1,0:T(8,128)(2,1)S(1)}, bf16[9,432,384]{2,1,0:T(8,128)(2,1)S(1)}, u32[]{:S(2)}, u32[]{:S(2)}) collective-permute-start(bf16[9,432,384]{2,1,0:T(8,128)(2,1)S(1)} %constant_dynamic-update-slice_fusion.2.early), channel_id=1, source_target_pairs={{0,1},{1,0},{2,3},{3,2},{4,5},{5,4},{6,7},{7,6},{8,9},{9,8},{10,11... | collective-permute-start | bytes 8957960 | tf_op jit(solution)/shard_map/ppermute | solution.py:121
  65.4 14.3 %collective-permute-start.19 = (bf16[3,432,384]{2,1,0:T(8,128)(2,1)S(1)}, bf16[3,432,384]{2,1,0:T(8,128)(2,1)S(1)}, u32[]{:S(2)}, u32[]{:S(2)}) collective-permute-start(bf16[3,432,384]{2,1,0:T(8,128)(2,1)S(1)} %pad_maximum_fusion.1), channel_id=1, source_target_pairs={{0,2},{1,17},{2,0},{3,19},{4,6},{5,21},{6,4},{7,23},{8,10},{9,25},... | collective-permute-start | bytes 2985992 | tf_op jit(solution)/shard_map/ppermute | solution.py:121
  67.0 4.6 %collective-permute-start.13 = (bf16[3,128,128]{2,1,0:T(8,128)(2,1)S(1)}, bf16[3,128,128]{2,1,0:T(8,128)(2,1)S(1)}, u32[]{:S(2)}, u32[]{:S(2)}) collective-permute-start(bf16[3,128,128]{2,1,0:T(8,128)(2,1)S(1)} %get-tuple-element.50), channel_id=1, source_target_pairs={{0,4},{1,5},{2,6},{3,7},{4,0},{5,1},{6,2},{7,3},{8,12},{9,13},{10,... | collective-permute-start | bytes 294920 | tf_op jit(solution)/shard_map/ppermute | solution.py:121
  67.7 8.9 %collective-permute-start.15 = (bf16[3,128,128]{2,1,0:T(8,128)(2,1)S(1)}, bf16[3,128,128]{2,1,0:T(8,128)(2,1)S(1)}, u32[]{:S(2)}, u32[]{:S(2)}) collective-permute-start(bf16[3,128,128]{2,1,0:T(8,128)(2,1)S(1)} %get-tuple-element.52), channel_id=1, source_target_pairs={{0,12},{1,13},{2,14},{3,15},{4,8},{5,9},{6,10},{7,11},{8,4},{9,5},... | collective-permute-start | bytes 294920 | tf_op jit(solution)/shard_map/ppermute | solution.py:121
  70.8 8.6 %collective-permute-start.14 = (bf16[3,128,128]{2,1,0:T(8,128)(2,1)S(1)}, bf16[3,128,128]{2,1,0:T(8,128)(2,1)S(1)}, u32[]{:S(2)}, u32[]{:S(2)}) collective-permute-start(bf16[3,128,128]{2,1,0:T(8,128)(2,1)S(1)} %get-tuple-element.51), channel_id=1, source_target_pairs={{0,8},{1,9},{2,10},{3,11},{4,12},{5,13},{6,14},{7,15},{8,0},{9,1},... | collective-permute-start | bytes 294920 | tf_op jit(solution)/shard_map/ppermute | solution.py:121
  79.7 2.6 %collective-permute-start.20 = (bf16[3,432,384]{2,1,0:T(8,128)(2,1)S(1)}, bf16[3,432,384]{2,1,0:T(8,128)(2,1)S(1)}, u32[]{:S(2)}, u32[]{:S(2)}) collective-permute-start(bf16[3,432,384]{2,1,0:T(8,128)(2,1)S(1)} %collective-permute-done.19.late), channel_id=1, source_target_pairs={{0,1},{1,0},{2,3},{3,2},{4,5},{5,4},{6,7},{7,6},{8,9},{9,8},{10,11... | collective-permute-start | bytes 2985992 | tf_op jit(solution)/shard_map/ppermute | solution.py:121
  79.7 2.6 %copy-start.3 = (bf16[256,768]{1,0:T(8,128)(2,1)S(1)}, bf16[256,768]{1,0:T(8,128)(2,1)}, u32[]{:S(2)}) copy-start(bf16[256,768]{1,0:T(8,128)(2,1)} %surface.1) | copy-start | bytes 1179652

commit v7 on v6

--- a/solution.py
+++ b/solution.py
@@ -145,41 +145,64 @@
     return lax.optimization_barrier((value,) + earlier)[0]
 
 
-def pack_kernel(listed_hbm, length_hbm, q_hbm, kv_hbm, out_w, up_w, down_w, *refs):
-    kv_slots, q_slots, piece = refs[:ZS], refs[ZS : 2 * ZS], refs[2 * ZS]
-    kv_all, q_all, q_ref, kv_ref, listed, length, sems = refs[2 * ZS + 1 :]
+def cut_kernel(out_w, up_w, down_w, piece, sem):
     x, z, y, c = (lax.axis_index(axis) for axis in AXES)
     p = 2 * x + y
     m = 2 * p + c
     ro, cols = out_w.shape[0] // 4, out_w.shape[1] // 2
     ru, rd = up_w.shape[0], down_w.shape[0] // 8
     rows = [ro, ro + ru, ro + ru + rd]
+    copies = []
+    copies += [
+        pltpu.make_async_copy(
+            out_w.at[pl.ds(pl.multiple_of(p * ro, 16), ro), pl.ds(pl.multiple_of(c * cols, 128), cols)],
+            piece.at[0, pl.ds(0, ro)],
+            sem.at[0],
+        ),
+        pltpu.make_async_copy(
+            up_w.at[:, pl.ds(pl.multiple_of(m * cols, 128), cols)],
+            piece.at[0, pl.ds(rows[0], ru)],
+            sem.at[0],
+        ),
+    ]
+    for side in range(2):
+        copies.append(
+            pltpu.make_async_copy(
+                down_w.at[pl.ds(pl.multiple_of(m * rd, 16), rd), pl.ds(side * cols, cols)],
+                piece.at[0, pl.ds(rows[1 + side], rd)],
+                sem.at[0],
+            )
+        )
+    for copy in copies:
+        copy.start()
+    for copy in copies:
+        copy.wait()
+
+
+def cut_piece(out_weight, up_weight, down_weight):
+    rows = out_weight.shape[0] // 4 + up_weight.shape[0] + down_weight.shape[0] // 4
+    return pl.pallas_call(
+        cut_kernel,
+        out_shape=jax.ShapeDtypeStruct((1, rows, out_weight.shape[1] // 2), jnp.bfloat16),
+        in_specs=[HBM] * 3,
+        out_specs=VMEM,
+        scratch_shapes=[pltpu.SemaphoreType.DMA((1,))],
+        compiler_params=pltpu.CompilerParams(vmem_limit_bytes=58 * MIB),
+        cost_estimate=pl.CostEstimate(flops=0, bytes_accessed=MIB, transcendentals=0),
+        name="cut_piece",
+    )(out_weight, up_weight, down_weight)
+
+
+def pack_kernel(listed_hbm, length_hbm, q_hbm, kv_hbm, *refs):
+    kv_slots, q_slots = refs[:ZS], refs[ZS : 2 * ZS]
+    kv_all, q_all, q_ref, kv_ref, listed, length, sems = refs[2 * ZS :]
+    z = lax.axis_index("head")
     copies = [
         pltpu.make_async_copy(kv_hbm, kv_ref, sems.at[0]),
         pltpu.make_async_copy(q_hbm, q_ref, sems.at[1]),
         pltpu.make_async_copy(listed_hbm, listed, sems.at[3]),
         pltpu.make_async_copy(length_hbm, length, sems.at[4]),
     ]
-    copies += [
-        pltpu.make_async_copy(
-            out_w.at[pl.ds(pl.multiple_of(p * ro, 16), ro), pl.ds(pl.multiple_of(c * cols, 128), cols)],
-            piece.at[0, pl.ds(0, ro)],
-            sems.at[2],
-        ),
-        pltpu.make_async_copy(
-            up_w.at[:, pl.ds(pl.multiple_of(m * cols, 128), cols)],
-            piece.at[0, pl.ds(rows[0], ru)],
-            sems.at[2],
-        ),
-    ]
-    for side in range(2):
-        copies.append(
-            pltpu.make_async_copy(
-                down_w.at[pl.ds(pl.multiple_of(m * rd, 16), rd), pl.ds(side * cols, cols)],
-                piece.at[0, pl.ds(rows[1 + side], rd)],
-                sems.at[2],
-            )
-        )
     for copy in copies:
         copy.start()
     n = q_ref.shape[0] // 2
@@ -215,21 +238,17 @@
         kv_slots[s][...] = kv_all[there]
         q_slots[s][: HZ * n] = q_all[there]
         q_slots[s][HZ * n :] = note
-    for copy in copies[4:]:
-        copy.wait()
-
-
-def packed(listed, length, queries, keys_values, out_weight, up_weight, down_weight):
-    rows, width = queries.shape
-    cols = width // 2
-    piece_rows = out_weight.shape[0] // 4 + up_weight.shape[0] + down_weight.shape[0] // 4
+
+
+def packed(listed, length, queries, keys_values):
+    rows = queries.shape[0]
     kv_shape, q_rows = (HZ, rows, 2 * HD), HZ * rows // 2
     made = lambda shape: jax.ShapeDtypeStruct(shape, jnp.bfloat16)
     outs = pl.pallas_call(
         pack_kernel,
-        out_shape=[made(kv_shape)] * ZS + [made((q_rows + NOTE, 2 * HD))] * ZS + [made((1, piece_rows, cols))],
-        in_specs=[HBM] * 7,
-        out_specs=[VMEM] * (2 * ZS + 1),
+        out_shape=[made(kv_shape)] * ZS + [made((q_rows + NOTE, 2 * HD))] * ZS,
+        in_specs=[HBM] * 4,
+        out_specs=[VMEM] * (2 * ZS),
         scratch_shapes=[
             pltpu.VMEM((ZS,) + kv_shape, jnp.bfloat16),
             pltpu.VMEM((ZS, q_rows, 2 * HD), jnp.bfloat16),
@@ -242,8 +261,8 @@
         compiler_params=pltpu.CompilerParams(vmem_limit_bytes=55 * MIB),
         cost_estimate=pl.CostEstimate(flops=0, bytes_accessed=4 * MIB, transcendentals=0),
         name="pack_heads",
-    )(listed, length, queries, keys_values, out_weight, up_weight, down_weight)
-    return outs[:ZS], outs[ZS : 2 * ZS], outs[2 * ZS]
+    )(listed, length, queries, keys_values)
+    return outs[:ZS], outs[ZS:]
 
 
 def attend_kernel(blocks, *refs):
@@ -485,9 +504,8 @@
     block_lists,
     list_lengths,
 ):
-    kv_slots, q_slots, piece = packed(
-        block_lists, list_lengths, queries, keys_values, out_weight, up_weight, down_weight
-    )
+    piece = cut_piece(out_weight, up_weight, down_weight)
+    kv_slots, q_slots = packed(block_lists, list_lengths, queries, keys_values)
     kv_slots, q_slots = list(kv_slots), list(q_slots)
     near, q, far = {0: kv_slots[0]}, {0: q_slots[0]}, {}
     w12 = jnp.concatenate([sent(piece, across_head(k)) for k in (1, 2)])

time: 87.6 us -> 85.9 us (0.981)
  waiting for transfers between devices: 41.4 us -> 38.4 us
  Pallas kernels: 14.4 us -> 15.7 us
    ppermute x21, waiting for transfers between devices: 41.4 us -> 38.4 us  [sent(): lax.ppermute(value, AXES, [(flat(*d), flat(*route(*d))) for d in DEVICES])]
    pallas_call x0 -> x1, Pallas kernels: none -> 1.74 us  [cut_piece(): pl.pallas_call(cut_kernel, out_shape=jax.ShapeDtypeStruct((1, rows, out_w...]
  transfers between devices with their start and end apart: 21 -> 21, of which waited for: 13 -> 13; matrix products, arithmetic and copies ran while one was open for 2% -> 2% of each run, Pallas kernels for 8% -> 10%
where the time goes in v7:
time: 85.9 us; the launch traced here: 85.7 us
  waiting for transfers between devices  38.4 us (45%)
  starting transfers between devices  28.5 us (33%)
  Pallas kernels  15.7 us (18%)
  local copies, waits for them, and re-layouts  1.73 us (2%)
  between operations  1.13 us (1%)
    ppermute x21, waiting for transfers between devices, sent(): lax.ppermute(value, AXES, [(flat(*d), flat(*route(*d))) for d in DEVICES])  38.4 us
    ppermute x21, starting transfers between devices, sent(): lax.ppermute(value, AXES, [(flat(*d), flat(*route(*d))) for d in DEVICES])  28.5 us
    pallas_call x1, Pallas kernels, fed(): pl.pallas_call(feed_kernel, out_shape=[jax.ShapeDtypeStruct(v.shape, jnp....  5.01 us
    pallas_call x2, Pallas kernels, attended(): pl.pallas_call(attend_kernel, out_shape=[made] * len(queries), in_specs=[...  4.07 us
    pallas_call x1, Pallas kernels, packed(): pl.pallas_call(pack_kernel, out_shape=[made(kv_shape)] * ZS + [made((q_ro...  2.76 us
    pallas_call x1, Pallas kernels, gathered(): pl.pallas_call(gather_kernel, out_shape=[made(width, width), made(width,...  2.06 us
    pallas_call x1, Pallas kernels, cut_piece(): pl.pallas_call(cut_kernel, out_shape=jax.ShapeDtypeStruct((1, rows, out_w...  1.74 us
  transfers between devices with their start and end apart: 21, of which 13 were waited for; matrix products, arithmetic and copies ran while one was open for 2% of the time, Pallas kernels for 10%

profile of v7, /device:TPU:0, one launch (start us, length us, event | category | flops | bytes accessed | tf_op | source)
XLA Modules:
  0.0 85.7 jit_solution(3668287707964771460)
XLA Ops:
  0.0 1.7 %cut_piece.1 = bf16[1,432,384]{2,1,0:T(8,128)(2,1)} custom-call(bf16[192,768]{1,0:T(8,128)(2,1)} %out_w.3, bf16[192,3072]{1,0:T(8,128)(2,1)} %up_w.3, bf16[768,768]{1,0:T(8,128)(2,1)} %down_w.3), custom_call_target="tpu_custom_call" | custom-call | bytes 1048576 | tf_op jit(solution)/shard_map/cut_piece/pallas_call | solution.py:184
  1.8 4.1 %collective-permute-start.2 = (bf16[1,432,384]{2,1,0:T(8,128)(2,1)}, bf16[1,432,384]{2,1,0:T(8,128)(2,1)S(1)}, u32[]{:S(2)}, u32[]{:S(2)}) collective-permute-start(bf16[1,432,384]{2,1,0:T(8,128)(2,1)} %cut_piece.1), channel_id=1, source_target_pairs={{0,8},{1,9},{2,10},{3,11},{4,12},{5,13},{6,14},{7,15},{8,0},{9,1},... | collective-permute-start | bytes 995336 | tf_op jit(solution)/shard_map/ppermute | solution.py:121
  5.9 1.6 %collective-permute-start.1 = (bf16[1,432,384]{2,1,0:T(8,128)(2,1)}, bf16[1,432,384]{2,1,0:T(8,128)(2,1)S(1)}, u32[]{:S(2)}, u32[]{:S(2)}) collective-permute-start(bf16[1,432,384]{2,1,0:T(8,128)(2,1)} %cut_piece.1), channel_id=1, source_target_pairs={{0,4},{1,5},{2,6},{3,7},{4,0},{5,1},{6,2},{7,3},{8,12},{9,13},{10,... | collective-permute-start | bytes 995336 | tf_op jit(solution)/shard_map/ppermute | solution.py:121
  8.1 2.8 %pack_heads.1 = (bf16[3,256,128]{2,1,0:T(8,128)(2,1)}, bf16[3,256,128]{2,1,0:T(8,128)(2,1)}, bf16[3,256,128]{2,1,0:T(8,128)(2,1)}, bf16[3,256,128]{2,1,0:T(8,128...) custom-call(s32[1,4]{1,0:T(1,128)} %listed_hbm.1, ...), custom_call_target="tpu_custom_call" | custom-call | bytes 4194304 | tf_op jit(solution)/shard_map/pack_heads/pallas_call | solution.py:247
  11.4 1.3 %collective-permute-start.4 = (bf16[3,256,128]{2,1,0:T(8,128)(2,1)}, bf16[3,256,128]{2,1,0:T(8,128)(2,1)S(1)}, u32[]{:S(2)}, u32[]{:S(2)}) collective-permute-start(bf16[3,256,128]{2,1,0:T(8,128)(2,1)} %get-tuple-element.35), channel_id=1, source_target_pairs={{0,12},{1,13},{2,14},{3,15},{4,8},{5,9},{6,10},{7,11},{8,4},{9,5},... | collective-permute-start | bytes 589832 | tf_op jit(solution)/shard_map/ppermute | solution.py:121
  12.7 1.7 %collective-permute-start.6 = (bf16[3,256,128]{2,1,0:T(8,128)(2,1)}, bf16[3,256,128]{2,1,0:T(8,128)(2,1)S(1)}, u32[]{:S(2)}, u32[]{:S(2)}) collective-permute-start(bf16[3,256,128]{2,1,0:T(8,128)(2,1)} %get-tuple-element.36), channel_id=1, source_target_pairs={{0,8},{1,9},{2,10},{3,11},{4,12},{5,13},{6,14},{7,15},{8,0},{9,1},... | collective-permute-start | bytes 589832 | tf_op jit(solution)/shard_map/ppermute | solution.py:121
  14.4 7.4 %collective-permute-done.2 = bf16[1,432,384]{2,1,0:T(8,128)(2,1)S(1)} collective-permute-done((bf16[1,432,384]{2,1,0:T(8,128)(2,1)}, bf16[1,432,384]{2,1,0:T(8,128)(2,1)S(1)}, u32[]{:S(2)}, u32[]{:S(2)}) %collective-permute-start.2) | collective-permute-done | bytes 331808 | tf_op jit(solution)/shard_map/ppermute | solution.py:121
  21.8 1.8 %collective-permute-start.8 = (bf16[3,256,128]{2,1,0:T(8,128)(2,1)}, bf16[3,256,128]{2,1,0:T(8,128)(2,1)S(1)}, u32[]{:S(2)}, u32[]{:S(2)}) collective-permute-start(bf16[3,256,128]{2,1,0:T(8,128)(2,1)} %get-tuple-element.33), channel_id=1, source_target_pairs={{0,16},{1,17},{2,18},{3,19},{4,20},{5,21},{6,22},{7,23},{8,24},{9,... | collective-permute-start | bytes 589832 | tf_op jit(solution)/shard_map/ppermute | solution.py:121
  23.8 0.7 collective-permute-start.3
  24.5 0.9 %bitcast_dynamic-update-slice_fusion.3 = bf16[8,3,256,128]{3,2,1,0:T(8,128)(2,1)S(1)} fusion(bf16[3,256,128]{2,1,0:T(8,128)(2,1)} %get-tuple-element.33), kind=kLoop, calls=%fused_computation.7 | loop fusion | bytes 393216
  25.4 4.6 %collective-permute-done = bf16[3,256,128]{2,1,0:T(8,128)(2,1)S(1)} collective-permute-done((bf16[3,256,128]{2,1,0:T(8,128)(2,1)}, bf16[3,256,128]{2,1,0:T(8,128)(2,1)S(1)}, u32[]{:S(2)}, u32[]{:S(2)}) %collective-permute-start) | collective-permute-done | bytes 196640 | tf_op jit(solution)/shard_map/ppermute | solution.py:121
  30.0 1.7 %collective-permute-done.4 = bf16[3,256,128]{2,1,0:T(8,128)(2,1)S(1)} collective-permute-done((bf16[3,256,128]{2,1,0:T(8,128)(2,1)}, bf16[3,256,128]{2,1,0:T(8,128)(2,1)S(1)}, u32[]{:S(2)}, u32[]{:S(2)}) %collective-permute-start.4) | collective-permute-done | bytes 196640 | tf_op jit(solution)/shard_map/ppermute | solution.py:121
  31.8 1.6 %collective-permute-start.5 = (bf16[2,3,256,128]{3,2,1,0:T(8,128)(2,1)S(1)}, bf16[2,3,256,128]{3,2,1,0:T(8,128)(2,1)S(1)}, u32[]{:S(2)}, u32[]{:S(2)}) collective-permute-start(bf16[2,3,256,128]{3,2,1,0:T(8,128)(2,1)S(1)} %pad_maximum_fusion.3), channel_id=1, source_target_pairs={{0,16},{1,17},{2,18},{3,19},{4,20},{5,21},{6,22},{7,23},{8,24},{9,... | collective-permute-start | bytes 1179656 | tf_op jit(solution)/shard_map/ppermute | solution.py:121
  33.3 2.6 %collective-permute-start.7 = (bf16[1,432,384]{2,1,0:T(8,128)(2,1)S(1)}, bf16[1,432,384]{2,1,0:T(8,128)(2,1)S(1)}, u32[]{:S(2)}, u32[]{:S(2)}) collective-permute-start(bf16[1,432,384]{2,1,0:T(8,128)(2,1)S(1)} %collective-permute-done.2), channel_id=1, source_target_pairs={{0,4},{1,5},{2,6},{3,7},{4,0},{5,1},{6,2},{7,3},{8,12},{9,13},{10,... | collective-permute-start | bytes 995336 | tf_op jit(solution)/shard_map/ppermute | solution.py:121
  36.1 1.9 %collective-permute-done.6 = bf16[3,256,128]{2,1,0:T(8,128)(2,1)S(1)} collective-permute-done((bf16[3,256,128]{2,1,0:T(8,128)(2,1)}, bf16[3,256,128]{2,1,0:T(8,128)(2,1)S(1)}, u32[]{:S(2)}, u32[]{:S(2)}) %collective-permute-start.6) | collective-permute-done | bytes 196640 | tf_op jit(solution)/shard_map/ppermute | solution.py:121
  38.0 5.7 %collective-permute-done.7 = bf16[1,432,384]{2,1,0:T(8,128)(2,1)S(1)} collective-permute-done((bf16[1,432,384]{2,1,0:T(8,128)(2,1)S(1)}, bf16[1,432,384]{2,1,0:T(8,128)(2,1)S(1)}, u32[]{:S(2)}, u32[]{:S(2)}) %collective-permute-start.7) | collective-permute-done | bytes 331808 | tf_op jit(solution)/shard_map/ppermute | solution.py:121
  43.6 3.6 %collective-permute-start.11 = (bf16[400,128]{1,0:T(8,128)(2,1)S(1)}, bf16[400,128]{1,0:T(8,128)(2,1)S(1)}, u32[]{:S(2)}, u32[]{:S(2)}) collective-permute-start(bf16[400,128]{1,0:T(8,128)(2,1)S(1)} %copy-done.7), channel_id=1, source_target_pairs={{0,12},{1,13},{2,14},{3,15},{4,8},{5,9},{6,10},{7,11},{8,4},{9,5},... | collective-permute-start | bytes 307208 | tf_op jit(solution)/shard_map/ppermute | solution.py:121
  47.2 0.6 collective-permute-start.12
  48.5 1.6 %collective-permute-start.16 = (bf16[3,432,384]{2,1,0:T(8,128)(2,1)S(1)}, bf16[3,432,384]{2,1,0:T(8,128)(2,1)S(1)}, u32[]{:S(2)}, u32[]{:S(2)}) collective-permute-start(bf16[3,432,384]{2,1,0:T(8,128)(2,1)S(1)} %pad_maximum_fusion), channel_id=1, source_target_pairs={{0,2},{1,17},{2,0},{3,19},{4,6},{5,21},{6,4},{7,23},{8,10},{9,25},... | collective-permute-start | bytes 2985992 | tf_op jit(solution)/shard_map/ppermute | solution.py:121
  50.2 5.4 %collective-permute-done.9 = bf16[3,256,128]{2,1,0:T(8,128)(2,1)S(1)} collective-permute-done((bf16[3,256,128]{2,1,0:T(8,128)(2,1)S(1)}, bf16[3,256,128]{2,1,0:T(8,128)(2,1)S(1)}, u32[]{:S(2)}, u32[]{:S(2)}) %collective-permute-start.9) | collective-permute-done | bytes 196640 | tf_op jit(solution)/shard_map/ppermute | solution.py:121
  55.6 0.6 collective-permute-start.17
  56.3 1.4 %attend.2.refs_0_ = bf16[3,128,128]{2,1,0:T(8,128)(2,1)S(1)} custom-call(bf16[8,3,256,128]{3,2,1,0:T(8,128)(2,1)S(1)} %slice_dynamic-update-slice_fusion.blocks, bf16[400,128]{1,0:T(8,128)(2,1)S(1)} %copy-done.4), custom_call_target="tpu_custom_call" | custom-call | flops 500000000 | bytes 1048576 | tf_op jit(solution)/shard_map/attend/pallas_call | solution.py:327
  57.7 2.6 %attend.3 = (bf16[3,128,128]{2,1,0:T(8,128)(2,1)S(1)}, bf16[3,128,128]{2,1,0:T(8,128)(2,1)S(1)}, bf16[3,128,128]{2,1,0:T(8,128)(2,1)S(1)}) custom-call(bf16[8,3,256,128]{3,2,1,0:T(8,128)(2,1)S(1)} %slice_dynamic-update-slice_fusion.blocks, bf16[400,128]{1,0:T(8,128)(2,1)S(1)} %collective-permute-done.10.refs_0_, ...), custom_call_target="tpu_custom_call" | custom-call | flops 500000000 | bytes 1048576 | tf_op jit(solution)/shard_map/attend/pallas_call | solution.py:327
  60.5 2.2 %collective-permute-done.17 = bf16[1,432,384]{2,1,0:T(8,128)(2,1)S(1)} collective-permute-done((bf16[1,432,384]{2,1,0:T(8,128)(2,1)S(1)}, bf16[1,432,384]{2,1,0:T(8,128)(2,1)S(1)}, u32[]{:S(2)}, u32[]{:S(2)}) %collective-permute-start.17) | collective-permute-done | bytes 331808 | tf_op jit(solution)/shard_map/ppermute | solution.py:121
  63.7 1.6 %collective-permute-start.19 = (bf16[3,432,384]{2,1,0:T(8,128)(2,1)S(1)}, bf16[3,432,384]{2,1,0:T(8,128)(2,1)S(1)}, u32[]{:S(2)}, u32[]{:S(2)}) collective-permute-start(bf16[3,432,384]{2,1,0:T(8,128)(2,1)S(1)} %pad_maximum_fusion.1), channel_id=1, source_target_pairs={{0,2},{1,17},{2,0},{3,19},{4,6},{5,21},{6,4},{7,23},{8,10},{9,25},... | collective-permute-start | bytes 2985992 | tf_op jit(solution)/shard_map/ppermute | solution.py:121
  65.2 0.7 collective-permute-start.13
  66.0 3.1 %collective-permute-start.15 = (bf16[3,128,128]{2,1,0:T(8,128)(2,1)S(1)}, bf16[3,128,128]{2,1,0:T(8,128)(2,1)S(1)}, u32[]{:S(2)}, u32[]{:S(2)}) collective-permute-start(bf16[3,128,128]{2,1,0:T(8,128)(2,1)S(1)} %get-tuple-element.50), channel_id=1, source_target_pairs={{0,12},{1,13},{2,14},{3,15},{4,8},{5,9},{6,10},{7,11},{8,4},{9,5},... | collective-permute-start | bytes 294920 | tf_op jit(solution)/shard_map/ppermute | solution.py:121
  69.1 0.8 collective-permute-done.13.refs_1_
  69.9 5.0 %collective-permute-done.15.refs_3_ = bf16[3,128,128]{2,1,0:T(8,128)(2,1)S(1)} collective-permute-done((bf16[3,128,128]{2,1,0:T(8,128)(2,1)S(1)}, bf16[3,128,128]{2,1,0:T(8,128)(2,1)S(1)}, u32[]{:S(2)}, u32[]{:S(2)}) %collective-permute-start.15) | collective-permute-done | bytes 98336 | tf_op jit(solution)/shard_map/ppermute | solution.py:121
  74.9 2.7 %collective-permute-done.14.refs_2_ = bf16[3,128,128]{2,1,0:T(8,128)(2,1)S(1)} collective-permute-done((bf16[3,128,128]{2,1,0:T(8,128)(2,1)S(1)}, bf16[3,128,128]{2,1,0:T(8,128)(2,1)S(1)}, u32[]{:S(2)}, u32[]{:S(2)}) %collective-permute-start.14) | collective-permute-done | bytes 98336 | tf_op jit(solution)/shard_map/ppermute | solution.py:121
  78.0 2.1 %gather.1 = (bf16[768,768]{1,0:T(8,128)(2,1)S(1)}, bf16[768,3072]{1,0:T(8,128)(2,1)S(1)}, bf16[3072,768]{1,0:T(8,128)(2,1)S(1)}) custom-call(bf16[192,768]{1,0:T(8,128)(2,1)S(1)} %copy-done.2, bf16[192,3072]{1,0:T(8,128)(2,1)S(1)} %copy-done, bf16[768,768]{1,0:T(8,128)(2,1)S(1)} %copy-done.1, ...), custom_call_target="tpu_custom_call" | custom-call | bytes 12582912 | tf_op jit(solution)/shard_map/gather/pallas_call | solution.py:421
  80.5 5.0 %feed.1 = (bf16[256,768]{1,0:T(8,128)(2,1)}, bf16[768,768]{1,0:T(8,128)(2,1)S(1)}, bf16[768,3072]{1,0:T(8,128)(2,1)S(1)}, bf16[3072,768]{1,0:T(8,128)(2,1)S(1)}) custom-call(f32[1,768]{1,0:T(1,128)S(1)} %broadcast_in_dim.3.gain, bf16[256,768]{1,0:T(8,128)(2,1)S(1)} %copy-done.3, ...), custom_call_target="tpu_custom_call", output_to_operand_aliasing={{1}: (6, {}), {2}: (7, {}), {3}: (8, {})} | custom-call | flops 3000000000 | bytes 12582912 | tf_op jit(solution)/shard_map/feed/pallas_call | solution.py:480
  (54 shorter events, 3.4 us)
Async XLA Ops:
  1.8 20.1 %collective-permute-start.2 = (bf16[1,432,384]{2,1,0:T(8,128)(2,1)}, bf16[1,432,384]{2,1,0:T(8,128)(2,1)S(1)}, u32[]{:S(2)}, u32[]{:S(2)}) collective-permute-start(bf16[1,432,384]{2,1,0:T(8,128)(2,1)} %cut_piece.1), channel_id=1, source_target_pairs={{0,8},{1,9},{2,10},{3,11},{4,12},{5,13},{6,14},{7,15},{8,0},{9,1},... | collective-permute-start | bytes 995336 | tf_op jit(solution)/shard_map/ppermute | solution.py:121
  5.9 17.8 %collective-permute-start.1 = (bf16[1,432,384]{2,1,0:T(8,128)(2,1)}, bf16[1,432,384]{2,1,0:T(8,128)(2,1)S(1)}, u32[]{:S(2)}, u32[]{:S(2)}) collective-permute-start(bf16[1,432,384]{2,1,0:T(8,128)(2,1)} %cut_piece.1), channel_id=1, source_target_pairs={{0,4},{1,5},{2,6},{3,7},{4,0},{5,1},{6,2},{7,3},{8,12},{9,13},{10,... | collective-permute-start | bytes 995336 | tf_op jit(solution)/shard_map/ppermute | solution.py:121
  10.9 19.2 %collective-permute-start = (bf16[3,256,128]{2,1,0:T(8,128)(2,1)}, bf16[3,256,128]{2,1,0:T(8,128)(2,1)S(1)}, u32[]{:S(2)}, u32[]{:S(2)}) collective-permute-start(bf16[3,256,128]{2,1,0:T(8,128)(2,1)} %get-tuple-element.34), channel_id=1, source_target_pairs={{0,4},{1,5},{2,6},{3,7},{4,0},{5,1},{6,2},{7,3},{8,12},{9,13},{10,... | collective-permute-start | bytes 589832 | tf_op jit(solution)/shard_map/ppermute | solution.py:121
  11.4 20.3 %collective-permute-start.4 = (bf16[3,256,128]{2,1,0:T(8,128)(2,1)}, bf16[3,256,128]{2,1,0:T(8,128)(2,1)S(1)}, u32[]{:S(2)}, u32[]{:S(2)}) collective-permute-start(bf16[3,256,128]{2,1,0:T(8,128)(2,1)} %get-tuple-element.35), channel_id=1, source_target_pairs={{0,12},{1,13},{2,14},{3,15},{4,8},{5,9},{6,10},{7,11},{8,4},{9,5},... | collective-permute-start | bytes 589832 | tf_op jit(solution)/shard_map/ppermute | solution.py:121
  12.7 25.3 %collective-permute-start.6 = (bf16[3,256,128]{2,1,0:T(8,128)(2,1)}, bf16[3,256,128]{2,1,0:T(8,128)(2,1)S(1)}, u32[]{:S(2)}, u32[]{:S(2)}) collective-permute-start(bf16[3,256,128]{2,1,0:T(8,128)(2,1)} %get-tuple-element.36), channel_id=1, source_target_pairs={{0,8},{1,9},{2,10},{3,11},{4,12},{5,13},{6,14},{7,15},{8,0},{9,1},... | collective-permute-start | bytes 589832 | tf_op jit(solution)/shard_map/ppermute | solution.py:121
  21.8 26.7 %collective-permute-start.8 = (bf16[3,256,128]{2,1,0:T(8,128)(2,1)}, bf16[3,256,128]{2,1,0:T(8,128)(2,1)S(1)}, u32[]{:S(2)}, u32[]{:S(2)}) collective-permute-start(bf16[3,256,128]{2,1,0:T(8,128)(2,1)} %get-tuple-element.33), channel_id=1, source_target_pairs={{0,16},{1,17},{2,18},{3,19},{4,20},{5,21},{6,22},{7,23},{8,24},{9,... | collective-permute-start | bytes 589832 | tf_op jit(solution)/shard_map/ppermute | solution.py:121
  23.8 19.9 %copy-start.8 = (bf16[400,128]{1,0:T(8,128)(2,1)S(1)}, bf16[400,128]{1,0:T(8,128)(2,1)}, u32[]{:S(2)}) copy-start(bf16[400,128]{1,0:T(8,128)(2,1)} %get-tuple-element.45) | copy-start | bytes 307204
  23.8 19.9 %copy-start.7 = (bf16[400,128]{1,0:T(8,128)(2,1)S(1)}, bf16[400,128]{1,0:T(8,128)(2,1)}, u32[]{:S(2)}) copy-start(bf16[400,128]{1,0:T(8,128)(2,1)} %get-tuple-element.46) | copy-start | bytes 307204
  23.8 23.4 %copy-start.6 = (bf16[400,128]{1,0:T(8,128)(2,1)S(1)}, bf16[400,128]{1,0:T(8,128)(2,1)}, u32[]{:S(2)}) copy-start(bf16[400,128]{1,0:T(8,128)(2,1)} %get-tuple-element.47) | copy-start | bytes 307204
  23.8 24.0 %collective-permute-start.3 = (bf16[2,432,384]{2,1,0:T(8,128)(2,1)S(1)}, bf16[2,432,384]{2,1,0:T(8,128)(2,1)S(1)}, u32[]{:S(2)}, u32[]{:S(2)}) collective-permute-start(bf16[2,432,384]{2,1,0:T(8,128)(2,1)S(1)} %pad_maximum_fusion.2), channel_id=1, source_target_pairs={{0,16},{1,3},{2,18},{3,1},{4,20},{5,7},{6,22},{7,5},{8,24},{9,11},... | collective-permute-start | bytes 1990664 | tf_op jit(solution)/shard_map/ppermute | solution.py:121
  31.8 15.5 %collective-permute-start.5 = (bf16[2,3,256,128]{3,2,1,0:T(8,128)(2,1)S(1)}, bf16[2,3,256,128]{3,2,1,0:T(8,128)(2,1)S(1)}, u32[]{:S(2)}, u32[]{:S(2)}) collective-permute-start(bf16[2,3,256,128]{3,2,1,0:T(8,128)(2,1)S(1)} %pad_maximum_fusion.3), channel_id=1, source_target_pairs={{0,16},{1,17},{2,18},{3,19},{4,20},{5,21},{6,22},{7,23},{8,24},{9,... | collective-permute-start | bytes 1179656 | tf_op jit(solution)/shard_map/ppermute | solution.py:121
  33.3 10.3 %collective-permute-start.7 = (bf16[1,432,384]{2,1,0:T(8,128)(2,1)S(1)}, bf16[1,432,384]{2,1,0:T(8,128)(2,1)S(1)}, u32[]{:S(2)}, u32[]{:S(2)}) collective-permute-start(bf16[1,432,384]{2,1,0:T(8,128)(2,1)S(1)} %collective-permute-done.2), channel_id=1, source_target_pairs={{0,4},{1,5},{2,6},{3,7},{4,0},{5,1},{6,2},{7,3},{8,12},{9,13},{10,... | collective-permute-start | bytes 995336 | tf_op jit(solution)/shard_map/ppermute | solution.py:121
  43.6 14.1 %collective-permute-start.10 = (bf16[400,128]{1,0:T(8,128)(2,1)S(1)}, bf16[400,128]{1,0:T(8,128)(2,1)S(1)}, u32[]{:S(2)}, u32[]{:S(2)}) collective-permute-start(bf16[400,128]{1,0:T(8,128)(2,1)S(1)} %copy-done.8), channel_id=1, source_target_pairs={{0,4},{1,5},{2,6},{3,7},{4,0},{5,1},{6,2},{7,3},{8,12},{9,13},{10,... | collective-permute-start | bytes 307208 | tf_op jit(solution)/shard_map/ppermute | solution.py:121
  43.6 14.1 %collective-permute-start.11 = (bf16[400,128]{1,0:T(8,128)(2,1)S(1)}, bf16[400,128]{1,0:T(8,128)(2,1)S(1)}, u32[]{:S(2)}, u32[]{:S(2)}) collective-permute-start(bf16[400,128]{1,0:T(8,128)(2,1)S(1)} %copy-done.7), channel_id=1, source_target_pairs={{0,12},{1,13},{2,14},{3,15},{4,8},{5,9},{6,10},{7,11},{8,4},{9,5},... | collective-permute-start | bytes 307208 | tf_op jit(solution)/shard_map/ppermute | solution.py:121
  47.2 10.5 %collective-permute-start.12 = (bf16[400,128]{1,0:T(8,128)(2,1)S(1)}, bf16[400,128]{1,0:T(8,128)(2,1)S(1)}, u32[]{:S(2)}, u32[]{:S(2)}) collective-permute-start(bf16[400,128]{1,0:T(8,128)(2,1)S(1)} %copy-done.6), channel_id=1, source_target_pairs={{0,8},{1,9},{2,10},{3,11},{4,12},{5,13},{6,14},{7,15},{8,0},{9,1},... | collective-permute-start | bytes 307208 | tf_op jit(solution)/shard_map/ppermute | solution.py:121
  47.8 7.8 %collective-permute-start.9 = (bf16[3,256,128]{2,1,0:T(8,128)(2,1)S(1)}, bf16[3,256,128]{2,1,0:T(8,128)(2,1)S(1)}, u32[]{:S(2)}, u32[]{:S(2)}) collective-permute-start(bf16[3,256,128]{2,1,0:T(8,128)(2,1)S(1)} %collective-permute-done.6), channel_id=1, source_target_pairs={{0,16},{1,17},{2,18},{3,19},{4,20},{5,21},{6,22},{7,23},{8,24},{9,... | collective-permute-start | bytes 589832 | tf_op jit(solution)/shard_map/ppermute | solution.py:121
  48.5 7.8 %copy-start.4 = (bf16[400,128]{1,0:T(8,128)(2,1)S(1)}, bf16[400,128]{1,0:T(8,128)(2,1)}, u32[]{:S(2)}) copy-start(bf16[400,128]{1,0:T(8,128)(2,1)} %get-tuple-element.44.refs_0_) | copy-start | bytes 307204
  48.5 14.3 %collective-permute-start.16 = (bf16[3,432,384]{2,1,0:T(8,128)(2,1)S(1)}, bf16[3,432,384]{2,1,0:T(8,128)(2,1)S(1)}, u32[]{:S(2)}, u32[]{:S(2)}) collective-permute-start(bf16[3,432,384]{2,1,0:T(8,128)(2,1)S(1)} %pad_maximum_fusion), channel_id=1, source_target_pairs={{0,2},{1,17},{2,0},{3,19},{4,6},{5,21},{6,4},{7,23},{8,10},{9,25},... | collective-permute-start | bytes 2985992 | tf_op jit(solution)/shard_map/ppermute | solution.py:121
  55.6 7.1 %collective-permute-start.17 = (bf16[1,432,384]{2,1,0:T(8,128)(2,1)S(1)}, bf16[1,432,384]{2,1,0:T(8,128)(2,1)S(1)}, u32[]{:S(2)}, u32[]{:S(2)}) collective-permute-start(bf16[1,432,384]{2,1,0:T(8,128)(2,1)S(1)} %slice.11), channel_id=1, source_target_pairs={{0,4},{1,5},{2,6},{3,7},{4,0},{5,1},{6,2},{7,3},{8,12},{9,13},{10,... | collective-permute-start | bytes 995336 | tf_op jit(solution)/shard_map/ppermute | solution.py:121
  63.0 14.9 %copy-start.5 = (f32[768]{0:T(1024)S(1)}, f32[768]{0:T(1024)}, u32[]{:S(2)}) copy-start(f32[768]{0:T(1024)} %param.15) | copy-start | bytes 9220
  63.0 14.9 %copy-start = (bf16[192,3072]{1,0:T(8,128)(2,1)S(1)}, bf16[192,3072]{1,0:T(8,128)(2,1)}, u32[]{:S(2)}) copy-start(bf16[192,3072]{1,0:T(8,128)(2,1)} %up_w.3) | copy-start | bytes 3538948
  63.0 14.9 %copy-start.1 = (bf16[768,768]{1,0:T(8,128)(2,1)S(1)}, bf16[768,768]{1,0:T(8,128)(2,1)}, u32[]{:S(2)}) copy-start(bf16[768,768]{1,0:T(8,128)(2,1)} %down_w.3) | copy-start | bytes 3538948
  63.1 14.9 %copy-start.2 = (bf16[192,768]{1,0:T(8,128)(2,1)S(1)}, bf16[192,768]{1,0:T(8,128)(2,1)}, u32[]{:S(2)}) copy-start(bf16[192,768]{1,0:T(8,128)(2,1)} %out_w.3) | copy-start | bytes 884740
  63.2 14.8 %collective-permute-start.18 = (bf16[9,432,384]{2,1,0:T(8,128)(2,1)S(1)}, bf16[9,432,384]{2,1,0:T(8,128)(2,1)S(1)}, u32[]{:S(2)}, u32[]{:S(2)}) collective-permute-start(bf16[9,432,384]{2,1,0:T(8,128)(2,1)S(1)} %constant_dynamic-update-slice_fusion.2.early), channel_id=1, source_target_pairs={{0,1},{1,0},{2,3},{3,2},{4,5},{5,4},{6,7},{7,6},{8,9},{9,8},{10,11... | collective-permute-start | bytes 8957960 | tf_op jit(solution)/shard_map/ppermute | solution.py:121
  63.7 14.3 %collective-permute-start.19 = (bf16[3,432,384]{2,1,0:T(8,128)(2,1)S(1)}, bf16[3,432,384]{2,1,0:T(8,128)(2,1)S(1)}, u32[]{:S(2)}, u32[]{:S(2)}) collective-permute-start(bf16[3,432,384]{2,1,0:T(8,128)(2,1)S(1)} %pad_maximum_fusion.1), channel_id=1, source_target_pairs={{0,2},{1,17},{2,0},{3,19},{4,6},{5,21},{6,4},{7,23},{8,10},{9,25},... | collective-permute-start | bytes 2985992 | tf_op jit(solution)/shard_map/ppermute | solution.py:121
  65.2 4.6 %collective-permute-start.13 = (bf16[3,128,128]{2,1,0:T(8,128)(2,1)S(1)}, bf16[3,128,128]{2,1,0:T(8,128)(2,1)S(1)}, u32[]{:S(2)}, u32[]{:S(2)}) collective-permute-start(bf16[3,128,128]{2,1,0:T(8,128)(2,1)S(1)} %get-tuple-element.48), channel_id=1, source_target_pairs={{0,4},{1,5},{2,6},{3,7},{4,0},{5,1},{6,2},{7,3},{8,12},{9,13},{10,... | collective-permute-start | bytes 294920 | tf_op jit(solution)/shard_map/ppermute | solution.py:121
  66.0 8.9 %collective-permute-start.15 = (bf16[3,128,128]{2,1,0:T(8,128)(2,1)S(1)}, bf16[3,128,128]{2,1,0:T(8,128)(2,1)S(1)}, u32[]{:S(2)}, u32[]{:S(2)}) collective-permute-start(bf16[3,128,128]{2,1,0:T(8,128)(2,1)S(1)} %get-tuple-element.50), channel_id=1, source_target_pairs={{0,12},{1,13},{2,14},{3,15},{4,8},{5,9},{6,10},{7,11},{8,4},{9,5},... | collective-permute-start | bytes 294920 | tf_op jit(solution)/shard_map/ppermute | solution.py:121
  69.1 8.6 %collective-permute-start.14 = (bf16[3,128,128]{2,1,0:T(8,128)(2,1)S(1)}, bf16[3,128,128]{2,1,0:T(8,128)(2,1)S(1)}, u32[]{:S(2)}, u32[]{:S(2)}) collective-permute-start(bf16[3,128,128]{2,1,0:T(8,128)(2,1)S(1)} %get-tuple-element.49), channel_id=1, source_target_pairs={{0,8},{1,9},{2,10},{3,11},{4,12},{5,13},{6,14},{7,15},{8,0},{9,1},... | collective-permute-start | bytes 294920 | tf_op jit(solution)/shard_map/ppermute | solution.py:121
  77.9 2.6 %collective-permute-start.20 = (bf16[3,432,384]{2,1,0:T(8,128)(2,1)S(1)}, bf16[3,432,384]{2,1,0:T(8,128)(2,1)S(1)}, u32[]{:S(2)}, u32[]{:S(2)}) collective-permute-start(bf16[3,432,384]{2,1,0:T(8,128)(2,1)S(1)} %collective-permute-done.19.late), channel_id=1, source_target_pairs={{0,1},{1,0},{2,3},{3,2},{4,5},{5,4},{6,7},{7,6},{8,9},{9,8},{10,11... | collective-permute-start | bytes 2985992 | tf_op jit(solution)/shard_map/ppermute | solution.py:121
  78.0 2.6 %copy-start.3 = (bf16[256,768]{1,0:T(8,128)(2,1)S(1)}, bf16[256,768]{1,0:T(8,128)(2,1)}, u32[]{:S(2)}) copy-start(bf16[256,768]{1,0:T(8,128)(2,1)} %surface.1) | copy-start | bytes 1179652
